TPU v7x, 512 devices: a whole 4x4x16 slice. The times are simulated.
512 devices in a mesh: ctx: 64 (over x, z_lo, core), tp: 8 (over z_hi, y).
Axes of the slice: x: 4, y: 4, z: 16 (z_hi: 2, z_lo: 8; z = z_hi * 8 + z_lo), core: 2. Of those that a mesh axis runs over, the one named last changes fastest.
Arguments:
- tokens: bfloat16 [8192, 8192], P('ctx', 'tp'), may hold values from -6 to 6
- in_weight: bfloat16 [3, 8192, 1024], P(None, 'ctx', 'tp'), may hold values from -0.0625 to 0.0625
- short_taps: float32 [3, 1024, 3], P(None, 'tp'), may hold values from -3 to 3
- residues: float32 [1024, 16], P('tp'), may hold values from -1.5 to 1.5
- rates: float32 [1024, 16], P('tp'), may hold values from 0.00012207031 to 0.03
- skip_gain: float32 [1024], P('tp'), may hold values from 0.5 to 1.5
Outputs:
- gated: float32 [1024, 8192], P('tp', 'ctx')
All inputs are finite; a program needn't handle non-finite values.
Results may differ from a plain program's by a relative error of at most 0.0049.
Values may be sent and summed in bfloat16 or wider, within the bound.
No kernel may reach another device: no remote copies, remote signals or barrier semaphores. Data moves between devices by JAX's collectives and lax.ppermute only.
A program may use at most 64 MiB of HBM per device.

v0:
```python
import math

import jax
import jax.numpy as jnp
from jax import lax
from jax.sharding import PartitionSpec as P

HIGH = lax.Precision.HIGHEST


def passed_along(x, axis, by):
    length = lax.axis_size(axis)
    pairs = [(i, i + by) for i in range(length) if 0 <= i + by < length]
    return lax.ppermute(x, axis, pairs)


def angle_table(first, second, length):
    phase = first[:, None] * second[None, :] % length
    angle = phase.astype(jnp.float32) * (2.0 * math.pi / length)
    return (jnp.cos(angle), jnp.sin(angle))


def forward_blocks(signal, groups):
    cosine, sine = angle_table(
        jnp.arange(groups, dtype=jnp.int32), jnp.arange(2 * groups, dtype=jnp.int32), 2 * groups
    )
    real = jnp.einsum("cpw,pk->ckw", signal, cosine, precision=HIGH)
    imaginary = -jnp.einsum("cpw,pk->ckw", signal, sine, precision=HIGH)
    return (real, imaginary)


def inverse_blocks(real, imaginary, groups, full_length):
    cosine, sine = angle_table(
        jnp.arange(2 * groups, dtype=jnp.int32), jnp.arange(groups, dtype=jnp.int32), 2 * groups
    )
    summed = jnp.einsum("ckw,kp->cpw", real, cosine, precision=HIGH) - jnp.einsum(
        "ckw,kp->cpw", imaginary, sine, precision=HIGH
    )
    return summed / full_length


def twist(real, imaginary, freqs, places, full_length, forward):
    cosine, sine = angle_table(freqs, places, full_length)
    if forward:
        return (real * cosine + imaginary * sine, imaginary * cosine - real * sine)
    return (real * cosine - imaginary * sine, imaginary * cosine + real * sine)


def within_block(real, imaginary, forward):
    count = real.shape[-1]
    indices = jnp.arange(count, dtype=jnp.int32)
    cosine, sine = angle_table(indices, indices, count)
    real_cos = jnp.matmul(real, cosine, precision=HIGH)
    real_sin = jnp.matmul(real, sine, precision=HIGH)
    imag_cos = jnp.matmul(imaginary, cosine, precision=HIGH)
    imag_sin = jnp.matmul(imaginary, sine, precision=HIGH)
    if forward:
        return (real_cos + imag_sin, imag_cos - real_sin)
    return (real_cos - imag_sin, imag_cos + real_sin)


def spectrum(residues, rates, freq_grid, full_length, seq_length):
    theta = freq_grid.astype(jnp.float32) * (2.0 * math.pi / full_length)
    parity = 1.0 - 2.0 * (freq_grid % 2).astype(jnp.float32)
    half_sine = jnp.sin(0.5 * theta)
    wave_sine = jnp.sin(theta)
    shape = (residues.shape[0],) + freq_grid.shape
    spec_real = jnp.zeros(shape, jnp.float32)
    spec_imag = jnp.zeros(shape, jnp.float32)
    for mode in range(residues.shape[1]):
        decay = rates[:, mode][:, None, None]
        amplitude = residues[:, mode][:, None, None] * jnp.sqrt(2.0 * decay)
        factor = jnp.exp(-decay)
        numer = 1.0 - jnp.exp(-decay * seq_length) * parity
        denom_real = -jnp.expm1(-decay) + factor * 2.0 * half_sine * half_sine
        denom_imag = factor * wave_sine
        weight = amplitude * numer / (denom_real * denom_real + denom_imag * denom_imag)
        spec_real = spec_real + weight * denom_real
        spec_imag = spec_imag - weight * denom_imag
    return (spec_real, spec_imag)


def apply_filter(real, imaginary, residues, rates, freq_grid, full_length, seq_length):
    spec_real, spec_imag = spectrum(residues, rates, freq_grid, full_length, seq_length)
    return (real * spec_real - imaginary * spec_imag, real * spec_imag + imaginary * spec_real)


def conv_fourstep(driven, residues, rates):
    groups = lax.axis_size("ctx")
    own = lax.axis_index("ctx")
    chans, count = driven.shape
    per_group = count // groups
    full_length = 2 * groups * count
    seq_length = groups * count
    columns = lax.all_to_all(
        driven.reshape(chans, 1, groups, per_group), "ctx", split_axis=2, concat_axis=1, tiled=True
    )
    real, imaginary = forward_blocks(columns.reshape(chans, groups, per_group), groups)
    places = own * per_group + jnp.arange(per_group, dtype=jnp.int32)
    real, imaginary = twist(
        real, imaginary, jnp.arange(2 * groups, dtype=jnp.int32), places, full_length, True
    )
    stacked = jnp.stack([real, imaginary]).reshape(2, chans, groups, 2, 1, per_group)
    stacked = lax.all_to_all(stacked, "ctx", split_axis=2, concat_axis=4, tiled=True).reshape(
        2, chans, 2, count
    )
    real, imaginary = within_block(stacked[0], stacked[1], True)
    own_freqs = 2 * own + jnp.arange(2, dtype=jnp.int32)
    freq_grid = own_freqs[:, None] + 2 * groups * jnp.arange(count, dtype=jnp.int32)[None, :]
    real, imaginary = apply_filter(
        real, imaginary, residues, rates, freq_grid, full_length, seq_length
    )
    real, imaginary = within_block(real, imaginary, False)
    real, imaginary = twist(
        real, imaginary, own_freqs, jnp.arange(count, dtype=jnp.int32), full_length, False
    )
    stacked = jnp.stack([real, imaginary]).reshape(2, chans, 1, 2, groups, per_group)
    stacked = lax.all_to_all(stacked, "ctx", split_axis=4, concat_axis=2, tiled=True).reshape(
        2, chans, 2 * groups, per_group
    )
    signal = inverse_blocks(stacked[0], stacked[1], groups, full_length)
    back = lax.all_to_all(
        signal.reshape(chans, groups, 1, per_group), "ctx", split_axis=1, concat_axis=2, tiled=True
    )
    return back.reshape(chans, count)


def body(tokens, in_weight, short_taps, residues, rates, skip_gain):
    features = lax.all_gather(tokens, "tp", axis=1, tiled=True)
    count = features.shape[0]
    piece = lax.all_gather(in_weight, "ctx", axis=1, tiled=True)
    terms = [
        lax.dot_general(
            piece[j], features, (((0,), (1,)), ((), ())), preferred_element_type=jnp.float32
        )
        for j in range(3)
    ]
    proj = jnp.stack(terms).astype(jnp.bfloat16)
    before = passed_along(proj[:, :, count - 2 :], "ctx", 1)
    wide = jnp.concatenate([before, proj], axis=2).astype(jnp.float32)
    filtered = (
        short_taps[:, :, 0:1] * wide[:, :, 2:]
        + short_taps[:, :, 1:2] * wide[:, :, 1:-1]
        + short_taps[:, :, 2:3] * wide[:, :, :-2]
    )
    query = filtered[0]
    driven = filtered[1] * filtered[2]
    conv = conv_fourstep(driven, residues, rates)
    return query * (conv + skip_gain[:, None] * driven)


def solution(mesh):
    in_specs = (
        P("ctx", "tp"),
        P(None, "ctx", "tp"),
        P(None, "tp", None),
        P("tp", None),
        P("tp", None),
        P("tp"),
    )
    out_specs = P("tp", "ctx")
    return jax.shard_map(body, mesh=mesh, in_specs=in_specs, out_specs=out_specs, check_vma=False)
```

profile of v0, /device:TPU:1, one launch (start us, length us, event | category | flops | bytes accessed | tf_op | source)
XLA Modules:
  0.0 379.1 jit_solution(15787196650666571171)
XLA Ops:
  6.5 0.0 all-gather.5.cloned.1.call-start
  6.5 0.7 all-gather.5.cloned.1.call-update
  7.3 0.0 all-gather.3.cloned.1.call-start
  7.3 0.7 all-gather.3.cloned.1.call-update
  8.0 0.8 exponential_bitcast_fusion.7
  8.9 0.8 fusion.190
  9.7 123.0 %all-gather.5.cloned.1.call-done = bf16[128,8192]{1,0:T(8,128)(2,1)} async-done(((bf16[128,1024]{1,0:T(8,128)(2,1)}), bf16[128,8192]{1,0:T(8,128)(2,1)}) %all-gather.5.cloned.1.call-update) | async-done | bytes 2097168 | tf_op jit(solution)/shard_map/all_gather | solution.py:129
  132.6 0.0 copy-start.3
  132.6 122.8 %all-gather.3.cloned.1.call-done = bf16[3,8192,128]{2,1,0:T(8,128)(2,1)} async-done(((bf16[3,128,128]{2,1,0:T(8,128)(2,1)}), bf16[3,8192,128]{2,1,0:T(8,128)(2,1)}) %all-gather.3.cloned.1.call-update) | async-done | bytes 6291472 | tf_op jit(solution)/shard_map/all_gather | solution.py:131
  255.5 2.9 fusion.10
  258.4 0.0 copy-done.3
  258.4 2.3 fusion.8
  260.7 0.0 copy-start
  260.8 2.3 fusion.9
  263.1 0.0 copy-start.1
  263.1 3.0 collective-permute-start
  266.2 0.1 fusion.136
  266.3 0.6 collective-permute-done
  266.9 0.1 fusion.11
  267.0 0.6 slice_multiply_fusion.3
  267.6 12.0 %all-to-all-start = ((f32[128,1,64,2]{0,3,1,2:T(2,128)}), f32[128,1,64,2]{0,3,1,2:T(2,128)S(1)}, u32[]{:S(2)}, u32[]{:S(2)}) async-start(f32[128,1,64,2]{0,3,1,2:T(2,128)} %bitcast.10), calls=%async_computation | async-start | bytes 131072 | tf_op jit(solution)/shard_map/all_to_all | solution.py:95
  279.7 0.0 copy-done
  279.7 12.8 %all-to-all-done = f32[128,1,64,2]{0,3,1,2:T(2,128)S(1)} async-done(((f32[128,1,64,2]{0,3,1,2:T(2,128)}), f32[128,1,64,2]{0,3,1,2:T(2,128)S(1)}, u32[]{:S(2)}, u32[]{:S(2)}) %all-to-all-start) | async-done | bytes 65568 | tf_op jit(solution)/shard_map/all_to_all | solution.py:95
  292.5 0.4 fusion.79
  292.9 0.5 multiply_add_fusion.19
  293.4 0.1 copy.37
  293.5 0.1 copy.38
  293.6 0.8 pad_maximum_fusion
  294.4 5.0 %all-to-all-start.1 = ((f32[2,128,64,2,1,2]{1,5,3,0,4,2:T(2,128)}), f32[2,128,64,2,1,2]{1,5,3,0,4,2:T(2,128)S(1)}, u32[]{:S(2)}, u32[]{:S(2)}) async-start(f32[2,128,64,2,1,2]{1,5,3,0,4,2:T(2,128)} %pad_maximum_fusion), calls=%async_computation.1 | async-start | bytes 524288 | tf_op jit(solution)/shard_map/all_to_all | solution.py:104
  299.5 0.1 fusion.138
  299.6 0.0 copy-done.1
  299.7 19.0 %all-to-all-done.1 = f32[2,128,64,2,1,2]{1,5,3,0,4,2:T(2,128)S(1)} async-done(((f32[2,128,64,2,1,2]{1,5,3,0,4,2:T(2,128)}), f32[2,128,64,2,1,2]{1,5,3,0,4,2:T(2,128)S(1)}, u32[]{:S(2)}, u32[]{:S(2)}) %all-to-all-start.1) | async-done | bytes 262176 | tf_op jit(solution)/shard_map/all_to_all | solution.py:104
  318.8 0.5 fusion.76
  319.5 0.5 fusion.74
  320.0 0.5 convolution_add_fusion.1
  320.6 1.9 multiply_add_fusion.1
  322.5 0.5 fusion.72
  323.0 0.5 fusion.70
  323.5 0.5 convolution_subtract_fusion
  324.0 0.0 copy-start.2
  324.0 0.5 multiply_subtract_fusion
  324.6 0.1 copy.49
  324.7 0.1 copy.50
  324.8 0.1 pad_maximum_fusion.1
  324.9 26.2 %all_to_all.48 = f32[2,128,1,2,64,2]{1,3,5,0,2,4:T(2,128)S(1)} all-to-all(f32[2,128,1,2,64,2]{1,3,5,0,2,4:T(2,128)S(1)} %pad_maximum_fusion.1), channel_id=1, replica_groups=mesh['ctx'=64,'tp'=8] {'ctx'}, dimensions={4} | all-to-all | bytes 524288 | tf_op jit(solution)/shard_map/all_to_all | solution.py:118
  351.2 0.3 fusion.95
  351.6 0.3 fusion.4
  351.9 0.1 copy.55
  352.0 19.5 %all_to_all.49 = f32[128,64,1,2]{0,3,2,1:T(2,128)S(1)} all-to-all(f32[128,64,1,2]{0,3,2,1:T(2,128)S(1)} %copy.55), channel_id=1, replica_groups=mesh['ctx'=64,'tp'=8] {'ctx'}, dimensions={1} | all-to-all | bytes 131072 | tf_op jit(solution)/shard_map/all_to_all | solution.py:122
  371.5 0.0 copy-done.2
  371.5 0.7 copy.56
  (19 shorter events, 0.5 us)
Async XLA Ops:
  6.5 126.1 %all-gather.5.cloned.1.call-start = ((), (), s32[]{:S(2)}) async-start(), calls=%async_computation.5 | async-start | bytes 2359296 | tf_op jit(solution)/shard_map/all_gather | solution.py:129
  7.3 248.2 %all-gather.3.cloned.1.call-start = ((), (), s32[]{:S(2)}) async-start(), calls=%async_computation.4 | async-start | bytes 6389760 | tf_op jit(solution)/shard_map/all_gather | solution.py:131
  132.6 125.8 %copy-start.3 = (bf16[128,8192]{1,0:T(8,128)(2,1)S(1)}, bf16[128,8192]{1,0:T(8,128)(2,1)}, u32[]{:S(2)}) copy-start(bf16[128,8192]{1,0:T(8,128)(2,1)} %all-gather.5.cloned.1.call-done) | copy-start | bytes 6291460
  260.7 18.9 %copy-start = (f32[128,16]{0,1:T(8,128)S(1)}, f32[128,16]{0,1:T(8,128)}, u32[]{:S(2)}) copy-start(f32[128,16]{0,1:T(8,128)} %param.10) | copy-start | bytes 24580
  263.1 36.5 %copy-start.1 = (f32[128,16]{0,1:T(8,128)S(1)}, f32[128,16]{0,1:T(8,128)}, u32[]{:S(2)}) copy-start(f32[128,16]{0,1:T(8,128)} %param.9) | copy-start | bytes 24580
  263.1 3.8 collective-permute-start
  267.6 24.9 %all-to-all-start = ((f32[128,1,64,2]{0,3,1,2:T(2,128)}), f32[128,1,64,2]{0,3,1,2:T(2,128)S(1)}, u32[]{:S(2)}, u32[]{:S(2)}) async-start(f32[128,1,64,2]{0,3,1,2:T(2,128)} %bitcast.10), calls=%async_computation | async-start | bytes 131072 | tf_op jit(solution)/shard_map/all_to_all | solution.py:95
  294.4 24.3 %all-to-all-start.1 = ((f32[2,128,64,2,1,2]{1,5,3,0,4,2:T(2,128)}), f32[2,128,64,2,1,2]{1,5,3,0,4,2:T(2,128)S(1)}, u32[]{:S(2)}, u32[]{:S(2)}) async-start(f32[2,128,64,2,1,2]{1,5,3,0,4,2:T(2,128)} %pad_maximum_fusion), calls=%async_computation.1 | async-start | bytes 524288 | tf_op jit(solution)/shard_map/all_to_all | solution.py:104
  324.0 47.5 %copy-start.2 = (f32[128]{0:T(128)S(1)}, f32[128]{0:T(128)}, u32[]{:S(2)}) copy-start(f32[128]{0:T(128)} %param.11) | copy-start | bytes 1540
Sparse Core Ops, SparseCore 0:
  10.6 122.0 all-gather.4
  134.8 120.6 all-gather.2
where the time goes:
time: 380 us; the launch traced here: 379 us
  waiting for transfers between devices  280 us (74%)
  blocking collectives  45.7 us (12%)
  starting transfers between devices  20.1 us (5%)
  matrix products  14.7 us (4%)
  between operations  13.8 us (4%)
    all_gather x1, waiting for transfers between devices, body(): features = lax.all_gather(tokens, 'tp', axis=1, tiled=True)  123 us
    all_gather x1, waiting for transfers between devices, body(): piece = lax.all_gather(in_weight, 'ctx', axis=1, tiled=True)  123 us
    all_to_all x1, blocking collectives, conv_fourstep(): lax.all_to_all(stacked, 'ctx', split_axis=4, concat_axis=2, tiled=True)  26.2 us
    all_to_all x1, blocking collectives, conv_fourstep(): lax.all_to_all(signal.reshape(chans, groups, 1, per_group), 'ctx', split_...  19.5 us
    all_to_all x1, waiting for transfers between devices, conv_fourstep(): lax.all_to_all(stacked, 'ctx', split_axis=2, concat_axis=4, tiled=True)  19 us
    all_to_all x1, waiting for transfers between devices, conv_fourstep(): lax.all_to_all(driven.reshape(chans, 1, groups, per_group), 'ctx', split_...  12.8 us
    all_to_all x1, starting transfers between devices, conv_fourstep(): lax.all_to_all(driven.reshape(chans, 1, groups, per_group), 'ctx', split_...  12 us
  transfers between devices with their start and end apart: 5, of which 5 were waited for; matrix products, arithmetic and copies ran while one was open for 1% of the time, Pallas kernels for 0%

commit v1 on v0

v1 whole, which is shorter than its diff:
```python
import jax
import jax.numpy as jnp
from jax import lax
from jax.experimental import pallas as pl
from jax.experimental.pallas import tpu as pltpu
from jax.sharding import PartitionSpec as P

F32 = jnp.float32
BF16 = jnp.bfloat16
HALO = 16
BLOCK = 128
MODES = 16
VMEM = pl.BlockSpec(memory_space=pltpu.VMEM)
SMEM = pl.BlockSpec(memory_space=pltpu.SMEM)
PARAMS = pltpu.CompilerParams(vmem_limit_bytes=48 * 1024 * 1024)


def flip(x, axis, mask):
    length = lax.axis_size(axis)
    return lax.ppermute(x, axis, [(i, i ^ mask) for i in range(length)])


def ahead(x, axis, by):
    length = lax.axis_size(axis)
    return lax.ppermute(x, axis, [(i, i + by) for i in range(length - by)])


def ordered(upper, own, other, axis):
    first = jnp.where(upper, other, own)
    second = jnp.where(upper, own, other)
    return jnp.concatenate([first, second], axis=axis)


def gather_tokens(tokens, core):
    split = tokens.reshape(BLOCK, 2, 2, 2, BLOCK)
    kept = lax.dynamic_index_in_dim(split, core, 3, keepdims=False)
    given = lax.dynamic_index_in_dim(split, 1 - core, 3, keepdims=False)
    kept = kept.reshape(BLOCK, 2, 256).transpose(1, 0, 2)
    given = given.reshape(BLOCK, 2, 256).transpose(1, 0, 2)
    other = flip(given, "ctx", 1)
    both = ordered(core == 1, kept, other, 1)
    halo = ahead(both[:, 2 * BLOCK - HALO :], "ctx", 2)
    rows = jnp.concatenate([halo, both], axis=1)
    pair = jnp.stack([rows, flip(rows, "tp", 4)])
    turns = [pair] + [flip(pair, "tp", m) for m in (1, 3, 2)]
    return jnp.stack([turns[0], turns[1], turns[3], turns[2]])


def gather_weights(piece, place):
    held = piece[None]
    held = jnp.concatenate([held, flip(held, "ctx", 8)], axis=0)
    held = jnp.concatenate([held, flip(held, "ctx", 4)], axis=0)
    held = ordered((place & 2) == 2, held, flip(held, "ctx", 2), 1)
    return [held] + [flip(held, "ctx", m << 4) for m in (1, 2, 3)]


def project_kernel(order, tokens, w0, w1, w2, w3, out):
    total = jnp.zeros(out.shape, F32)
    for i, w in enumerate((w0, w1, w2, w3)):
        for j in range(4):
            total += jnp.dot(tokens[order[4 * i + j]], w[j], preferred_element_type=F32)
    out[...] = total


def project(order, tokens, weights):
    rows, columns = tokens.shape[1], weights[0].shape[2]
    return pl.pallas_call(
        project_kernel,
        out_shape=jax.ShapeDtypeStruct((rows, columns), F32),
        in_specs=[SMEM] + [VMEM] * 5,
        out_specs=VMEM,
        compiler_params=PARAMS,
        cost_estimate=pl.CostEstimate(
            flops=2 * rows * 4096 * columns, bytes_accessed=4096 * 2 * (rows + columns), transcendentals=0
        ),
        name="project",
    )(order, tokens, *weights)


def short(proj, taps):
    n = proj.shape[0] - HALO
    return (
        taps[0:1] * proj[HALO : HALO + n]
        + taps[1:2] * proj[HALO - 1 : HALO - 1 + n]
        + taps[2:3] * proj[HALO - 2 : HALO - 2 + n]
    )


def drive_kernel(place, mine, theirs, key_taps, value_taps, weigh, step, driven, before, state):
    proj = (mine[...] + theirs[...]).astype(BF16).astype(F32)
    key = short(proj[:, :BLOCK], key_taps[...])
    value = short(proj[:, BLOCK:], value_taps[...])
    signal = key * value
    first, second = signal[:BLOCK], signal[BLOCK:]
    upper = place[0] == 1
    driven[...] = jnp.where(upper, second, first)
    for r in range(MODES):
        w = weigh[r]
        one = jnp.sum(w * first, axis=0, keepdims=True)
        two = jnp.sum(w * second, axis=0, keepdims=True)
        before[r : r + 1] = jnp.where(upper, one, 0.0)
        state[r : r + 1] = two + step[r : r + 1] * one


def drive(place, mine, theirs, key_taps, value_taps, weigh, step):
    return pl.pallas_call(
        drive_kernel,
        out_shape=(
            jax.ShapeDtypeStruct((BLOCK, BLOCK), F32),
            jax.ShapeDtypeStruct((MODES, BLOCK), F32),
            jax.ShapeDtypeStruct((MODES, BLOCK), F32),
        ),
        in_specs=[SMEM] + [VMEM] * 6,
        out_specs=(VMEM, VMEM, VMEM),
        compiler_params=PARAMS,
        name="drive",
    )(place, mine, theirs, key_taps, value_taps, weigh, step)


def near_kernel(driven, taps, gain, out, padded):
    signal = driven[...]
    padded[:BLOCK] = jnp.zeros((BLOCK, BLOCK), F32)
    padded[BLOCK:] = signal
    total = gain[...] * signal
    for s in range(BLOCK):
        low = s // 8 * 8
        part = taps[s : s + 1] * padded[BLOCK + low - s : 2 * BLOCK - s]
        if low:
            part = jnp.concatenate([jnp.zeros((low, BLOCK), F32), part], axis=0)
        total = total + part
    out[...] = total


def near(driven, taps, gain):
    return pl.pallas_call(
        near_kernel,
        out_shape=jax.ShapeDtypeStruct((BLOCK, BLOCK), F32),
        in_specs=[VMEM] * 3,
        out_specs=VMEM,
        scratch_shapes=[pltpu.VMEM((2 * BLOCK, BLOCK), F32)],
        compiler_params=PARAMS,
        cost_estimate=pl.CostEstimate(flops=2 * BLOCK**3, bytes_accessed=3 * BLOCK * BLOCK * 4, transcendentals=0),
        name="near",
    )(driven, taps, gain)


def finish_kernel(mine, theirs, query_taps, inner, reach, carry, out):
    proj = (mine[...] + theirs[...]).astype(BF16).astype(F32)
    query = short(proj, query_taps[...])
    conv = inner[...]
    for r in range(MODES):
        conv = conv + reach[r] * carry[r : r + 1]
    out[...] = (query * conv).T


def finish(mine, theirs, query_taps, inner, reach, carry):
    return pl.pallas_call(
        finish_kernel,
        out_shape=jax.ShapeDtypeStruct((BLOCK, BLOCK), F32),
        in_specs=[VMEM] * 6,
        out_specs=VMEM,
        compiler_params=PARAMS,
        name="finish",
    )(mine, theirs, query_taps, inner, reach, carry)


def body(tokens, in_weight, short_taps, residues, rates, skip_gain):
    place = lax.axis_index("ctx")
    tp = lax.axis_index("tp")
    core = place & 1
    chip_z, chip_x = (place >> 1) & 7, place >> 4
    tp_y, tp_h = tp & 3, tp >> 2

    rate = rates.T
    amount = residues.T * jnp.sqrt(2.0 * rate)
    index = jnp.arange(BLOCK, dtype=F32)[None, :, None]
    weigh = jnp.exp(-rate[:, None, :] * (BLOCK - 1.0 - index))
    reach = amount[:, None, :] * jnp.exp(-rate[:, None, :] * (index + 1.0))
    taps = jnp.sum(amount[:, None, :] * jnp.exp(-rate[:, None, :] * index), axis=0)
    step = jnp.exp(-rate * float(BLOCK))

    features = gather_tokens(tokens, core).reshape(16, HALO + 2 * BLOCK, 256)
    pair = gather_weights(jnp.concatenate([in_weight[1], in_weight[2]], axis=1), place)
    single = gather_weights(in_weight[0], place)

    turn = jnp.arange(16, dtype=jnp.int32)
    src_x = chip_x ^ (turn >> 2)
    src_z = (chip_z >> 1) ^ (((turn & 1) << 1) | ((turn >> 1) & 1))
    need_h = (src_x >> 1) ^ tp_h
    need_y = (((src_x & 1) << 1) | (src_z >> 1)) ^ tp_y
    order = (need_y << 2) | (need_h << 1) | (src_z & 1)

    mine = project(order, features, pair)
    theirs = flip(mine, "ctx", 1)
    driven, before, state = drive(
        core[None], mine, theirs, short_taps[1].T, short_taps[2].T, weigh, step
    )

    far = project(order, features, single)
    length = HALO + BLOCK
    own = lax.dynamic_slice_in_dim(far, core * BLOCK, length, 0)
    gift = lax.dynamic_slice_in_dim(far, (1 - core) * BLOCK, length, 0)
    other = flip(gift, "ctx", 1)

    inner = near(driven, taps, skip_gain[None])

    for bit in range(1, 6):
        group = 1 << bit
        upper = (place & group) == group
        past = flip(state, "ctx", group)
        whole = jnp.exp(-rate * float(BLOCK * group))
        since = jnp.exp(-rate * (BLOCK * (place & (group - 1))).astype(F32))
        before = before + jnp.where(upper, since * past, 0.0)
        if bit < 5:
            state = jnp.where(upper, state + whole * past, whole * state + past)

    return finish(own, other, short_taps[0].T, inner, reach, before)


def solution(mesh):
    in_specs = (
        P("ctx", "tp"),
        P(None, "ctx", "tp"),
        P(None, "tp", None),
        P("tp", None),
        P("tp", None),
        P("tp"),
    )
    return jax.shard_map(
        body, mesh=mesh, in_specs=in_specs, out_specs=P("tp", "ctx"), check_vma=False
    )
```

time: 380 us -> 171 us (0.45)
  waiting for transfers between devices: 280 us -> 21.6 us
  starting transfers between devices: 20.1 us -> 130 us
  blocking collectives: 45.7 us -> 0 us
  matrix products: 14.7 us -> 0 us
  between operations: 13.8 us -> 0.74 us
  other arithmetic: 2.94 us -> 7.6 us
  Pallas kernels: 0 us -> 4.58 us
    all_gather x2 -> x0, waiting for transfers between devices: 246 us -> none  [the longest x1 123 us: body(): features = lax.all_gather(tokens, 'tp', axis=1, tiled=True)]
    ppermute x1 -> x25, starting transfers between devices: 3.04 us -> 130 us  [the longest x24 129 us: flip(): return lax.ppermute(x, axis, [(i, i ^ mask) for i in range(length)])]
    all_to_all x2 -> x0, blocking collectives: 45.7 us -> none  [the longest x1 26.2 us: conv_fourstep(): lax.all_to_all(stacked, 'ctx', split_axis=4, concat_axis=2, tiled=True)]
    all_to_all x2 -> x0, waiting for transfers between devices: 31.8 us -> none  [the longest x1 19 us: conv_fourstep(): lax.all_to_all(stacked, 'ctx', split_axis=2, concat_axis=4, tiled=True)]
    ppermute x1 -> x25, waiting for transfers between devices: 0.58 us -> 21.6 us  [the longest x24 21.6 us: flip(): return lax.ppermute(x, axis, [(i, i ^ mask) for i in range(length)])]
    all_to_all x2 -> x0, starting transfers between devices: 17.1 us -> none  [the longest x1 12 us: conv_fourstep(): lax.all_to_all(driven.reshape(chans, 1, groups, per_group), 'ctx', split_...]
    dot_general x15 -> x0, matrix products: 14.7 us -> none  [the longest x3 7.57 us: body(): lax.dot_general(piece[j], features, (((0,), (1,)), ((), ())), preferred_e...]
    pallas_call x0 -> x5, Pallas kernels: none -> 4.58 us  [the longest x2 3.15 us: project(): pl.pallas_call(project_kernel, out_shape=jax.ShapeDtypeStruct((rows, colu...]
  transfers between devices with their start and end apart: 5 -> 25, of which waited for: 5 -> 7; matrix products, arithmetic and copies ran while one was open for 1% -> 5% of each run, Pallas kernels for 0% -> 2%
where the time goes in v1:
time: 171 us; the launch traced here: 169 us
  starting transfers between devices  130 us (76%)
  waiting for transfers between devices  21.6 us (13%)
  other arithmetic  7.6 us (4%)
  local copies, waits for them, and re-layouts  4.67 us (3%)
  Pallas kernels  4.58 us (3%)
    ppermute x24, starting transfers between devices, flip(): return lax.ppermute(x, axis, [(i, i ^ mask) for i in range(length)])  129 us
    ppermute x24, waiting for transfers between devices, flip(): return lax.ppermute(x, axis, [(i, i ^ mask) for i in range(length)])  21.6 us
  transfers between devices with their start and end apart: 25, of which 7 were waited for; matrix products, arithmetic and copies ran while one was open for 5% of the time, Pallas kernels for 2%

profile of v1, /device:TPU:1, one launch (start us, length us, event | category | flops | bytes accessed | tf_op | source)
XLA Modules:
  0.0 169.0 jit_solution(2879532165384422328)
XLA Ops:
  0.0 1.1 reshape.27
  1.2 1.8 %dynamic-slice_reduce_fusion.1 = (bf16[128,2,2,128]{3,2,1,0:T(2,128)(2,1)S(1)}, bf16[128,2,2,128]{3,2,1,0:T(2,128)(2,1)S(1)}) fusion(bf16[128,2,2,2,128]{4,3,2,1,0:T(2,128)(2,1)S(1)} %reshape.27, s32[]{:T(128)S(6)} %select_n.100, s32[]{:T(128)S(6)} %select_n.101), kind=kLoop, calls=%fused_computation.10 | loop fusion | bytes 524296 | tf_op jit(solution)/shard_map/jit(dynamic_index_in_dim)/dynamic_slice | solution.py:36
  2.9 0.1 reshape.32
  3.1 8.8 %collective-permute-start = (bf16[2,128,256]{2,1,0:T(8,128)(2,1)S(1)}, bf16[2,128,256]{2,1,0:T(8,128)(2,1)S(1)}, u32[]{:S(2)}, u32[]{:S(2)}) collective-permute-start(bf16[2,128,256]{2,1,0:T(8,128)(2,1)S(1)} %bitcast.58), channel_id=1, source_target_pairs={{0,8},{8,0},{16,24},{24,16},{32,40},{40,32},{48,56},{56,48},{64,72... | collective-permute-start | bytes 393224 | tf_op jit(solution)/shard_map/ppermute | solution.py:20
  11.9 0.8 slice_bitcast_fusion.1
  12.7 3.4 %collective-permute-start.6 = (bf16[1,128,128]{2,1,0:T(8,128)(2,1)S(1)}, bf16[1,128,128]{2,1,0:T(8,128)(2,1)S(1)}, u32[]{:S(2)}, u32[]{:S(2)}) collective-permute-start(bf16[1,128,128]{2,1,0:T(8,128)(2,1)S(1)} %get-tuple-element.26), channel_id=1, source_target_pairs={{0,64},{8,72},{16,80},{24,88},{32,96},{40,104},{48,112},{56,120},{... | collective-permute-start | bytes 98312 | tf_op jit(solution)/shard_map/ppermute | solution.py:20
  16.1 5.7 %collective-permute-start.13 = (bf16[1,128,256]{2,1,0:T(8,128)(2,1)S(1)}, bf16[1,128,256]{2,1,0:T(8,128)(2,1)S(1)}, u32[]{:S(2)}, u32[]{:S(2)}) collective-permute-start(bf16[1,128,256]{2,1,0:T(8,128)(2,1)S(1)} %maximum_bitcast_fusion), channel_id=1, source_target_pairs={{0,64},{8,72},{16,80},{24,88},{32,96},{40,104},{48,112},{56,120},{... | collective-permute-start | bytes 196616 | tf_op jit(solution)/shard_map/ppermute | solution.py:20
  21.9 0.1 reshape.31
  22.0 1.3 collective-permute-start.1
  23.3 1.7 %collective-permute-done.13 = bf16[1,128,256]{2,1,0:T(8,128)(2,1)S(1)} collective-permute-done((bf16[1,128,256]{2,1,0:T(8,128)(2,1)S(1)}, bf16[1,128,256]{2,1,0:T(8,128)(2,1)S(1)}, u32[]{:S(2)}, u32[]{:S(2)}) %collective-permute-start.13) | collective-permute-done | bytes 65568 | tf_op jit(solution)/shard_map/ppermute | solution.py:20
  25.1 5.1 %collective-permute-start.14 = (bf16[2,128,256]{2,1,0:T(8,128)(2,1)S(1)}, bf16[2,128,256]{2,1,0:T(8,128)(2,1)S(1)}, u32[]{:S(2)}, u32[]{:S(2)}) collective-permute-start(bf16[2,128,256]{2,1,0:T(8,128)(2,1)S(1)} %pad_maximum_fusion.7), channel_id=1, source_target_pairs={{0,32},{8,40},{16,48},{24,56},{32,0},{40,8},{48,16},{56,24},{64,96... | collective-permute-start | bytes 393224 | tf_op jit(solution)/shard_map/ppermute | solution.py:20
  30.2 12.2 %collective-permute-start.2 = (bf16[2,272,256]{2,1,0:T(8,128)(2,1)S(1)}, bf16[2,272,256]{2,1,0:T(8,128)(2,1)S(1)}, u32[]{:S(2)}, u32[]{:S(2)}) collective-permute-start(bf16[2,272,256]{2,1,0:T(8,128)(2,1)S(1)} %get-tuple-element.18), channel_id=1, source_target_pairs={{0,4},{1,5},{2,6},{3,7},{4,0},{5,1},{6,2},{7,3},{8,12},{9,13},{10,... | collective-permute-start | bytes 835592 | tf_op jit(solution)/shard_map/ppermute | solution.py:20
  42.4 0.0 collective-permute-done.14
  42.5 1.9 %collective-permute-start.15 = (bf16[4,128,256]{2,1,0:T(8,128)(2,1)S(1)}, bf16[4,128,256]{2,1,0:T(8,128)(2,1)}, u32[]{:S(2)}, u32[]{:S(2)}) collective-permute-start(bf16[4,128,256]{2,1,0:T(8,128)(2,1)S(1)} %pad_maximum_fusion.5), channel_id=1, source_target_pairs={{0,16},{8,24},{16,0},{24,8},{32,48},{40,56},{48,32},{56,40},{64,80... | collective-permute-start | bytes 786440 | tf_op jit(solution)/shard_map/ppermute | solution.py:20
  44.4 4.9 %collective-permute-done.2 = bf16[2,272,256]{2,1,0:T(8,128)(2,1)S(1)} collective-permute-done((bf16[2,272,256]{2,1,0:T(8,128)(2,1)S(1)}, bf16[2,272,256]{2,1,0:T(8,128)(2,1)S(1)}, u32[]{:S(2)}, u32[]{:S(2)}) %collective-permute-start.2) | collective-permute-done | bytes 278560 | tf_op jit(solution)/shard_map/ppermute | solution.py:20
  49.3 0.9 fusion.5
  50.2 4.6 %collective-permute-start.5 = (bf16[2,2,272,256]{3,2,1,0:T(8,128)(2,1)S(1)}, bf16[2,2,272,256]{3,2,1,0:T(8,128)(2,1)S(1)}, u32[]{:S(2)}, u32[]{:S(2)}) collective-permute-start(bf16[2,2,272,256]{3,2,1,0:T(8,128)(2,1)S(1)} %get-tuple-element.14), channel_id=1, source_target_pairs={{0,3},{1,2},{2,1},{3,0},{4,7},{5,6},{6,5},{7,4},{8,11},{9,10},{10,... | collective-permute-start | bytes 1671176 | tf_op jit(solution)/shard_map/ppermute | solution.py:20
  54.8 1.9 %exponential_multiply_fusion = (f32[16,128,128]{2,1,0:T(8,128)}, f32[128,128]{1,0:T(8,128)}, f32[16,128,128]{2,1,0:T(8,128)S(1)}) fusion(f32[128]{0:T(128)S(1)} %get-tuple-element.36, f32[16,128]{1,0:T(8,128)S(1)} %get-tuple-element.31, f32[16,128]{1,0:T(8,128)S(1)} %get-tuple-element.32, f32[128]{0:T(128)S(1)} %get-tuple-element.37), kind=kLoop, calls=%fused_computation.1 | loop fusion | flops 1556480 | bytes 2180096 | tf_op jit(solution)/shard_map/mul | solution.py:178
  56.7 2.2 %collective-permute-start.4 = (bf16[2,2,272,256]{3,2,1,0:T(8,128)(2,1)S(1)}, bf16[2,2,272,256]{3,2,1,0:T(8,128)(2,1)S(1)}, u32[]{:S(2)}, u32[]{:S(2)}) collective-permute-start(bf16[2,2,272,256]{3,2,1,0:T(8,128)(2,1)S(1)} %get-tuple-element.14), channel_id=1, source_target_pairs={{0,2},{1,3},{2,0},{3,1},{4,6},{5,7},{6,4},{7,5},{8,10},{9,11},{10,... | collective-permute-start | bytes 1671176 | tf_op jit(solution)/shard_map/ppermute | solution.py:20
  58.9 2.1 %collective-permute-start.3 = (bf16[2,2,272,256]{3,2,1,0:T(8,128)(2,1)S(1)}, bf16[2,2,272,256]{3,2,1,0:T(8,128)(2,1)S(1)}, u32[]{:S(2)}, u32[]{:S(2)}) collective-permute-start(bf16[2,2,272,256]{3,2,1,0:T(8,128)(2,1)S(1)} %get-tuple-element.14), channel_id=1, source_target_pairs={{0,1},{1,0},{2,3},{3,2},{4,5},{5,4},{6,7},{7,6},{8,9},{9,8},{10,11... | collective-permute-start | bytes 1671176 | tf_op jit(solution)/shard_map/ppermute | solution.py:20
  61.1 9.9 %collective-permute-done.15 = bf16[4,128,256]{2,1,0:T(8,128)(2,1)} collective-permute-done((bf16[4,128,256]{2,1,0:T(8,128)(2,1)S(1)}, bf16[4,128,256]{2,1,0:T(8,128)(2,1)}, u32[]{:S(2)}, u32[]{:S(2)}) %collective-permute-start.15) | collective-permute-done | bytes 262176 | tf_op jit(solution)/shard_map/ppermute | solution.py:20
  71.0 1.0 broadcast_select_fusion.1
  72.0 3.1 %collective-permute-start.16 = (bf16[4,256,256]{2,1,0:T(8,128)(2,1)S(1)}, bf16[4,256,256]{2,1,0:T(8,128)(2,1)S(1)}, u32[]{:S(2)}, u32[]{:S(2)}) collective-permute-start(bf16[4,256,256]{2,1,0:T(8,128)(2,1)S(1)} %pad_maximum_fusion.2.w0), channel_id=1, source_target_pairs={{0,128},{8,136},{16,144},{24,152},{32,160},{40,168},{48,176},{56,1... | collective-permute-start | bytes 1572872 | tf_op jit(solution)/shard_map/ppermute | solution.py:20
  75.1 0.0 collective-permute-done.6
  75.1 4.4 %collective-permute-start.17 = (bf16[4,256,256]{2,1,0:T(8,128)(2,1)S(1)}, bf16[4,256,256]{2,1,0:T(8,128)(2,1)S(1)}, u32[]{:S(2)}, u32[]{:S(2)}) collective-permute-start(bf16[4,256,256]{2,1,0:T(8,128)(2,1)S(1)} %pad_maximum_fusion.2.w0), channel_id=1, source_target_pairs={{0,256},{8,264},{16,272},{24,280},{32,288},{40,296},{48,304},{56,3... | collective-permute-start | bytes 1572872 | tf_op jit(solution)/shard_map/ppermute | solution.py:20
  79.5 0.0 collective-permute-done.5
  79.5 2.1 %collective-permute-start.18 = (bf16[4,256,256]{2,1,0:T(8,128)(2,1)S(1)}, bf16[4,256,256]{2,1,0:T(8,128)(2,1)S(1)}, u32[]{:S(2)}, u32[]{:S(2)}) collective-permute-start(bf16[4,256,256]{2,1,0:T(8,128)(2,1)S(1)} %pad_maximum_fusion.2.w0), channel_id=1, source_target_pairs={{0,384},{8,392},{16,400},{24,408},{32,416},{40,424},{48,432},{56,4... | collective-permute-start | bytes 1572872 | tf_op jit(solution)/shard_map/ppermute | solution.py:20
  81.7 0.0 collective-permute-done.4
  81.7 21.4 %collective-permute-start.7 = (bf16[2,128,128]{2,1,0:T(8,128)(2,1)S(1)}, bf16[2,128,128]{2,1,0:T(8,128)(2,1)S(1)}, u32[]{:S(2)}, u32[]{:S(2)}) collective-permute-start(bf16[2,128,128]{2,1,0:T(8,128)(2,1)S(1)} %pad_maximum_fusion.8), channel_id=1, source_target_pairs={{0,32},{8,40},{16,48},{24,56},{32,0},{40,8},{48,16},{56,24},{64,96... | collective-permute-start | bytes 196616 | tf_op jit(solution)/shard_map/ppermute | solution.py:20
  103.1 1.5 pad_maximum_fusion
  104.6 0.0 collective-permute-done.16.w1
  104.7 0.0 copy-start.14
  104.7 1.3 project.3.mine
  106.0 0.0 copy-start.7
  106.0 4.9 %collective-permute-start.19 = (f32[272,256]{1,0:T(8,128)S(1)}, f32[272,256]{1,0:T(8,128)S(1)}, u32[]{:S(2)}, u32[]{:S(2)}) collective-permute-start(f32[272,256]{1,0:T(8,128)S(1)} %project.3.mine), channel_id=1, source_target_pairs={{0,8},{8,0},{16,24},{24,16},{32,40},{40,32},{48,56},{56,48},{64,72... | collective-permute-start | bytes 835592 | tf_op jit(solution)/shard_map/ppermute | solution.py:20
  110.9 0.0 collective-permute-done.7
  110.9 11.4 %collective-permute-start.8 = (bf16[4,128,128]{2,1,0:T(8,128)(2,1)S(1)}, bf16[4,128,128]{2,1,0:T(8,128)(2,1)S(1)}, u32[]{:S(2)}, u32[]{:S(2)}) collective-permute-start(bf16[4,128,128]{2,1,0:T(8,128)(2,1)S(1)} %pad_maximum_fusion.6), channel_id=1, source_target_pairs={{0,16},{8,24},{16,0},{24,8},{32,48},{40,56},{48,32},{56,40},{64,80... | collective-permute-start | bytes 393224 | tf_op jit(solution)/shard_map/ppermute | solution.py:20
  122.4 0.0 collective-permute-done.19.theirs
  122.4 0.3 drive.1
  122.7 1.9 %collective-permute-start.20 = (f32[16,128]{1,0:T(8,128)S(1)}, f32[16,128]{1,0:T(8,128)S(1)}, u32[]{:S(2)}, u32[]{:S(2)}) collective-permute-start(f32[16,128]{1,0:T(8,128)S(1)} %get-tuple-element.10), channel_id=1, source_target_pairs={{0,16},{8,24},{16,0},{24,8},{32,48},{40,56},{48,32},{56,40},{64,80... | collective-permute-start | bytes 24584 | tf_op jit(solution)/shard_map/ppermute | solution.py:20
  124.6 1.6 collective-permute-done.8
  126.2 0.9 collective-permute-done.20
  127.1 7.0 %collective-permute-start.21 = (f32[16,128]{1,0:T(8,128)S(1)}, f32[16,128]{1,0:T(8,128)S(1)}, u32[]{:S(2)}, u32[]{:S(2)}) collective-permute-start(f32[16,128]{1,0:T(8,128)S(1)} %add_select_fusion.3), channel_id=1, source_target_pairs={{0,32},{8,40},{16,48},{24,56},{32,0},{40,8},{48,16},{56,24},{64,96... | collective-permute-start | bytes 24584 | tf_op jit(solution)/shard_map/ppermute | solution.py:20
  134.2 2.1 %collective-permute-start.9 = (bf16[4,256,128]{2,1,0:T(8,128)(2,1)S(1)}, bf16[4,256,128]{2,1,0:T(8,128)(2,1)}, u32[]{:S(2)}, u32[]{:S(2)}) collective-permute-start(bf16[4,256,128]{2,1,0:T(8,128)(2,1)S(1)} %pad_maximum_fusion.4.w0), channel_id=1, source_target_pairs={{0,128},{8,136},{16,144},{24,152},{32,160},{40,168},{48,176},{56,1... | collective-permute-start | bytes 786440 | tf_op jit(solution)/shard_map/ppermute | solution.py:20
  136.2 3.0 %collective-permute-start.10 = (bf16[4,256,128]{2,1,0:T(8,128)(2,1)S(1)}, bf16[4,256,128]{2,1,0:T(8,128)(2,1)}, u32[]{:S(2)}, u32[]{:S(2)}) collective-permute-start(bf16[4,256,128]{2,1,0:T(8,128)(2,1)S(1)} %pad_maximum_fusion.4.w0), channel_id=1, source_target_pairs={{0,256},{8,264},{16,272},{24,280},{32,288},{40,296},{48,304},{56,3... | collective-permute-start | bytes 786440 | tf_op jit(solution)/shard_map/ppermute | solution.py:20
  139.3 4.6 %collective-permute-start.11 = (bf16[4,256,128]{2,1,0:T(8,128)(2,1)S(1)}, bf16[4,256,128]{2,1,0:T(8,128)(2,1)}, u32[]{:S(2)}, u32[]{:S(2)}) collective-permute-start(bf16[4,256,128]{2,1,0:T(8,128)(2,1)S(1)} %pad_maximum_fusion.4.w0), channel_id=1, source_target_pairs={{0,384},{8,392},{16,400},{24,408},{32,416},{40,424},{48,432},{56,4... | collective-permute-start | bytes 786440 | tf_op jit(solution)/shard_map/ppermute | solution.py:20
  143.9 0.0 collective-permute-done.21
  144.0 0.6 add_select_fusion.2
  144.6 6.4 %collective-permute-start.22 = (f32[16,128]{1,0:T(8,128)}, f32[16,128]{1,0:T(8,128)}, u32[]{:S(2)}, u32[]{:S(2)}) collective-permute-start(f32[16,128]{1,0:T(8,128)} %add_select_fusion.2), channel_id=1, source_target_pairs={{0,64},{8,72},{16,80},{24,88},{32,96},{40,104},{48,112},{56,120},{... | collective-permute-start | bytes 24584 | tf_op jit(solution)/shard_map/ppermute | solution.py:20
  151.0 0.0 copy-start.8
  151.0 0.0 copy-start.1
  151.1 2.1 %collective-permute-done.22 = f32[16,128]{1,0:T(8,128)} collective-permute-done((f32[16,128]{1,0:T(8,128)}, f32[16,128]{1,0:T(8,128)}, u32[]{:S(2)}, u32[]{:S(2)}) %collective-permute-start.22) | collective-permute-done | bytes 8224 | tf_op jit(solution)/shard_map/ppermute | solution.py:20
  153.2 0.7 add_select_fusion.1
  153.9 1.9 %collective-permute-start.23 = (f32[16,128]{1,0:T(8,128)S(1)}, f32[16,128]{1,0:T(8,128)S(1)}, u32[]{:S(2)}, u32[]{:S(2)}) collective-permute-start(f32[16,128]{1,0:T(8,128)S(1)} %add_select_fusion.1), channel_id=1, source_target_pairs={{0,128},{8,136},{16,144},{24,152},{32,160},{40,168},{48,176},{56,1... | collective-permute-start | bytes 24584 | tf_op jit(solution)/shard_map/ppermute | solution.py:20
  155.8 0.0 collective-permute-done.10.w2
  155.9 1.9 %project.2 = f32[272,128]{1,0:T(8,128)S(1)} custom-call(s32[16]{0:T(128)S(1)} %and_or_fusion.order, bf16[16,272,256]{2,1,0:T(8,128)(2,1)S(1)} %bitcast.52, bf16[4,256,128]{2,1,0:T(8,128)(2,1)S(1)} %pad_maximum_fusion.4.w0, bf16[4,256,128]{2,1,0:T(8,128)(2,1)} %collective-permute-done.9.w1, bf16[4,256,128]{2,1,0:T(8,128)(2,1)} %collective-permute-done.10.w2, ...), custom_call_target="tpu_custom_call" | custom-call | flops 285212672 | bytes 3276800 | tf_op jit(solution)/shard_map/project/pallas_call | solution.py:67
  157.7 0.6 collective-permute-done.23
  158.3 2.5 %collective-permute-start.24 = (f32[16,128]{1,0:T(8,128)S(1)}, f32[16,128]{1,0:T(8,128)S(1)}, u32[]{:S(2)}, u32[]{:S(2)}) collective-permute-start(f32[16,128]{1,0:T(8,128)S(1)} %add_select_fusion), channel_id=1, source_target_pairs={{0,256},{8,264},{16,272},{24,280},{32,288},{40,296},{48,304},{56,3... | collective-permute-start | bytes 24584 | tf_op jit(solution)/shard_map/ppermute | solution.py:20
  160.9 5.5 %collective-permute-start.12 = (f32[144,128]{1,0:T(8,128)S(1)}, f32[144,128]{1,0:T(8,128)S(1)}, u32[]{:S(2)}, u32[]{:S(2)}) collective-permute-start(f32[144,128]{1,0:T(8,128)S(1)} %get-tuple-element.23), channel_id=1, source_target_pairs={{0,8},{8,0},{16,24},{24,16},{32,40},{40,32},{48,56},{56,48},{64,72... | collective-permute-start | bytes 221192 | tf_op jit(solution)/shard_map/ppermute | solution.py:20
  166.4 0.0 copy-start.4
  166.4 0.6 copy-done.4
  167.1 0.3 near.1.inner
  167.4 0.7 select_add_fusion.carry
  168.2 0.8 finish.1
  (53 shorter events, 0.4 us)
Async XLA Ops:
  0.0 42.4 %copy-start.13 = (f32[128,16]{0,1:T(8,128)S(1)}, f32[128,16]{0,1:T(8,128)}, u32[]{:S(2)}) copy-start(f32[128,16]{0,1:T(8,128)} %param.9) | copy-start | bytes 24580
  0.0 42.4 %copy-start.6 = (f32[128,16]{0,1:T(8,128)S(1)}, f32[128,16]{0,1:T(8,128)}, u32[]{:S(2)}) copy-start(f32[128,16]{0,1:T(8,128)} %param.10) | copy-start | bytes 24580
  3.1 18.9 %collective-permute-start = (bf16[2,128,256]{2,1,0:T(8,128)(2,1)S(1)}, bf16[2,128,256]{2,1,0:T(8,128)(2,1)S(1)}, u32[]{:S(2)}, u32[]{:S(2)}) collective-permute-start(bf16[2,128,256]{2,1,0:T(8,128)(2,1)S(1)} %bitcast.58), channel_id=1, source_target_pairs={{0,8},{8,0},{16,24},{24,16},{32,40},{40,32},{48,56},{56,48},{64,72... | collective-permute-start | bytes 393224 | tf_op jit(solution)/shard_map/ppermute | solution.py:20
  12.7 62.5 %collective-permute-start.6 = (bf16[1,128,128]{2,1,0:T(8,128)(2,1)S(1)}, bf16[1,128,128]{2,1,0:T(8,128)(2,1)S(1)}, u32[]{:S(2)}, u32[]{:S(2)}) collective-permute-start(bf16[1,128,128]{2,1,0:T(8,128)(2,1)S(1)} %get-tuple-element.26), channel_id=1, source_target_pairs={{0,64},{8,72},{16,80},{24,88},{32,96},{40,104},{48,112},{56,120},{... | collective-permute-start | bytes 98312 | tf_op jit(solution)/shard_map/ppermute | solution.py:20
  16.1 8.9 %collective-permute-start.13 = (bf16[1,128,256]{2,1,0:T(8,128)(2,1)S(1)}, bf16[1,128,256]{2,1,0:T(8,128)(2,1)S(1)}, u32[]{:S(2)}, u32[]{:S(2)}) collective-permute-start(bf16[1,128,256]{2,1,0:T(8,128)(2,1)S(1)} %maximum_bitcast_fusion), channel_id=1, source_target_pairs={{0,64},{8,72},{16,80},{24,88},{32,96},{40,104},{48,112},{56,120},{... | collective-permute-start | bytes 196616 | tf_op jit(solution)/shard_map/ppermute | solution.py:20
  22.0 8.1 %collective-permute-start.1 = (bf16[2,16,256]{2,1,0:T(8,128)(2,1)S(1)}, bf16[2,16,256]{2,1,0:T(8,128)(2,1)S(1)}, u32[]{:S(2)}, u32[]{:S(2)}) collective-permute-start(bf16[2,16,256]{2,1,0:T(8,128)(2,1)S(1)} %slice.28), channel_id=1, source_target_pairs={{0,16},{8,24},{16,32},{24,40},{32,48},{40,56},{48,64},{56,72},{64,... | collective-permute-start | bytes 49160 | tf_op jit(solution)/shard_map/ppermute | solution.py:25
  25.1 17.4 %collective-permute-start.14 = (bf16[2,128,256]{2,1,0:T(8,128)(2,1)S(1)}, bf16[2,128,256]{2,1,0:T(8,128)(2,1)S(1)}, u32[]{:S(2)}, u32[]{:S(2)}) collective-permute-start(bf16[2,128,256]{2,1,0:T(8,128)(2,1)S(1)} %pad_maximum_fusion.7), channel_id=1, source_target_pairs={{0,32},{8,40},{16,48},{24,56},{32,0},{40,8},{48,16},{56,24},{64,96... | collective-permute-start | bytes 393224 | tf_op jit(solution)/shard_map/ppermute | solution.py:20
  30.2 19.1 %collective-permute-start.2 = (bf16[2,272,256]{2,1,0:T(8,128)(2,1)S(1)}, bf16[2,272,256]{2,1,0:T(8,128)(2,1)S(1)}, u32[]{:S(2)}, u32[]{:S(2)}) collective-permute-start(bf16[2,272,256]{2,1,0:T(8,128)(2,1)S(1)} %get-tuple-element.18), channel_id=1, source_target_pairs={{0,4},{1,5},{2,6},{3,7},{4,0},{5,1},{6,2},{7,3},{8,12},{9,13},{10,... | collective-permute-start | bytes 835592 | tf_op jit(solution)/shard_map/ppermute | solution.py:20
  42.5 28.5 %collective-permute-start.15 = (bf16[4,128,256]{2,1,0:T(8,128)(2,1)S(1)}, bf16[4,128,256]{2,1,0:T(8,128)(2,1)}, u32[]{:S(2)}, u32[]{:S(2)}) collective-permute-start(bf16[4,128,256]{2,1,0:T(8,128)(2,1)S(1)} %pad_maximum_fusion.5), channel_id=1, source_target_pairs={{0,16},{8,24},{16,0},{24,8},{32,48},{40,56},{48,32},{56,40},{64,80... | collective-permute-start | bytes 786440 | tf_op jit(solution)/shard_map/ppermute | solution.py:20
  50.2 29.3 %collective-permute-start.5 = (bf16[2,2,272,256]{3,2,1,0:T(8,128)(2,1)S(1)}, bf16[2,2,272,256]{3,2,1,0:T(8,128)(2,1)S(1)}, u32[]{:S(2)}, u32[]{:S(2)}) collective-permute-start(bf16[2,2,272,256]{3,2,1,0:T(8,128)(2,1)S(1)} %get-tuple-element.14), channel_id=1, source_target_pairs={{0,3},{1,2},{2,1},{3,0},{4,7},{5,6},{6,5},{7,4},{8,11},{9,10},{10,... | collective-permute-start | bytes 1671176 | tf_op jit(solution)/shard_map/ppermute | solution.py:20
  56.7 25.0 %collective-permute-start.4 = (bf16[2,2,272,256]{3,2,1,0:T(8,128)(2,1)S(1)}, bf16[2,2,272,256]{3,2,1,0:T(8,128)(2,1)S(1)}, u32[]{:S(2)}, u32[]{:S(2)}) collective-permute-start(bf16[2,2,272,256]{3,2,1,0:T(8,128)(2,1)S(1)} %get-tuple-element.14), channel_id=1, source_target_pairs={{0,2},{1,3},{2,0},{3,1},{4,6},{5,7},{6,4},{7,5},{8,10},{9,11},{10,... | collective-permute-start | bytes 1671176 | tf_op jit(solution)/shard_map/ppermute | solution.py:20
  58.9 44.2 %collective-permute-start.3 = (bf16[2,2,272,256]{3,2,1,0:T(8,128)(2,1)S(1)}, bf16[2,2,272,256]{3,2,1,0:T(8,128)(2,1)S(1)}, u32[]{:S(2)}, u32[]{:S(2)}) collective-permute-start(bf16[2,2,272,256]{3,2,1,0:T(8,128)(2,1)S(1)} %get-tuple-element.14), channel_id=1, source_target_pairs={{0,1},{1,0},{2,3},{3,2},{4,5},{5,4},{6,7},{7,6},{8,9},{9,8},{10,11... | collective-permute-start | bytes 1671176 | tf_op jit(solution)/shard_map/ppermute | solution.py:20
  72.0 32.6 %collective-permute-start.16 = (bf16[4,256,256]{2,1,0:T(8,128)(2,1)S(1)}, bf16[4,256,256]{2,1,0:T(8,128)(2,1)S(1)}, u32[]{:S(2)}, u32[]{:S(2)}) collective-permute-start(bf16[4,256,256]{2,1,0:T(8,128)(2,1)S(1)} %pad_maximum_fusion.2.w0), channel_id=1, source_target_pairs={{0,128},{8,136},{16,144},{24,152},{32,160},{40,168},{48,176},{56,1... | collective-permute-start | bytes 1572872 | tf_op jit(solution)/shard_map/ppermute | solution.py:20
  75.1 29.5 %collective-permute-start.17 = (bf16[4,256,256]{2,1,0:T(8,128)(2,1)S(1)}, bf16[4,256,256]{2,1,0:T(8,128)(2,1)S(1)}, u32[]{:S(2)}, u32[]{:S(2)}) collective-permute-start(bf16[4,256,256]{2,1,0:T(8,128)(2,1)S(1)} %pad_maximum_fusion.2.w0), channel_id=1, source_target_pairs={{0,256},{8,264},{16,272},{24,280},{32,288},{40,296},{48,304},{56,3... | collective-permute-start | bytes 1572872 | tf_op jit(solution)/shard_map/ppermute | solution.py:20
  79.5 23.6 %copy-start.5 = (bf16[2,2,272,256]{3,2,1,0:T(8,128)(2,1)}, bf16[2,2,272,256]{3,2,1,0:T(8,128)(2,1)S(1)}, u32[]{:S(2)}) copy-start(bf16[2,2,272,256]{3,2,1,0:T(8,128)(2,1)S(1)} %collective-permute-done.5) | copy-start | bytes 1671172
  79.5 25.1 %collective-permute-start.18 = (bf16[4,256,256]{2,1,0:T(8,128)(2,1)S(1)}, bf16[4,256,256]{2,1,0:T(8,128)(2,1)S(1)}, u32[]{:S(2)}, u32[]{:S(2)}) collective-permute-start(bf16[4,256,256]{2,1,0:T(8,128)(2,1)S(1)} %pad_maximum_fusion.2.w0), channel_id=1, source_target_pairs={{0,384},{8,392},{16,400},{24,408},{32,416},{40,424},{48,432},{56,4... | collective-permute-start | bytes 1572872 | tf_op jit(solution)/shard_map/ppermute | solution.py:20
  81.7 29.2 %collective-permute-start.7 = (bf16[2,128,128]{2,1,0:T(8,128)(2,1)S(1)}, bf16[2,128,128]{2,1,0:T(8,128)(2,1)S(1)}, u32[]{:S(2)}, u32[]{:S(2)}) collective-permute-start(bf16[2,128,128]{2,1,0:T(8,128)(2,1)S(1)} %pad_maximum_fusion.8), channel_id=1, source_target_pairs={{0,32},{8,40},{16,48},{24,56},{32,0},{40,8},{48,16},{56,24},{64,96... | collective-permute-start | bytes 196616 | tf_op jit(solution)/shard_map/ppermute | solution.py:20
  104.7 17.7 %copy-start.14 = (f32[3,128,3]{1,2,0:T(4,128)S(1)}, f32[3,128,3]{1,2,0:T(4,128)}, u32[]{:S(2)}) copy-start(f32[3,128,3]{1,2,0:T(4,128)} %param.8) | copy-start | bytes 13828
  106.0 38.0 %copy-start.7 = (f32[128,16]{0,1:T(8,128)S(1)}, f32[128,16]{0,1:T(8,128)}, u32[]{:S(2)}) copy-start(f32[128,16]{0,1:T(8,128)} %param.10) | copy-start | bytes 24580
  106.0 16.4 %collective-permute-start.19 = (f32[272,256]{1,0:T(8,128)S(1)}, f32[272,256]{1,0:T(8,128)S(1)}, u32[]{:S(2)}, u32[]{:S(2)}) collective-permute-start(f32[272,256]{1,0:T(8,128)S(1)} %project.3.mine), channel_id=1, source_target_pairs={{0,8},{8,0},{16,24},{24,16},{32,40},{40,32},{48,56},{56,48},{64,72... | collective-permute-start | bytes 835592 | tf_op jit(solution)/shard_map/ppermute | solution.py:20
  110.9 15.3 %collective-permute-start.8 = (bf16[4,128,128]{2,1,0:T(8,128)(2,1)S(1)}, bf16[4,128,128]{2,1,0:T(8,128)(2,1)S(1)}, u32[]{:S(2)}, u32[]{:S(2)}) collective-permute-start(bf16[4,128,128]{2,1,0:T(8,128)(2,1)S(1)} %pad_maximum_fusion.6), channel_id=1, source_target_pairs={{0,16},{8,24},{16,0},{24,8},{32,48},{40,56},{48,32},{56,40},{64,80... | collective-permute-start | bytes 393224 | tf_op jit(solution)/shard_map/ppermute | solution.py:20
  122.7 13.6 %copy-start.2 = (f32[128,128]{1,0:T(8,128)}, f32[128,128]{1,0:T(8,128)S(1)}, u32[]{:S(2)}) copy-start(f32[128,128]{1,0:T(8,128)S(1)} %get-tuple-element.8.driven) | copy-start | bytes 196612
  122.7 4.4 %collective-permute-start.20 = (f32[16,128]{1,0:T(8,128)S(1)}, f32[16,128]{1,0:T(8,128)S(1)}, u32[]{:S(2)}, u32[]{:S(2)}) collective-permute-start(f32[16,128]{1,0:T(8,128)S(1)} %get-tuple-element.10), channel_id=1, source_target_pairs={{0,16},{8,24},{16,0},{24,8},{32,48},{40,56},{48,32},{56,40},{64,80... | collective-permute-start | bytes 24584 | tf_op jit(solution)/shard_map/ppermute | solution.py:20
  127.1 17.5 %copy-start.9 = (f32[16,128]{1,0:T(8,128)}, f32[16,128]{1,0:T(8,128)S(1)}, u32[]{:S(2)}) copy-start(f32[16,128]{1,0:T(8,128)S(1)} %collective-permute-done.20) | copy-start | bytes 24580
  127.1 16.8 %collective-permute-start.21 = (f32[16,128]{1,0:T(8,128)S(1)}, f32[16,128]{1,0:T(8,128)S(1)}, u32[]{:S(2)}, u32[]{:S(2)}) collective-permute-start(f32[16,128]{1,0:T(8,128)S(1)} %add_select_fusion.3), channel_id=1, source_target_pairs={{0,32},{8,40},{16,48},{24,56},{32,0},{40,8},{48,16},{56,24},{64,96... | collective-permute-start | bytes 24584 | tf_op jit(solution)/shard_map/ppermute | solution.py:20
  134.1 34.0 %copy-start = (f32[16,128,128]{2,1,0:T(8,128)S(1)}, f32[16,128,128]{2,1,0:T(8,128)}, u32[]{:S(2)}) copy-start(f32[16,128,128]{2,1,0:T(8,128)} %get-tuple-element.28.reach) | copy-start | bytes 3145732
  134.2 21.7 %collective-permute-start.9 = (bf16[4,256,128]{2,1,0:T(8,128)(2,1)S(1)}, bf16[4,256,128]{2,1,0:T(8,128)(2,1)}, u32[]{:S(2)}, u32[]{:S(2)}) collective-permute-start(bf16[4,256,128]{2,1,0:T(8,128)(2,1)S(1)} %pad_maximum_fusion.4.w0), channel_id=1, source_target_pairs={{0,128},{8,136},{16,144},{24,152},{32,160},{40,168},{48,176},{56,1... | collective-permute-start | bytes 786440 | tf_op jit(solution)/shard_map/ppermute | solution.py:20
  136.2 19.6 %collective-permute-start.10 = (bf16[4,256,128]{2,1,0:T(8,128)(2,1)S(1)}, bf16[4,256,128]{2,1,0:T(8,128)(2,1)}, u32[]{:S(2)}, u32[]{:S(2)}) collective-permute-start(bf16[4,256,128]{2,1,0:T(8,128)(2,1)S(1)} %pad_maximum_fusion.4.w0), channel_id=1, source_target_pairs={{0,256},{8,264},{16,272},{24,280},{32,288},{40,296},{48,304},{56,3... | collective-permute-start | bytes 786440 | tf_op jit(solution)/shard_map/ppermute | solution.py:20
  139.3 16.6 %collective-permute-start.11 = (bf16[4,256,128]{2,1,0:T(8,128)(2,1)S(1)}, bf16[4,256,128]{2,1,0:T(8,128)(2,1)}, u32[]{:S(2)}, u32[]{:S(2)}) collective-permute-start(bf16[4,256,128]{2,1,0:T(8,128)(2,1)S(1)} %pad_maximum_fusion.4.w0), channel_id=1, source_target_pairs={{0,384},{8,392},{16,400},{24,408},{32,416},{40,424},{48,432},{56,4... | collective-permute-start | bytes 786440 | tf_op jit(solution)/shard_map/ppermute | solution.py:20
  143.9 0.6 copy-start.11
  144.6 8.6 %collective-permute-start.22 = (f32[16,128]{1,0:T(8,128)}, f32[16,128]{1,0:T(8,128)}, u32[]{:S(2)}, u32[]{:S(2)}) collective-permute-start(f32[16,128]{1,0:T(8,128)} %add_select_fusion.2), channel_id=1, source_target_pairs={{0,64},{8,72},{16,80},{24,88},{32,96},{40,104},{48,112},{56,120},{... | collective-permute-start | bytes 24584 | tf_op jit(solution)/shard_map/ppermute | solution.py:20
  151.0 7.3 %copy-start.8 = (f32[128,16]{0,1:T(8,128)S(1)}, f32[128,16]{0,1:T(8,128)}, u32[]{:S(2)}) copy-start(f32[128,16]{0,1:T(8,128)} %param.10) | copy-start | bytes 24580
  151.0 15.4 %copy-start.1 = (f32[128,128]{1,0:T(8,128)S(1)}, f32[128,128]{1,0:T(8,128)}, u32[]{:S(2)}) copy-start(f32[128,128]{1,0:T(8,128)} %get-tuple-element.29.taps) | copy-start | bytes 196612
  151.0 15.4 %copy-start.3 = (f32[128,128]{1,0:T(8,128)S(1)}, f32[128,128]{1,0:T(8,128)}, u32[]{:S(2)}) copy-start(f32[128,128]{1,0:T(8,128)} %copy-done.2) | copy-start | bytes 196612
  151.0 16.4 %copy-start.10 = (f32[16,128]{1,0:T(8,128)S(1)}, f32[16,128]{1,0:T(8,128)}, u32[]{:S(2)}) copy-start(f32[16,128]{1,0:T(8,128)} %copy-done.9) | copy-start | bytes 24580
  151.0 16.4 %copy-start.12 = (f32[16,128]{1,0:T(8,128)S(1)}, f32[16,128]{1,0:T(8,128)}, u32[]{:S(2)}) copy-start(f32[16,128]{1,0:T(8,128)} %copy-done.11) | copy-start | bytes 24580
  153.9 4.4 %collective-permute-start.23 = (f32[16,128]{1,0:T(8,128)S(1)}, f32[16,128]{1,0:T(8,128)S(1)}, u32[]{:S(2)}, u32[]{:S(2)}) collective-permute-start(f32[16,128]{1,0:T(8,128)S(1)} %add_select_fusion.1), channel_id=1, source_target_pairs={{0,128},{8,136},{16,144},{24,152},{32,160},{40,168},{48,176},{56,1... | collective-permute-start | bytes 24584 | tf_op jit(solution)/shard_map/ppermute | solution.py:20
  158.3 9.1 %collective-permute-start.24 = (f32[16,128]{1,0:T(8,128)S(1)}, f32[16,128]{1,0:T(8,128)S(1)}, u32[]{:S(2)}, u32[]{:S(2)}) collective-permute-start(f32[16,128]{1,0:T(8,128)S(1)} %add_select_fusion), channel_id=1, source_target_pairs={{0,256},{8,264},{16,272},{24,280},{32,288},{40,296},{48,304},{56,3... | collective-permute-start | bytes 24584 | tf_op jit(solution)/shard_map/ppermute | solution.py:20
  160.9 7.3 %collective-permute-start.12 = (f32[144,128]{1,0:T(8,128)S(1)}, f32[144,128]{1,0:T(8,128)S(1)}, u32[]{:S(2)}, u32[]{:S(2)}) collective-permute-start(f32[144,128]{1,0:T(8,128)S(1)} %get-tuple-element.23), channel_id=1, source_target_pairs={{0,8},{8,0},{16,24},{24,16},{32,40},{40,32},{48,56},{56,48},{64,72... | collective-permute-start | bytes 221192 | tf_op jit(solution)/shard_map/ppermute | solution.py:20
  166.4 0.7 copy-start.4

commit v2 on v1

v2 whole, which is shorter than its diff:
```python
import jax
import jax.numpy as jnp
from jax import lax
from jax.experimental import pallas as pl
from jax.experimental.pallas import tpu as pltpu
from jax.sharding import PartitionSpec as P

F32 = jnp.float32
BF16 = jnp.bfloat16
HALO = 16
BLOCK = 128
GROUP = 4 * BLOCK
ROWS = HALO + GROUP
PIECE = HALO + BLOCK
HALF = 80
MODES = 16
VMEM = pl.BlockSpec(memory_space=pltpu.VMEM)
SMEM = pl.BlockSpec(memory_space=pltpu.SMEM)
PARAMS = pltpu.CompilerParams(vmem_limit_bytes=48 * 1024 * 1024)


def flip(x, axis, mask):
    length = lax.axis_size(axis)
    return lax.ppermute(x, axis, [(i, i ^ mask) for i in range(length)])


def ahead(x, axis, by):
    length = lax.axis_size(axis)
    return lax.ppermute(x, axis, [(i, i + by) for i in range(length - by)])


def ordered(upper, own, other, axis):
    first = jnp.where(upper, other, own)
    second = jnp.where(upper, own, other)
    return jnp.concatenate([first, second], axis=axis)


def split_kernel(place, tokens, halo, kept, given):
    core = place[0] & 1
    for out, side in ((kept, core), (given, 1 - core)):
        for bit8 in range(2):
            for bit9 in range(2):
                start = pl.multiple_of(512 * bit9 + 256 * bit8 + side * 128, 128)
                there = slice(128 * bit9, 128 * bit9 + 128)
                out[bit8, :HALO, there] = halo[:, pl.ds(start, 128)]
                out[bit8, HALO:, there] = tokens[:, pl.ds(start, 128)]


def split(place, tokens, halo):
    shape = jax.ShapeDtypeStruct((2, PIECE, 256), BF16)
    return pl.pallas_call(
        split_kernel,
        out_shape=(shape, shape),
        in_specs=[SMEM, VMEM, VMEM],
        out_specs=(VMEM, VMEM),
        compiler_params=PARAMS,
        name="split",
    )(place, tokens, halo)


def joined(upper, own, other, axis):
    first = jnp.where(upper, other, own)
    second = jnp.where(upper, own, other)
    rest = lax.slice_in_dim(second, HALO, second.shape[axis], axis=axis)
    return jnp.concatenate([first, rest], axis=axis)


def gather_tokens(tokens, place):
    halo = ahead(tokens[BLOCK - HALO :], "ctx", 1)
    kept, given = split(place[None], tokens, halo)
    both = joined((place & 1) == 1, kept, flip(given, "ctx", 1), 1)
    upper = (place & 2) == 2
    keep = jnp.where(upper, both[1], both[0])
    give = jnp.where(upper, both[0], both[1])
    near_h = joined(upper, keep, flip(give, "ctx", 2), 0)
    far_h = flip(near_h, "tp", 4)
    found = []
    for part in (near_h, far_h):
        found += [part] + [flip(part, "tp", m) for m in (1, 2, 3)]
    return found


def gather_weights(piece, place):
    held = piece[None]
    held = jnp.concatenate([held, flip(held, "ctx", 8)], axis=0)
    held = ordered((place & 4) == 4, held, flip(held, "ctx", 4), 1)
    return [held] + [flip(held, "ctx", m << 4) for m in (1, 2, 3)]


def project_kernel(match, t0, t1, t2, t3, t4, t5, t6, t7, w0, w1, w2, w3, out):
    tokens, weights = (t0, t1, t2, t3, t4, t5, t6, t7), (w0, w1, w2, w3)
    for case in range(4):

        @pl.when(match[0] == case)
        def _():
            total = jnp.zeros(out.shape, F32)
            for turn in range(8):
                turn_h, turn_y = turn >> 2, turn & 3
                turn_x = case ^ (turn_h << 1 | turn_y >> 1)
                weight = weights[turn_x][match[1] ^ (turn_y & 1)]
                total += jnp.dot(tokens[turn][...], weight, preferred_element_type=F32)
            out[...] = total


def project(match, tokens, weights):
    columns = weights[0].shape[2]
    return pl.pallas_call(
        project_kernel,
        out_shape=jax.ShapeDtypeStruct((ROWS, columns), F32),
        in_specs=[SMEM] + [VMEM] * 12,
        out_specs=VMEM,
        compiler_params=PARAMS,
        cost_estimate=pl.CostEstimate(
            flops=2 * ROWS * 2048 * columns, bytes_accessed=2048 * 2 * (ROWS + columns), transcendentals=0
        ),
        name="project",
    )(match, *tokens, *weights)


def merge_kernel(place, mine, theirs, total, gift):
    total[...] = mine[...] + theirs[...]
    gift[:ROWS] = total[:, : 2 * BLOCK].astype(BF16)
    start = pl.multiple_of(((place[0] & 3) ^ 2) * BLOCK, BLOCK)
    gift[ROWS:, :BLOCK] = total[pl.ds(start, HALF), 2 * BLOCK :].astype(BF16)
    start = pl.multiple_of(start + PIECE - HALF, 16)
    gift[ROWS:, BLOCK:] = total[pl.ds(start, HALF), 2 * BLOCK :].astype(BF16)


def merge(place, mine, theirs):
    return pl.pallas_call(
        merge_kernel,
        out_shape=(
            jax.ShapeDtypeStruct(mine.shape, F32),
            jax.ShapeDtypeStruct((ROWS + HALF, 2 * BLOCK), BF16),
        ),
        in_specs=[SMEM, VMEM, VMEM],
        out_specs=(VMEM, VMEM),
        compiler_params=PARAMS,
        name="merge",
    )(place, mine, theirs)


def short(proj, taps):
    n = proj.shape[0] - HALO
    return (
        taps[0:1] * proj[HALO : HALO + n]
        + taps[1:2] * proj[HALO - 1 : HALO - 1 + n]
        + taps[2:3] * proj[HALO - 2 : HALO - 2 + n]
    )


def rounded(x):
    return x.astype(BF16).astype(F32)


def drive_kernel(place, mine, theirs, taps, weigh, step, query, driven, before, state, signal):
    spot = place[0] & 3
    pair = rounded(mine[:, : 2 * BLOCK] + theirs[:ROWS].astype(F32))
    key = short(pair[:, :BLOCK], taps[1])
    value = short(pair[:, BLOCK:], taps[2])
    signal[...] = key * value
    start = pl.multiple_of(spot * BLOCK, BLOCK)
    driven[...] = signal[pl.ds(start, BLOCK)]
    own = mine[pl.ds(start, PIECE), 2 * BLOCK :]
    other = theirs[ROWS:].astype(F32)
    other = jnp.concatenate([other[:, :BLOCK], other[2 * HALF - PIECE :, BLOCK:]], axis=0)
    query[...] = short(rounded(own + other), taps[0])
    for r in range(MODES):
        w, decay = weigh[r], step[r : r + 1]
        past = jnp.zeros((1, BLOCK), F32)
        held = past
        for b in range(4):
            held = jnp.where(spot == b, past, held)
            past = decay * past + jnp.sum(w * signal[BLOCK * b : BLOCK * b + BLOCK], axis=0, keepdims=True)
        before[r : r + 1] = held
        state[r : r + 1] = past


def drive(place, mine, theirs, taps, weigh, step):
    square = jax.ShapeDtypeStruct((BLOCK, BLOCK), F32)
    modes = jax.ShapeDtypeStruct((MODES, BLOCK), F32)
    return pl.pallas_call(
        drive_kernel,
        out_shape=(square, square, modes, modes),
        in_specs=[SMEM] + [VMEM] * 5,
        out_specs=(VMEM,) * 4,
        scratch_shapes=[pltpu.VMEM((GROUP, BLOCK), F32)],
        compiler_params=PARAMS,
        name="drive",
    )(place, mine, theirs, taps, weigh, step)


def near_kernel(driven, taps, gain, out, padded):
    signal = driven[...]
    padded[:BLOCK] = jnp.zeros((BLOCK, BLOCK), F32)
    padded[BLOCK:] = signal
    total = gain[...] * signal
    for s in range(BLOCK):
        low = s // 8 * 8
        part = taps[s : s + 1] * padded[BLOCK + low - s : 2 * BLOCK - s]
        if low:
            part = jnp.concatenate([jnp.zeros((low, BLOCK), F32), part], axis=0)
        total = total + part
    out[...] = total


def near(driven, taps, gain):
    return pl.pallas_call(
        near_kernel,
        out_shape=jax.ShapeDtypeStruct((BLOCK, BLOCK), F32),
        in_specs=[VMEM] * 3,
        out_specs=VMEM,
        scratch_shapes=[pltpu.VMEM((2 * BLOCK, BLOCK), F32)],
        compiler_params=PARAMS,
        cost_estimate=pl.CostEstimate(flops=2 * BLOCK**3, bytes_accessed=3 * BLOCK * BLOCK * 4, transcendentals=0),
        name="near",
    )(driven, taps, gain)


def finish_kernel(query, inner, reach, carry, out):
    conv = inner[...]
    for r in range(MODES):
        conv = conv + reach[r] * carry[r : r + 1]
    out[...] = (query[...] * conv).T


def finish(query, inner, reach, carry):
    return pl.pallas_call(
        finish_kernel,
        out_shape=jax.ShapeDtypeStruct((BLOCK, BLOCK), F32),
        in_specs=[VMEM] * 4,
        out_specs=VMEM,
        compiler_params=PARAMS,
        name="finish",
    )(query, inner, reach, carry)


def body(tokens, in_weight, short_taps, residues, rates, skip_gain):
    place = lax.axis_index("ctx")
    tp = lax.axis_index("tp")

    rate = rates.T
    amount = residues.T * jnp.sqrt(2.0 * rate)
    index = jnp.arange(BLOCK, dtype=F32)[None, :, None]
    weigh = jnp.exp(-rate[:, None, :] * (BLOCK - 1.0 - index))
    reach = amount[:, None, :] * jnp.exp(-rate[:, None, :] * (index + 1.0))
    taps = jnp.sum(amount[:, None, :] * jnp.exp(-rate[:, None, :] * index), axis=0)
    step = jnp.exp(-rate * float(BLOCK))

    weights = gather_weights(jnp.concatenate([in_weight[1], in_weight[2], in_weight[0]], axis=1), place)
    features = gather_tokens(tokens, place)
    apart = tp ^ (place >> 3)
    match = jnp.stack([apart >> 1, apart & 1])

    spot = place[None]
    mine = project(match, features, weights)
    total, gift = merge(spot, mine, flip(mine, "ctx", 1))
    theirs = flip(gift, "ctx", 2)
    short_rows = short_taps.transpose(0, 2, 1)
    query, driven, before, state = drive(spot, total, theirs, short_rows, weigh, step)
    inner = near(driven, taps, skip_gain[None])

    for bit in range(2, 6):
        size = 1 << bit
        upper = (place & size) == size
        past = flip(state, "ctx", size)
        whole = jnp.exp(-rate * float(BLOCK * size))
        since = jnp.exp(-rate * (BLOCK * (place & (size - 1))).astype(F32))
        before = before + jnp.where(upper, since * past, 0.0)
        if bit < 5:
            state = jnp.where(upper, state + whole * past, whole * state + past)

    return finish(query, inner, reach, before)


def solution(mesh):
    in_specs = (
        P("ctx", "tp"),
        P(None, "ctx", "tp"),
        P(None, "tp", None),
        P("tp", None),
        P("tp", None),
        P("tp"),
    )
    return jax.shard_map(
        body, mesh=mesh, in_specs=in_specs, out_specs=P("tp", "ctx"), check_vma=False
    )
```

time: 171 us -> 152 us (0.89)
  the two profiles are of different devices: /device:TPU:1 before, /device:TPU:32 now
where the time goes in v2:
time: 152 us; the launch traced here: 151 us
  starting transfers between devices  97.4 us (64%)
  waiting for transfers between devices  46.2 us (30%)
  Pallas kernels  4.34 us (3%)
    ppermute x20, starting transfers between devices, flip(): return lax.ppermute(x, axis, [(i, i ^ mask) for i in range(length)])  95.4 us
    ppermute x20, waiting for transfers between devices, flip(): return lax.ppermute(x, axis, [(i, i ^ mask) for i in range(length)])  42.9 us
    ppermute x1, waiting for transfers between devices, ahead(): return lax.ppermute(x, axis, [(i, i + by) for i in range(length - by)])  3.3 us
  transfers between devices with their start and end apart: 21, of which 12 were waited for; matrix products, arithmetic and copies ran while one was open for 1% of the time, Pallas kernels for 0%

profile of v2, /device:TPU:32, one launch (start us, length us, event | category | flops | bytes accessed | tf_op | source)
XLA Modules:
  0.0 150.9 jit_solution(5564464188025515086)
XLA Ops:
  0.0 0.0 copy-start
  0.0 0.8 slice_bitcast_fusion.2
  0.9 9.1 %collective-permute-start.10 = (bf16[1,128,384]{2,1,0:T(8,128)(2,1)S(1)}, bf16[1,128,384]{2,1,0:T(8,128)(2,1)S(1)}, u32[]{:S(2)}, u32[]{:S(2)}) collective-permute-start(bf16[1,128,384]{2,1,0:T(8,128)(2,1)S(1)} %maximum_bitcast_fusion), channel_id=1, source_target_pairs={{0,64},{8,72},{16,80},{24,88},{32,96},{40,104},{48,112},{56,120},{... | collective-permute-start | bytes 294920 | tf_op jit(solution)/shard_map/ppermute | solution.py:24
  10.0 0.0 copy-done
  10.0 1.9 %collective-permute-start = (bf16[16,1024]{1,0:T(8,128)(2,1)S(1)}, bf16[16,1024]{1,0:T(8,128)(2,1)S(1)}, u32[]{:S(2)}, u32[]{:S(2)}) collective-permute-start(bf16[16,1024]{1,0:T(8,128)(2,1)S(1)} %slice.26), channel_id=1, source_target_pairs={{0,8},{8,16},{16,24},{24,32},{32,40},{40,48},{48,56},{56,64},{64,7... | collective-permute-start | bytes 98312 | tf_op jit(solution)/shard_map/ppermute | solution.py:29
  11.9 3.3 %collective-permute-done.halo = bf16[16,1024]{1,0:T(8,128)(2,1)S(1)} collective-permute-done((bf16[16,1024]{1,0:T(8,128)(2,1)S(1)}, bf16[16,1024]{1,0:T(8,128)(2,1)S(1)}, u32[]{:S(2)}, u32[]{:S(2)}) %collective-permute-start) | collective-permute-done | bytes 32800 | tf_op jit(solution)/shard_map/ppermute | solution.py:29
  15.2 0.1 split.1
  15.3 1.9 %collective-permute-start.1 = (bf16[2,144,256]{2,1,0:T(8,128)(2,1)S(1)}, bf16[2,144,256]{2,1,0:T(8,128)(2,1)S(1)}, u32[]{:S(2)}, u32[]{:S(2)}) collective-permute-start(bf16[2,144,256]{2,1,0:T(8,128)(2,1)S(1)} %get-tuple-element.13), channel_id=1, source_target_pairs={{0,8},{8,0},{16,24},{24,16},{32,40},{40,32},{48,56},{56,48},{64,72... | collective-permute-start | bytes 442376 | tf_op jit(solution)/shard_map/ppermute | solution.py:24
  17.2 0.0 collective-permute-done.10
  17.3 7.4 %collective-permute-start.11 = (bf16[2,128,384]{2,1,0:T(8,128)(2,1)S(1)}, bf16[2,128,384]{2,1,0:T(8,128)(2,1)S(1)}, u32[]{:S(2)}, u32[]{:S(2)}) collective-permute-start(bf16[2,128,384]{2,1,0:T(8,128)(2,1)S(1)} %pad_maximum_fusion.2), channel_id=1, source_target_pairs={{0,32},{8,40},{16,48},{24,56},{32,0},{40,8},{48,16},{56,24},{64,96... | collective-permute-start | bytes 589832 | tf_op jit(solution)/shard_map/ppermute | solution.py:24
  24.7 0.0 collective-permute-done.1
  24.8 1.9 %collective-permute-start.2 = (bf16[272,256]{1,0:T(8,128)(2,1)S(1)}, bf16[272,256]{1,0:T(8,128)(2,1)S(1)}, u32[]{:S(2)}, u32[]{:S(2)}) collective-permute-start(bf16[272,256]{1,0:T(8,128)(2,1)S(1)} %select_bitcast_fusion.1), channel_id=1, source_target_pairs={{0,16},{8,24},{16,0},{24,8},{32,48},{40,56},{48,32},{56,40},{64,80... | collective-permute-start | bytes 417800 | tf_op jit(solution)/shard_map/ppermute | solution.py:24
  26.7 4.5 %collective-permute-done.11 = bf16[2,128,384]{2,1,0:T(8,128)(2,1)S(1)} collective-permute-done((bf16[2,128,384]{2,1,0:T(8,128)(2,1)S(1)}, bf16[2,128,384]{2,1,0:T(8,128)(2,1)S(1)}, u32[]{:S(2)}, u32[]{:S(2)}) %collective-permute-start.11) | collective-permute-done | bytes 196640 | tf_op jit(solution)/shard_map/ppermute | solution.py:24
  31.2 0.1 broadcast_select_fusion.1
  31.2 0.8 collective-permute-done.2
  32.0 0.1 broadcast_select_fusion.3
  32.1 12.1 %collective-permute-start.6 = (bf16[528,256]{1,0:T(8,128)(2,1)S(1)}, bf16[528,256]{1,0:T(8,128)(2,1)S(1)}, u32[]{:S(2)}, u32[]{:S(2)}) collective-permute-start(bf16[528,256]{1,0:T(8,128)(2,1)S(1)} %pad_maximum_fusion.1.t0), channel_id=1, source_target_pairs={{0,4},{1,5},{2,6},{3,7},{4,0},{5,1},{6,2},{7,3},{8,12},{9,13},{10,... | collective-permute-start | bytes 811016 | tf_op jit(solution)/shard_map/ppermute | solution.py:24
  44.2 3.5 %collective-permute-start.3 = (bf16[528,256]{1,0:T(8,128)(2,1)S(1)}, bf16[528,256]{1,0:T(8,128)(2,1)S(1)}, u32[]{:S(2)}, u32[]{:S(2)}) collective-permute-start(bf16[528,256]{1,0:T(8,128)(2,1)S(1)} %pad_maximum_fusion.1.t0), channel_id=1, source_target_pairs={{0,1},{1,0},{2,3},{3,2},{4,5},{5,4},{6,7},{7,6},{8,9},{9,8},{10,11... | collective-permute-start | bytes 811016 | tf_op jit(solution)/shard_map/ppermute | solution.py:24
  47.7 5.8 %collective-permute-start.12 = (bf16[2,256,384]{2,1,0:T(8,128)(2,1)S(1)}, bf16[2,256,384]{2,1,0:T(8,128)(2,1)S(1)}, u32[]{:S(2)}, u32[]{:S(2)}) collective-permute-start(bf16[2,256,384]{2,1,0:T(8,128)(2,1)S(1)} %pad_maximum_fusion.w0), channel_id=1, source_target_pairs={{0,128},{8,136},{16,144},{24,152},{32,160},{40,168},{48,176},{56,1... | collective-permute-start | bytes 1179656 | tf_op jit(solution)/shard_map/ppermute | solution.py:24
  53.5 4.8 %collective-permute-start.4 = (bf16[528,256]{1,0:T(8,128)(2,1)S(1)}, bf16[528,256]{1,0:T(8,128)(2,1)S(1)}, u32[]{:S(2)}, u32[]{:S(2)}) collective-permute-start(bf16[528,256]{1,0:T(8,128)(2,1)S(1)} %pad_maximum_fusion.1.t0), channel_id=1, source_target_pairs={{0,2},{1,3},{2,0},{3,1},{4,6},{5,7},{6,4},{7,5},{8,10},{9,11},{10,... | collective-permute-start | bytes 811016 | tf_op jit(solution)/shard_map/ppermute | solution.py:24
  58.3 2.1 %collective-permute-start.5 = (bf16[528,256]{1,0:T(8,128)(2,1)S(1)}, bf16[528,256]{1,0:T(8,128)(2,1)S(1)}, u32[]{:S(2)}, u32[]{:S(2)}) collective-permute-start(bf16[528,256]{1,0:T(8,128)(2,1)S(1)} %pad_maximum_fusion.1.t0), channel_id=1, source_target_pairs={{0,3},{1,2},{2,1},{3,0},{4,7},{5,6},{6,5},{7,4},{8,11},{9,10},{10,... | collective-permute-start | bytes 811016 | tf_op jit(solution)/shard_map/ppermute | solution.py:24
  60.5 0.0 collective-permute-done.6.t4
  60.5 17.0 %collective-permute-start.13 = (bf16[2,256,384]{2,1,0:T(8,128)(2,1)S(1)}, bf16[2,256,384]{2,1,0:T(8,128)(2,1)S(1)}, u32[]{:S(2)}, u32[]{:S(2)}) collective-permute-start(bf16[2,256,384]{2,1,0:T(8,128)(2,1)S(1)} %pad_maximum_fusion.w0), channel_id=1, source_target_pairs={{0,256},{8,264},{16,272},{24,280},{32,288},{40,296},{48,304},{56,3... | collective-permute-start | bytes 1179656 | tf_op jit(solution)/shard_map/ppermute | solution.py:24
  77.5 0.0 collective-permute-done.3.t1
  77.5 3.0 %collective-permute-start.14 = (bf16[2,256,384]{2,1,0:T(8,128)(2,1)S(1)}, bf16[2,256,384]{2,1,0:T(8,128)(2,1)S(1)}, u32[]{:S(2)}, u32[]{:S(2)}) collective-permute-start(bf16[2,256,384]{2,1,0:T(8,128)(2,1)S(1)} %pad_maximum_fusion.w0), channel_id=1, source_target_pairs={{0,384},{8,392},{16,400},{24,408},{32,416},{40,424},{48,432},{56,4... | collective-permute-start | bytes 1179656 | tf_op jit(solution)/shard_map/ppermute | solution.py:24
  80.6 0.0 collective-permute-done.4.t2
  80.6 3.5 %collective-permute-start.7 = (bf16[528,256]{1,0:T(8,128)(2,1)S(1)}, bf16[528,256]{1,0:T(8,128)(2,1)S(1)}, u32[]{:S(2)}, u32[]{:S(2)}) collective-permute-start(bf16[528,256]{1,0:T(8,128)(2,1)S(1)} %collective-permute-done.6.t4), channel_id=1, source_target_pairs={{0,1},{1,0},{2,3},{3,2},{4,5},{5,4},{6,7},{7,6},{8,9},{9,8},{10,11... | collective-permute-start | bytes 811016 | tf_op jit(solution)/shard_map/ppermute | solution.py:24
  84.1 0.0 collective-permute-done.5.t3
  84.1 4.8 %collective-permute-start.8 = (bf16[528,256]{1,0:T(8,128)(2,1)S(1)}, bf16[528,256]{1,0:T(8,128)(2,1)S(1)}, u32[]{:S(2)}, u32[]{:S(2)}) collective-permute-start(bf16[528,256]{1,0:T(8,128)(2,1)S(1)} %collective-permute-done.6.t4), channel_id=1, source_target_pairs={{0,2},{1,3},{2,0},{3,1},{4,6},{5,7},{6,4},{7,5},{8,10},{9,11},{10,... | collective-permute-start | bytes 811016 | tf_op jit(solution)/shard_map/ppermute | solution.py:24
  88.9 0.0 collective-permute-done.12.w1
  88.9 2.1 %collective-permute-start.9 = (bf16[528,256]{1,0:T(8,128)(2,1)S(1)}, bf16[528,256]{1,0:T(8,128)(2,1)}, u32[]{:S(2)}, u32[]{:S(2)}) collective-permute-start(bf16[528,256]{1,0:T(8,128)(2,1)S(1)} %collective-permute-done.6.t4), channel_id=1, source_target_pairs={{0,3},{1,2},{2,1},{3,0},{4,7},{5,6},{6,5},{7,4},{8,11},{9,10},{10,... | collective-permute-start | bytes 811016 | tf_op jit(solution)/shard_map/ppermute | solution.py:24
  91.1 0.1 pad_add_fusion.match
  91.2 0.0 copy-start.3
  91.2 0.0 collective-permute-done.13.w2
  91.2 3.3 %collective-permute-done.14.w3 = bf16[2,256,384]{2,1,0:T(8,128)(2,1)S(1)} collective-permute-done((bf16[2,256,384]{2,1,0:T(8,128)(2,1)S(1)}, bf16[2,256,384]{2,1,0:T(8,128)(2,1)S(1)}, u32[]{:S(2)}, u32[]{:S(2)}) %collective-permute-start.14) | collective-permute-done | bytes 393248 | tf_op jit(solution)/shard_map/ppermute | solution.py:24
  94.4 0.0 collective-permute-done.7.t5
  94.4 3.5 %collective-permute-done.8.t6 = bf16[528,256]{1,0:T(8,128)(2,1)S(1)} collective-permute-done((bf16[528,256]{1,0:T(8,128)(2,1)S(1)}, bf16[528,256]{1,0:T(8,128)(2,1)S(1)}, u32[]{:S(2)}, u32[]{:S(2)}) %collective-permute-start.8) | collective-permute-done | bytes 270368 | tf_op jit(solution)/shard_map/ppermute | solution.py:24
  97.9 5.0 %collective-permute-done.9.t7 = bf16[528,256]{1,0:T(8,128)(2,1)} collective-permute-done((bf16[528,256]{1,0:T(8,128)(2,1)S(1)}, bf16[528,256]{1,0:T(8,128)(2,1)}, u32[]{:S(2)}, u32[]{:S(2)}) %collective-permute-start.9) | collective-permute-done | bytes 270368 | tf_op jit(solution)/shard_map/ppermute | solution.py:24
  102.9 2.3 %project.1.mine = f32[528,384]{1,0:T(8,128)S(1)} custom-call(s32[2]{0:T(128)S(1)} %pad_add_fusion.match, bf16[528,256]{1,0:T(8,128)(2,1)S(1)} %pad_maximum_fusion.1.t0, bf16[528,256]{1,0:T(8,128)(2,1)S(1)} %collective-permute-done.3.t1, bf16[528,256]{1,0:T(8,128)(2,1)S(1)} %collective-permute-done.4.t2, bf16[528,256]{1,0:T(8,128)(2,1)S(1)} %collective-permute-done.5.t3, ...), custom_call_target="tpu_custom_call" | custom-call | flops 830472192 | bytes 3735552 | tf_op jit(solution)/shard_map/project/pallas_call | solution.py:107
  105.1 0.0 copy-start.4
  105.2 1.9 %collective-permute-start.15 = (f32[528,384]{1,0:T(8,128)S(1)}, f32[528,384]{1,0:T(8,128)S(1)}, u32[]{:S(2)}, u32[]{:S(2)}) collective-permute-start(f32[528,384]{1,0:T(8,128)S(1)} %project.1.mine), channel_id=1, source_target_pairs={{0,8},{8,0},{16,24},{24,16},{32,40},{40,32},{48,56},{56,48},{64,72... | collective-permute-start | bytes 2433032 | tf_op jit(solution)/shard_map/ppermute | solution.py:24
  107.1 0.0 copy-done.3
  107.1 0.0 copy-done.4
  107.1 2.2 %collective-permute-done.15.theirs = f32[528,384]{1,0:T(8,128)S(1)} collective-permute-done((f32[528,384]{1,0:T(8,128)S(1)}, f32[528,384]{1,0:T(8,128)S(1)}, u32[]{:S(2)}, u32[]{:S(2)}) %collective-permute-start.15) | collective-permute-done | bytes 811040 | tf_op jit(solution)/shard_map/ppermute | solution.py:24
  109.4 0.1 merge.1
  109.5 1.9 %collective-permute-start.16 = (bf16[608,256]{1,0:T(8,128)(2,1)S(1)}, bf16[608,256]{1,0:T(8,128)(2,1)S(1)}, u32[]{:S(2)}, u32[]{:S(2)}) collective-permute-start(bf16[608,256]{1,0:T(8,128)(2,1)S(1)} %get-tuple-element.16), channel_id=1, source_target_pairs={{0,16},{8,24},{16,0},{24,8},{32,48},{40,56},{48,32},{56,40},{64,80... | collective-permute-start | bytes 933896 | tf_op jit(solution)/shard_map/ppermute | solution.py:24
  111.4 0.0 copy-start.1
  111.4 0.6 exponential_multiply_fusion
  112.0 8.8 %collective-permute-done.16.theirs = bf16[608,256]{1,0:T(8,128)(2,1)S(1)} collective-permute-done((bf16[608,256]{1,0:T(8,128)(2,1)S(1)}, bf16[608,256]{1,0:T(8,128)(2,1)S(1)}, u32[]{:S(2)}, u32[]{:S(2)}) %collective-permute-start.16) | collective-permute-done | bytes 311328 | tf_op jit(solution)/shard_map/ppermute | solution.py:24
  120.8 0.0 copy-done.1
  120.8 0.8 drive.1
  121.6 1.9 %collective-permute-start.17 = (f32[16,128]{1,0:T(8,128)S(1)}, f32[16,128]{1,0:T(8,128)S(1)}, u32[]{:S(2)}, u32[]{:S(2)}) collective-permute-start(f32[16,128]{1,0:T(8,128)S(1)} %get-tuple-element.20), channel_id=1, source_target_pairs={{0,32},{8,40},{16,48},{24,56},{32,0},{40,8},{48,16},{56,24},{64,96... | collective-permute-start | bytes 24584 | tf_op jit(solution)/shard_map/ppermute | solution.py:24
  123.5 4.5 %collective-permute-done.17 = f32[16,128]{1,0:T(8,128)S(1)} collective-permute-done((f32[16,128]{1,0:T(8,128)S(1)}, f32[16,128]{1,0:T(8,128)S(1)}, u32[]{:S(2)}, u32[]{:S(2)}) %collective-permute-start.17) | collective-permute-done | bytes 8224 | tf_op jit(solution)/shard_map/ppermute | solution.py:24
  128.0 5.2 %collective-permute-start.18 = (f32[16,128]{1,0:T(8,128)S(1)}, f32[16,128]{1,0:T(8,128)S(1)}, u32[]{:S(2)}, u32[]{:S(2)}) collective-permute-start(f32[16,128]{1,0:T(8,128)S(1)} %add_select_fusion.2), channel_id=1, source_target_pairs={{0,64},{8,72},{16,80},{24,88},{32,96},{40,104},{48,112},{56,120},{... | collective-permute-start | bytes 24584 | tf_op jit(solution)/shard_map/ppermute | solution.py:24
  133.2 4.2 %collective-permute-done.18 = f32[16,128]{1,0:T(8,128)S(1)} collective-permute-done((f32[16,128]{1,0:T(8,128)S(1)}, f32[16,128]{1,0:T(8,128)S(1)}, u32[]{:S(2)}, u32[]{:S(2)}) %collective-permute-start.18) | collective-permute-done | bytes 8224 | tf_op jit(solution)/shard_map/ppermute | solution.py:24
  137.5 1.9 %collective-permute-start.19 = (f32[16,128]{1,0:T(8,128)S(1)}, f32[16,128]{1,0:T(8,128)S(1)}, u32[]{:S(2)}, u32[]{:S(2)}) collective-permute-start(f32[16,128]{1,0:T(8,128)S(1)} %add_select_fusion.1), channel_id=1, source_target_pairs={{0,128},{8,136},{16,144},{24,152},{32,160},{40,168},{48,176},{56,1... | collective-permute-start | bytes 24584 | tf_op jit(solution)/shard_map/ppermute | solution.py:24
  139.4 3.6 %collective-permute-done.19 = f32[16,128]{1,0:T(8,128)S(1)} collective-permute-done((f32[16,128]{1,0:T(8,128)S(1)}, f32[16,128]{1,0:T(8,128)S(1)}, u32[]{:S(2)}, u32[]{:S(2)}) %collective-permute-start.19) | collective-permute-done | bytes 8224 | tf_op jit(solution)/shard_map/ppermute | solution.py:24
  143.0 3.5 %collective-permute-start.20 = (f32[16,128]{1,0:T(8,128)S(1)}, f32[16,128]{1,0:T(8,128)S(1)}, u32[]{:S(2)}, u32[]{:S(2)}) collective-permute-start(f32[16,128]{1,0:T(8,128)S(1)} %add_select_fusion), channel_id=1, source_target_pairs={{0,256},{8,264},{16,272},{24,280},{32,288},{40,296},{48,304},{56,3... | collective-permute-start | bytes 24584 | tf_op jit(solution)/shard_map/ppermute | solution.py:24
  146.5 0.0 copy-start.2
  146.5 0.6 copy-done.2
  147.2 0.3 near.1.inner
  147.5 2.6 %collective-permute-done.20 = f32[16,128]{1,0:T(8,128)S(1)} collective-permute-done((f32[16,128]{1,0:T(8,128)S(1)}, f32[16,128]{1,0:T(8,128)S(1)}, u32[]{:S(2)}, u32[]{:S(2)}) %collective-permute-start.20) | collective-permute-done | bytes 8224 | tf_op jit(solution)/shard_map/ppermute | solution.py:24
  150.1 0.8 finish.1
  (16 shorter events, 0.3 us)
Async XLA Ops:
  0.0 10.0 %copy-start = (bf16[128,1024]{1,0:T(8,128)(2,1)S(1)}, bf16[128,1024]{1,0:T(8,128)(2,1)}, u32[]{:S(2)}) copy-start(bf16[128,1024]{1,0:T(8,128)(2,1)} %tokens.1) | copy-start | bytes 786436
  0.9 16.4 %collective-permute-start.10 = (bf16[1,128,384]{2,1,0:T(8,128)(2,1)S(1)}, bf16[1,128,384]{2,1,0:T(8,128)(2,1)S(1)}, u32[]{:S(2)}, u32[]{:S(2)}) collective-permute-start(bf16[1,128,384]{2,1,0:T(8,128)(2,1)S(1)} %maximum_bitcast_fusion), channel_id=1, source_target_pairs={{0,64},{8,72},{16,80},{24,88},{32,96},{40,104},{48,112},{56,120},{... | collective-permute-start | bytes 294920 | tf_op jit(solution)/shard_map/ppermute | solution.py:24
  10.0 5.2 %collective-permute-start = (bf16[16,1024]{1,0:T(8,128)(2,1)S(1)}, bf16[16,1024]{1,0:T(8,128)(2,1)S(1)}, u32[]{:S(2)}, u32[]{:S(2)}) collective-permute-start(bf16[16,1024]{1,0:T(8,128)(2,1)S(1)} %slice.26), channel_id=1, source_target_pairs={{0,8},{8,16},{16,24},{24,32},{32,40},{40,48},{48,56},{56,64},{64,7... | collective-permute-start | bytes 98312 | tf_op jit(solution)/shard_map/ppermute | solution.py:29
  15.3 9.4 %collective-permute-start.1 = (bf16[2,144,256]{2,1,0:T(8,128)(2,1)S(1)}, bf16[2,144,256]{2,1,0:T(8,128)(2,1)S(1)}, u32[]{:S(2)}, u32[]{:S(2)}) collective-permute-start(bf16[2,144,256]{2,1,0:T(8,128)(2,1)S(1)} %get-tuple-element.13), channel_id=1, source_target_pairs={{0,8},{8,0},{16,24},{24,16},{32,40},{40,32},{48,56},{56,48},{64,72... | collective-permute-start | bytes 442376 | tf_op jit(solution)/shard_map/ppermute | solution.py:24
  17.3 13.9 %collective-permute-start.11 = (bf16[2,128,384]{2,1,0:T(8,128)(2,1)S(1)}, bf16[2,128,384]{2,1,0:T(8,128)(2,1)S(1)}, u32[]{:S(2)}, u32[]{:S(2)}) collective-permute-start(bf16[2,128,384]{2,1,0:T(8,128)(2,1)S(1)} %pad_maximum_fusion.2), channel_id=1, source_target_pairs={{0,32},{8,40},{16,48},{24,56},{32,0},{40,8},{48,16},{56,24},{64,96... | collective-permute-start | bytes 589832 | tf_op jit(solution)/shard_map/ppermute | solution.py:24
  24.8 7.2 %collective-permute-start.2 = (bf16[272,256]{1,0:T(8,128)(2,1)S(1)}, bf16[272,256]{1,0:T(8,128)(2,1)S(1)}, u32[]{:S(2)}, u32[]{:S(2)}) collective-permute-start(bf16[272,256]{1,0:T(8,128)(2,1)S(1)} %select_bitcast_fusion.1), channel_id=1, source_target_pairs={{0,16},{8,24},{16,0},{24,8},{32,48},{40,56},{48,32},{56,40},{64,80... | collective-permute-start | bytes 417800 | tf_op jit(solution)/shard_map/ppermute | solution.py:24
  32.1 28.4 %collective-permute-start.6 = (bf16[528,256]{1,0:T(8,128)(2,1)S(1)}, bf16[528,256]{1,0:T(8,128)(2,1)S(1)}, u32[]{:S(2)}, u32[]{:S(2)}) collective-permute-start(bf16[528,256]{1,0:T(8,128)(2,1)S(1)} %pad_maximum_fusion.1.t0), channel_id=1, source_target_pairs={{0,4},{1,5},{2,6},{3,7},{4,0},{5,1},{6,2},{7,3},{8,12},{9,13},{10,... | collective-permute-start | bytes 811016 | tf_op jit(solution)/shard_map/ppermute | solution.py:24
  44.2 33.3 %collective-permute-start.3 = (bf16[528,256]{1,0:T(8,128)(2,1)S(1)}, bf16[528,256]{1,0:T(8,128)(2,1)S(1)}, u32[]{:S(2)}, u32[]{:S(2)}) collective-permute-start(bf16[528,256]{1,0:T(8,128)(2,1)S(1)} %pad_maximum_fusion.1.t0), channel_id=1, source_target_pairs={{0,1},{1,0},{2,3},{3,2},{4,5},{5,4},{6,7},{7,6},{8,9},{9,8},{10,11... | collective-permute-start | bytes 811016 | tf_op jit(solution)/shard_map/ppermute | solution.py:24
  47.7 41.2 %collective-permute-start.12 = (bf16[2,256,384]{2,1,0:T(8,128)(2,1)S(1)}, bf16[2,256,384]{2,1,0:T(8,128)(2,1)S(1)}, u32[]{:S(2)}, u32[]{:S(2)}) collective-permute-start(bf16[2,256,384]{2,1,0:T(8,128)(2,1)S(1)} %pad_maximum_fusion.w0), channel_id=1, source_target_pairs={{0,128},{8,136},{16,144},{24,152},{32,160},{40,168},{48,176},{56,1... | collective-permute-start | bytes 1179656 | tf_op jit(solution)/shard_map/ppermute | solution.py:24
  53.5 27.1 %collective-permute-start.4 = (bf16[528,256]{1,0:T(8,128)(2,1)S(1)}, bf16[528,256]{1,0:T(8,128)(2,1)S(1)}, u32[]{:S(2)}, u32[]{:S(2)}) collective-permute-start(bf16[528,256]{1,0:T(8,128)(2,1)S(1)} %pad_maximum_fusion.1.t0), channel_id=1, source_target_pairs={{0,2},{1,3},{2,0},{3,1},{4,6},{5,7},{6,4},{7,5},{8,10},{9,11},{10,... | collective-permute-start | bytes 811016 | tf_op jit(solution)/shard_map/ppermute | solution.py:24
  58.3 25.8 %collective-permute-start.5 = (bf16[528,256]{1,0:T(8,128)(2,1)S(1)}, bf16[528,256]{1,0:T(8,128)(2,1)S(1)}, u32[]{:S(2)}, u32[]{:S(2)}) collective-permute-start(bf16[528,256]{1,0:T(8,128)(2,1)S(1)} %pad_maximum_fusion.1.t0), channel_id=1, source_target_pairs={{0,3},{1,2},{2,1},{3,0},{4,7},{5,6},{6,5},{7,4},{8,11},{9,10},{10,... | collective-permute-start | bytes 811016 | tf_op jit(solution)/shard_map/ppermute | solution.py:24
  60.5 30.7 %collective-permute-start.13 = (bf16[2,256,384]{2,1,0:T(8,128)(2,1)S(1)}, bf16[2,256,384]{2,1,0:T(8,128)(2,1)S(1)}, u32[]{:S(2)}, u32[]{:S(2)}) collective-permute-start(bf16[2,256,384]{2,1,0:T(8,128)(2,1)S(1)} %pad_maximum_fusion.w0), channel_id=1, source_target_pairs={{0,256},{8,264},{16,272},{24,280},{32,288},{40,296},{48,304},{56,3... | collective-permute-start | bytes 1179656 | tf_op jit(solution)/shard_map/ppermute | solution.py:24
  77.5 16.9 %collective-permute-start.14 = (bf16[2,256,384]{2,1,0:T(8,128)(2,1)S(1)}, bf16[2,256,384]{2,1,0:T(8,128)(2,1)S(1)}, u32[]{:S(2)}, u32[]{:S(2)}) collective-permute-start(bf16[2,256,384]{2,1,0:T(8,128)(2,1)S(1)} %pad_maximum_fusion.w0), channel_id=1, source_target_pairs={{0,384},{8,392},{16,400},{24,408},{32,416},{40,424},{48,432},{56,4... | collective-permute-start | bytes 1179656 | tf_op jit(solution)/shard_map/ppermute | solution.py:24
  80.6 13.8 %collective-permute-start.7 = (bf16[528,256]{1,0:T(8,128)(2,1)S(1)}, bf16[528,256]{1,0:T(8,128)(2,1)S(1)}, u32[]{:S(2)}, u32[]{:S(2)}) collective-permute-start(bf16[528,256]{1,0:T(8,128)(2,1)S(1)} %collective-permute-done.6.t4), channel_id=1, source_target_pairs={{0,1},{1,0},{2,3},{3,2},{4,5},{5,4},{6,7},{7,6},{8,9},{9,8},{10,11... | collective-permute-start | bytes 811016 | tf_op jit(solution)/shard_map/ppermute | solution.py:24
  84.1 13.8 %collective-permute-start.8 = (bf16[528,256]{1,0:T(8,128)(2,1)S(1)}, bf16[528,256]{1,0:T(8,128)(2,1)S(1)}, u32[]{:S(2)}, u32[]{:S(2)}) collective-permute-start(bf16[528,256]{1,0:T(8,128)(2,1)S(1)} %collective-permute-done.6.t4), channel_id=1, source_target_pairs={{0,2},{1,3},{2,0},{3,1},{4,6},{5,7},{6,4},{7,5},{8,10},{9,11},{10,... | collective-permute-start | bytes 811016 | tf_op jit(solution)/shard_map/ppermute | solution.py:24
  88.9 13.9 %collective-permute-start.9 = (bf16[528,256]{1,0:T(8,128)(2,1)S(1)}, bf16[528,256]{1,0:T(8,128)(2,1)}, u32[]{:S(2)}, u32[]{:S(2)}) collective-permute-start(bf16[528,256]{1,0:T(8,128)(2,1)S(1)} %collective-permute-done.6.t4), channel_id=1, source_target_pairs={{0,3},{1,2},{2,1},{3,0},{4,7},{5,6},{6,5},{7,4},{8,11},{9,10},{10,... | collective-permute-start | bytes 811016 | tf_op jit(solution)/shard_map/ppermute | solution.py:24
  91.2 15.9 %copy-start.3 = (f32[128,16]{0,1:T(8,128)S(1)}, f32[128,16]{0,1:T(8,128)}, u32[]{:S(2)}) copy-start(f32[128,16]{0,1:T(8,128)} %param.10) | copy-start | bytes 24580
  105.1 2.0 %copy-start.4 = (f32[128,16]{0,1:T(8,128)S(1)}, f32[128,16]{0,1:T(8,128)}, u32[]{:S(2)}) copy-start(f32[128,16]{0,1:T(8,128)} %param.9) | copy-start | bytes 24580
  105.2 4.2 %collective-permute-start.15 = (f32[528,384]{1,0:T(8,128)S(1)}, f32[528,384]{1,0:T(8,128)S(1)}, u32[]{:S(2)}, u32[]{:S(2)}) collective-permute-start(f32[528,384]{1,0:T(8,128)S(1)} %project.1.mine), channel_id=1, source_target_pairs={{0,8},{8,0},{16,24},{24,16},{32,40},{40,32},{48,56},{56,48},{64,72... | collective-permute-start | bytes 2433032 | tf_op jit(solution)/shard_map/ppermute | solution.py:24
  109.5 11.3 %collective-permute-start.16 = (bf16[608,256]{1,0:T(8,128)(2,1)S(1)}, bf16[608,256]{1,0:T(8,128)(2,1)S(1)}, u32[]{:S(2)}, u32[]{:S(2)}) collective-permute-start(bf16[608,256]{1,0:T(8,128)(2,1)S(1)} %get-tuple-element.16), channel_id=1, source_target_pairs={{0,16},{8,24},{16,0},{24,8},{32,48},{40,56},{48,32},{56,40},{64,80... | collective-permute-start | bytes 933896 | tf_op jit(solution)/shard_map/ppermute | solution.py:24
  111.4 9.4 %copy-start.1 = (f32[3,128,3]{1,2,0:T(4,128)S(1)}, f32[3,128,3]{1,2,0:T(4,128)}, u32[]{:S(2)}) copy-start(f32[3,128,3]{1,2,0:T(4,128)} %param.8) | copy-start | bytes 13828
  121.6 6.4 %collective-permute-start.17 = (f32[16,128]{1,0:T(8,128)S(1)}, f32[16,128]{1,0:T(8,128)S(1)}, u32[]{:S(2)}, u32[]{:S(2)}) collective-permute-start(f32[16,128]{1,0:T(8,128)S(1)} %get-tuple-element.20), channel_id=1, source_target_pairs={{0,32},{8,40},{16,48},{24,56},{32,0},{40,8},{48,16},{56,24},{64,96... | collective-permute-start | bytes 24584 | tf_op jit(solution)/shard_map/ppermute | solution.py:24
  128.0 9.5 %collective-permute-start.18 = (f32[16,128]{1,0:T(8,128)S(1)}, f32[16,128]{1,0:T(8,128)S(1)}, u32[]{:S(2)}, u32[]{:S(2)}) collective-permute-start(f32[16,128]{1,0:T(8,128)S(1)} %add_select_fusion.2), channel_id=1, source_target_pairs={{0,64},{8,72},{16,80},{24,88},{32,96},{40,104},{48,112},{56,120},{... | collective-permute-start | bytes 24584 | tf_op jit(solution)/shard_map/ppermute | solution.py:24
  137.5 5.5 %collective-permute-start.19 = (f32[16,128]{1,0:T(8,128)S(1)}, f32[16,128]{1,0:T(8,128)S(1)}, u32[]{:S(2)}, u32[]{:S(2)}) collective-permute-start(f32[16,128]{1,0:T(8,128)S(1)} %add_select_fusion.1), channel_id=1, source_target_pairs={{0,128},{8,136},{16,144},{24,152},{32,160},{40,168},{48,176},{56,1... | collective-permute-start | bytes 24584 | tf_op jit(solution)/shard_map/ppermute | solution.py:24
  143.0 7.0 %collective-permute-start.20 = (f32[16,128]{1,0:T(8,128)S(1)}, f32[16,128]{1,0:T(8,128)S(1)}, u32[]{:S(2)}, u32[]{:S(2)}) collective-permute-start(f32[16,128]{1,0:T(8,128)S(1)} %add_select_fusion), channel_id=1, source_target_pairs={{0,256},{8,264},{16,272},{24,280},{32,288},{40,296},{48,304},{56,3... | collective-permute-start | bytes 24584 | tf_op jit(solution)/shard_map/ppermute | solution.py:24
  146.5 0.7 copy-start.2

commit v3 on v2

v3 whole, which is shorter than its diff:
```python
import jax
import jax.numpy as jnp
from jax import lax
from jax.experimental import pallas as pl
from jax.experimental.pallas import tpu as pltpu
from jax.sharding import PartitionSpec as P

F32 = jnp.float32
BF16 = jnp.bfloat16
HALO = 16
BLOCK = 128
GROUP = 4 * BLOCK
ROWS = HALO + GROUP
PIECE = HALO + BLOCK
OWN = 2 * PIECE
MODES = 16
VMEM = pl.BlockSpec(memory_space=pltpu.VMEM)
SMEM = pl.BlockSpec(memory_space=pltpu.SMEM)
PARAMS = pltpu.CompilerParams(vmem_limit_bytes=48 * 1024 * 1024)


def flip(x, axis, mask):
    length = lax.axis_size(axis)
    return lax.ppermute(x, axis, [(i, i ^ mask) for i in range(length)])


def ahead(x, axis, by):
    length = lax.axis_size(axis)
    return lax.ppermute(x, axis, [(i, i + by) for i in range(length - by)])


def ordered(upper, own, other, axis):
    first = jnp.where(upper, other, own)
    second = jnp.where(upper, own, other)
    return jnp.concatenate([first, second], axis=axis)


def flip_many(x, axis, masks):
    return [flip(x, axis, m) for m in masks]


def split_kernel(place, tokens, kept, given):
    core = place[0] & 1
    for out, side in ((kept, core), (given, 1 - core)):
        for bit8 in range(2):
            for bit9 in range(2):
                start = pl.multiple_of(512 * bit9 + 256 * bit8 + side * 128, 128)
                out[bit8, :, 128 * bit9 : 128 * bit9 + 128] = tokens[:, pl.ds(start, 128)]


def split(place, tokens):
    shape = jax.ShapeDtypeStruct((2, BLOCK, 256), BF16)
    return pl.pallas_call(
        split_kernel,
        out_shape=(shape, shape),
        in_specs=[SMEM, VMEM],
        out_specs=(VMEM, VMEM),
        compiler_params=PARAMS,
        name="split",
    )(place, tokens)


def gather(tokens, in_weight, place):
    kept, given = split(place[None], tokens)
    both = ordered((place & 1) == 1, kept, flip(given, "ctx", 1), 1)
    upper = (place & 2) == 2
    keep = jnp.where(upper, both[1], both[0])
    give = jnp.where(upper, both[0], both[1])
    keep, give, in_weight = lax.optimization_barrier((keep, give, in_weight))
    held = jnp.concatenate([in_weight[1], in_weight[2], in_weight[0]], axis=1)[None]
    near_h = ordered(upper, keep, flip(give, "ctx", 2), 0)
    past = flip(held, "ctx", 8)
    far_h = flip(near_h, "tp", 4)
    near_h, past = lax.optimization_barrier((near_h, past))
    halo = ahead(near_h[GROUP - HALO :], "ctx", 4)
    held = jnp.concatenate([held, past], axis=0)
    held = ordered((place & 4) == 4, held, flip(held, "ctx", 4), 1)
    far_halo = flip(halo, "tp", 4)
    found = []
    for part in (jnp.concatenate([halo, near_h]), jnp.concatenate([far_halo, far_h])):
        found += [part] + flip_many(part, "tp", (1, 2, 3))
    return found, [held] + flip_many(held, "ctx", (16, 32, 48))


def project_kernel(match, *refs):
    tokens, weights, kept, given, total = refs[:8], refs[8:12], refs[12], refs[13], refs[14]
    for case in range(4):

        @pl.when(match[0] == case)
        def _():
            added = jnp.zeros(total.shape, F32)
            for turn in range(8):
                turn_h, turn_y = turn >> 2, turn & 3
                turn_x = case ^ (turn_h << 1 | turn_y >> 1)
                weight = weights[turn_x][match[1] ^ (turn_y & 1)]
                added += jnp.dot(tokens[turn][...], weight, preferred_element_type=F32)
            total[...] = added

    for core in range(2):

        @pl.when(match[2] == core)
        def _():
            for out, side in ((kept, core), (given, 1 - core)):
                out[:ROWS] = total[:, BLOCK * side : BLOCK * side + BLOCK]
                for chip in range(2):
                    start = BLOCK * (2 * chip + side)
                    out[ROWS + PIECE * chip : ROWS + PIECE * chip + PIECE] = total[
                        start : start + PIECE, 2 * BLOCK :
                    ]


def project(match, tokens, weights):
    columns = weights[0].shape[2]
    shape = jax.ShapeDtypeStruct((ROWS + OWN, BLOCK), F32)
    return pl.pallas_call(
        project_kernel,
        out_shape=(shape, shape),
        in_specs=[SMEM] + [VMEM] * 12,
        out_specs=(VMEM, VMEM),
        scratch_shapes=[pltpu.VMEM((ROWS, columns), F32)],
        compiler_params=PARAMS,
        cost_estimate=pl.CostEstimate(
            flops=2 * ROWS * 2048 * columns, bytes_accessed=2048 * 2 * (ROWS + columns), transcendentals=0
        ),
        name="project",
    )(match, *tokens, *weights)


def merge_kernel(place, mine, theirs, pair, query, gift):
    pair[...] = mine[:ROWS] + theirs[:ROWS]
    gift[:ROWS] = pair[...]
    chip = (place[0] >> 1) & 1
    for out, first, side in ((query, 0, chip), (gift, ROWS, 1 - chip)):
        start = pl.multiple_of(ROWS + PIECE * side, 16)
        out[first : first + PIECE] = mine[pl.ds(start, PIECE)] + theirs[pl.ds(start, PIECE)]


def merge(place, mine, theirs):
    return pl.pallas_call(
        merge_kernel,
        out_shape=(
            jax.ShapeDtypeStruct((ROWS, BLOCK), F32),
            jax.ShapeDtypeStruct((PIECE, BLOCK), F32),
            jax.ShapeDtypeStruct((ROWS + PIECE, BLOCK), F32),
        ),
        in_specs=[SMEM, VMEM, VMEM],
        out_specs=(VMEM, VMEM, VMEM),
        compiler_params=PARAMS,
        name="merge",
    )(place, mine, theirs)


def short(proj, taps):
    n = proj.shape[0] - HALO
    return (
        taps[0:1] * proj[HALO : HALO + n]
        + taps[1:2] * proj[HALO - 1 : HALO - 1 + n]
        + taps[2:3] * proj[HALO - 2 : HALO - 2 + n]
    )


def drive_kernel(place, mine, theirs, own, other, taps, weigh, step, query, driven, before, state, signal):
    spot = place[0] & 3
    core = place[0] & 1
    first = jnp.where(core == 0, taps[1], taps[2])
    second = jnp.where(core == 0, taps[2], taps[1])
    signal[...] = short(mine[...].astype(F32), first) * short(theirs[...].astype(F32), second)
    start = pl.multiple_of(spot * BLOCK, BLOCK)
    driven[...] = signal[pl.ds(start, BLOCK)]
    query[...] = short((own[...] + other[...]).astype(BF16).astype(F32), taps[0])
    for r in range(MODES):
        w, decay = weigh[r], step[r : r + 1]
        past = jnp.zeros((1, BLOCK), F32)
        held = past
        for b in range(4):
            held = jnp.where(spot == b, past, held)
            past = decay * past + jnp.sum(w * signal[BLOCK * b : BLOCK * b + BLOCK], axis=0, keepdims=True)
        before[r : r + 1] = held
        state[r : r + 1] = past


def drive(place, mine, theirs, own, other, taps, weigh, step):
    square = jax.ShapeDtypeStruct((BLOCK, BLOCK), F32)
    modes = jax.ShapeDtypeStruct((MODES, BLOCK), F32)
    return pl.pallas_call(
        drive_kernel,
        out_shape=(square, square, modes, modes),
        in_specs=[SMEM] + [VMEM] * 7,
        out_specs=(VMEM,) * 4,
        scratch_shapes=[pltpu.VMEM((GROUP, BLOCK), F32)],
        compiler_params=PARAMS,
        name="drive",
    )(place, mine, theirs, own, other, taps, weigh, step)


def tables_kernel(place, residues, rates, weigh, reach, taps, step, toward, whole, last):
    at = place[0]
    index = lax.broadcasted_iota(jnp.int32, (BLOCK, BLOCK), 0).astype(F32)
    line = at & 15
    total = jnp.zeros((BLOCK, BLOCK), F32)
    for r in range(MODES):
        rate = rates[r : r + 1]
        amount = residues[r : r + 1] * jnp.sqrt(2.0 * rate)
        weigh[r] = jnp.exp(-rate * (BLOCK - 1.0 - index))
        reach[r] = amount * jnp.exp(-rate * (index + 1.0))
        total = total + amount * jnp.exp(-rate * index)
    taps[...] = total
    rate = rates[...]
    step[...] = jnp.exp(-rate * float(BLOCK))
    for turn in range(4):
        group = (line >> 2) ^ turn
        whole[turn] = jnp.exp(-rate * (GROUP * (3 - group)).astype(F32))
        if turn:
            for out, after in ((toward, line - 4 * (group + 1)), (last, at - 16 * (((at >> 4) ^ turn) + 1))):
                decay = jnp.exp(-rate * (BLOCK * jnp.maximum(after, 0)).astype(F32))
                out[turn - 1] = jnp.where(after >= 0, decay, 0.0)


def tables(place, residues, rates):
    def full(*shape):
        return jax.ShapeDtypeStruct(shape, F32)

    return pl.pallas_call(
        tables_kernel,
        out_shape=(
            full(MODES, BLOCK, BLOCK),
            full(MODES, BLOCK, BLOCK),
            full(BLOCK, BLOCK),
            full(MODES, BLOCK),
            full(3, MODES, BLOCK),
            full(4, MODES, BLOCK),
            full(3, MODES, BLOCK),
        ),
        in_specs=[SMEM, VMEM, VMEM],
        out_specs=(VMEM,) * 7,
        compiler_params=PARAMS,
        name="tables",
    )(place, residues, rates)


def advance_kernel(state, p1, p2, p3, before, toward, whole, out_before, out_state):
    out_before[...] = before[...] + toward[0] * p1[...] + toward[1] * p2[...] + toward[2] * p3[...]
    out_state[...] = whole[0] * state[...] + whole[1] * p1[...] + whole[2] * p2[...] + whole[3] * p3[...]


def advance(state, others, before, toward, whole):
    modes = jax.ShapeDtypeStruct((MODES, BLOCK), F32)
    return pl.pallas_call(
        advance_kernel,
        out_shape=(modes, modes),
        in_specs=[VMEM] * 7,
        out_specs=(VMEM, VMEM),
        compiler_params=PARAMS,
        name="advance",
    )(state, *others, before, toward, whole)


def near_kernel(driven, taps, gain, out, padded):
    signal = driven[...]
    padded[:BLOCK] = jnp.zeros((BLOCK, BLOCK), F32)
    padded[BLOCK:] = signal
    total = gain[...] * signal
    for s in range(BLOCK):
        low = s // 8 * 8
        part = taps[s : s + 1] * padded[BLOCK + low - s : 2 * BLOCK - s]
        if low:
            part = jnp.concatenate([jnp.zeros((low, BLOCK), F32), part], axis=0)
        total = total + part
    out[...] = total


def near(driven, taps, gain):
    return pl.pallas_call(
        near_kernel,
        out_shape=jax.ShapeDtypeStruct((BLOCK, BLOCK), F32),
        in_specs=[VMEM] * 3,
        out_specs=VMEM,
        scratch_shapes=[pltpu.VMEM((2 * BLOCK, BLOCK), F32)],
        compiler_params=PARAMS,
        cost_estimate=pl.CostEstimate(flops=2 * BLOCK**3, bytes_accessed=3 * BLOCK * BLOCK * 4, transcendentals=0),
        name="near",
    )(driven, taps, gain)


def finish_kernel(query, inner, reach, before, p1, p2, p3, last, out):
    carry = before[...] + last[0] * p1[...] + last[1] * p2[...] + last[2] * p3[...]
    conv = inner[...]
    for r in range(MODES):
        conv = conv + reach[r] * carry[r : r + 1]
    out[...] = (query[...] * conv).T


def finish(query, inner, reach, before, others, last):
    return pl.pallas_call(
        finish_kernel,
        out_shape=jax.ShapeDtypeStruct((BLOCK, BLOCK), F32),
        in_specs=[VMEM] * 8,
        out_specs=VMEM,
        compiler_params=PARAMS,
        name="finish",
    )(query, inner, reach, before, *others, last)


def body(tokens, in_weight, short_taps, residues, rates, skip_gain):
    place = lax.axis_index("ctx")
    tp = lax.axis_index("tp")
    spot = place[None]
    apart = tp ^ (place >> 3)
    match = jnp.stack([apart >> 1, apart & 1, place & 1])

    features, weights = gather(tokens, in_weight, place)
    weigh, reach, taps, step, toward, whole, last = tables(spot, residues.T, rates.T)

    mine, gift = project(match, features, weights)
    pair, own, gift = merge(spot, mine, flip(gift, "ctx", 1))
    theirs = flip(gift, "ctx", 2)
    mine = (pair + theirs[:ROWS]).astype(BF16)
    query, driven, before, state = drive(
        spot, mine, flip(mine, "ctx", 1), own, theirs[ROWS:], short_taps.transpose(0, 2, 1), weigh, step
    )
    others = flip_many(state, "ctx", (4, 8, 12))
    inner = near(driven, taps, skip_gain[None])
    before, state = advance(state, others, before, toward, whole)
    others = flip_many(state, "ctx", (16, 32, 48))
    return finish(query, inner, reach, before, others, last)


def solution(mesh):
    in_specs = (
        P("ctx", "tp"),
        P(None, "ctx", "tp"),
        P(None, "tp", None),
        P("tp", None),
        P("tp", None),
        P("tp"),
    )
    return jax.shard_map(
        body, mesh=mesh, in_specs=in_specs, out_specs=P("tp", "ctx"), check_vma=False
    )
```

time: 152 us -> 160 us (1.053)
  the two profiles are of different devices: /device:TPU:32 before, /device:TPU:1 now
where the time goes in v3:
time: 160 us; the launch traced here: 158 us
  starting transfers between devices  121 us (76%)
  waiting for transfers between devices  29.6 us (18%)
  Pallas kernels  4.85 us (3%)
  local copies, waits for them, and re-layouts  1.99 us (1%)
    ppermute x24, starting transfers between devices, flip(): return lax.ppermute(x, axis, [(i, i ^ mask) for i in range(length)])  119 us
    ppermute x24, waiting for transfers between devices, flip(): return lax.ppermute(x, axis, [(i, i ^ mask) for i in range(length)])  23.4 us
    ppermute x1, waiting for transfers between devices, ahead(): return lax.ppermute(x, axis, [(i, i + by) for i in range(length - by)])  6.15 us
  transfers between devices with their start and end apart: 25, of which 11 were waited for; matrix products, arithmetic and copies ran while one was open for 0% of the time, Pallas kernels for 1%

profile of v3, /device:TPU:1, one launch (start us, length us, event | category | flops | bytes accessed | tf_op | source)
XLA Modules:
  0.0 157.9 jit_solution(2250217576602588303)
XLA Ops:
  0.0 0.9 copy-done
  1.0 0.1 split.1
  1.0 8.8 %collective-permute-start = (bf16[2,128,256]{2,1,0:T(8,128)(2,1)S(1)}, bf16[2,128,256]{2,1,0:T(8,128)(2,1)S(1)}, u32[]{:S(2)}, u32[]{:S(2)}) collective-permute-start(bf16[2,128,256]{2,1,0:T(8,128)(2,1)S(1)} %get-tuple-element.30), channel_id=1, source_target_pairs={{0,8},{8,0},{16,24},{24,16},{32,40},{40,32},{48,56},{56,48},{64,72... | collective-permute-start | bytes 393224 | tf_op jit(solution)/shard_map/ppermute | solution.py:24
  9.8 1.0 collective-permute-done
  10.8 0.0 copy-start.5
  10.9 1.9 %collective-permute-start.1 = (bf16[256,256]{1,0:T(8,128)(2,1)S(1)}, bf16[256,256]{1,0:T(8,128)(2,1)S(1)}, u32[]{:S(2)}, u32[]{:S(2)}) collective-permute-start(bf16[256,256]{1,0:T(8,128)(2,1)S(1)} %get-tuple-element.32), channel_id=1, source_target_pairs={{0,16},{8,24},{16,0},{24,8},{32,48},{40,56},{48,32},{56,40},{64,80... | collective-permute-start | bytes 393224 | tf_op jit(solution)/shard_map/ppermute | solution.py:24
  12.9 5.1 %collective-permute-start.2 = (bf16[1,128,384]{2,1,0:T(8,128)(2,1)S(1)}, bf16[1,128,384]{2,1,0:T(8,128)(2,1)S(1)}, u32[]{:S(2)}, u32[]{:S(2)}) collective-permute-start(bf16[1,128,384]{2,1,0:T(8,128)(2,1)S(1)} %maximum_bitcast_fusion), channel_id=1, source_target_pairs={{0,64},{8,72},{16,80},{24,88},{32,96},{40,104},{48,112},{56,120},{... | collective-permute-start | bytes 294920 | tf_op jit(solution)/shard_map/ppermute | solution.py:24
  17.9 0.0 collective-permute-done.1
  18.0 9.7 %collective-permute-start.8 = (bf16[512,256]{1,0:T(8,128)(2,1)S(1)}, bf16[512,256]{1,0:T(8,128)(2,1)S(1)}, u32[]{:S(2)}, u32[]{:S(2)}) collective-permute-start(bf16[512,256]{1,0:T(8,128)(2,1)S(1)} %pad_maximum_fusion.1), channel_id=1, source_target_pairs={{0,4},{1,5},{2,6},{3,7},{4,0},{5,1},{6,2},{7,3},{8,12},{9,13},{10,... | collective-permute-start | bytes 786440 | tf_op jit(solution)/shard_map/ppermute | solution.py:24
  27.7 1.5 collective-permute-done.2
  29.2 1.6 %collective-permute-start.3 = (bf16[16,256]{1,0:T(8,128)(2,1)S(1)}, bf16[16,256]{1,0:T(8,128)(2,1)S(1)}, u32[]{:S(2)}, u32[]{:S(2)}) collective-permute-start(bf16[16,256]{1,0:T(8,128)(2,1)S(1)} %slice.31), channel_id=1, source_target_pairs={{0,32},{8,40},{16,48},{24,56},{32,64},{40,72},{48,80},{56,88},{64,... | collective-permute-start | bytes 24584 | tf_op jit(solution)/shard_map/ppermute | solution.py:29
  30.9 4.3 %collective-permute-start.12 = (bf16[2,128,384]{2,1,0:T(8,128)(2,1)S(1)}, bf16[2,128,384]{2,1,0:T(8,128)(2,1)S(1)}, u32[]{:S(2)}, u32[]{:S(2)}) collective-permute-start(bf16[2,128,384]{2,1,0:T(8,128)(2,1)S(1)} %pad_maximum_fusion.2), channel_id=1, source_target_pairs={{0,32},{8,40},{16,48},{24,56},{32,0},{40,8},{48,16},{56,24},{64,96... | collective-permute-start | bytes 589832 | tf_op jit(solution)/shard_map/ppermute | solution.py:24
  35.2 6.2 %collective-permute-done.3 = bf16[16,256]{1,0:T(8,128)(2,1)S(1)} collective-permute-done((bf16[16,256]{1,0:T(8,128)(2,1)S(1)}, bf16[16,256]{1,0:T(8,128)(2,1)S(1)}, u32[]{:S(2)}, u32[]{:S(2)}) %collective-permute-start.3) | collective-permute-done | bytes 8224 | tf_op jit(solution)/shard_map/ppermute | solution.py:29
  41.3 20.0 %collective-permute-start.7 = (bf16[16,256]{1,0:T(8,128)(2,1)S(1)}, bf16[16,256]{1,0:T(8,128)(2,1)S(1)}, u32[]{:S(2)}, u32[]{:S(2)}) collective-permute-start(bf16[16,256]{1,0:T(8,128)(2,1)S(1)} %collective-permute-done.3), channel_id=1, source_target_pairs={{0,4},{1,5},{2,6},{3,7},{4,0},{5,1},{6,2},{7,3},{8,12},{9,13},{10,... | collective-permute-start | bytes 24584 | tf_op jit(solution)/shard_map/ppermute | solution.py:24
  61.4 4.7 %collective-permute-start.6 = (bf16[528,256]{1,0:T(8,128)(2,1)S(1)}, bf16[528,256]{1,0:T(8,128)(2,1)S(1)}, u32[]{:S(2)}, u32[]{:S(2)}) collective-permute-start(bf16[528,256]{1,0:T(8,128)(2,1)S(1)} %constant_dynamic-update-slice_fusion.refs_0_), channel_id=1, source_target_pairs={{0,3},{1,2},{2,1},{3,0},{4,7},{5,6},{6,5},{7,4},{8,11},{9,10},{10,... | collective-permute-start | bytes 811016 | tf_op jit(solution)/shard_map/ppermute | solution.py:24
  66.2 2.3 %collective-permute-start.5 = (bf16[528,256]{1,0:T(8,128)(2,1)S(1)}, bf16[528,256]{1,0:T(8,128)(2,1)S(1)}, u32[]{:S(2)}, u32[]{:S(2)}) collective-permute-start(bf16[528,256]{1,0:T(8,128)(2,1)S(1)} %constant_dynamic-update-slice_fusion.refs_0_), channel_id=1, source_target_pairs={{0,2},{1,3},{2,0},{3,1},{4,6},{5,7},{6,4},{7,5},{8,10},{9,11},{10,... | collective-permute-start | bytes 811016 | tf_op jit(solution)/shard_map/ppermute | solution.py:24
  68.4 0.0 collective-permute-done.7
  68.4 2.1 %collective-permute-start.4 = (bf16[528,256]{1,0:T(8,128)(2,1)S(1)}, bf16[528,256]{1,0:T(8,128)(2,1)S(1)}, u32[]{:S(2)}, u32[]{:S(2)}) collective-permute-start(bf16[528,256]{1,0:T(8,128)(2,1)S(1)} %constant_dynamic-update-slice_fusion.refs_0_), channel_id=1, source_target_pairs={{0,1},{1,0},{2,3},{3,2},{4,5},{5,4},{6,7},{7,6},{8,9},{9,8},{10,11... | collective-permute-start | bytes 811016 | tf_op jit(solution)/shard_map/ppermute | solution.py:24
  70.6 0.0 collective-permute-done.8
  70.7 4.6 %collective-permute-start.11 = (bf16[528,256]{1,0:T(8,128)(2,1)S(1)}, bf16[528,256]{1,0:T(8,128)(2,1)S(1)}, u32[]{:S(2)}, u32[]{:S(2)}) collective-permute-start(bf16[528,256]{1,0:T(8,128)(2,1)S(1)} %constant_dynamic-update-slice_fusion.2.refs_4_), channel_id=1, source_target_pairs={{0,3},{1,2},{2,1},{3,0},{4,7},{5,6},{6,5},{7,4},{8,11},{9,10},{10,... | collective-permute-start | bytes 811016 | tf_op jit(solution)/shard_map/ppermute | solution.py:24
  75.2 0.0 collective-permute-done.12
  75.2 0.1 broadcast_select_fusion.1
  75.4 12.2 %collective-permute-start.15 = (bf16[2,256,384]{2,1,0:T(8,128)(2,1)S(1)}, bf16[2,256,384]{2,1,0:T(8,128)(2,1)S(1)}, u32[]{:S(2)}, u32[]{:S(2)}) collective-permute-start(bf16[2,256,384]{2,1,0:T(8,128)(2,1)S(1)} %pad_maximum_fusion.refs_8_), channel_id=1, source_target_pairs={{0,384},{8,392},{16,400},{24,408},{32,416},{40,424},{48,432},{56,4... | collective-permute-start | bytes 1179656 | tf_op jit(solution)/shard_map/ppermute | solution.py:24
  87.6 0.0 collective-permute-done.6.refs_3_
  87.6 2.5 %collective-permute-start.14 = (bf16[2,256,384]{2,1,0:T(8,128)(2,1)S(1)}, bf16[2,256,384]{2,1,0:T(8,128)(2,1)S(1)}, u32[]{:S(2)}, u32[]{:S(2)}) collective-permute-start(bf16[2,256,384]{2,1,0:T(8,128)(2,1)S(1)} %pad_maximum_fusion.refs_8_), channel_id=1, source_target_pairs={{0,256},{8,264},{16,272},{24,280},{32,288},{40,296},{48,304},{56,3... | collective-permute-start | bytes 1179656 | tf_op jit(solution)/shard_map/ppermute | solution.py:24
  90.1 0.0 collective-permute-done.5.refs_2_
  90.1 1.9 %collective-permute-start.13 = (bf16[2,256,384]{2,1,0:T(8,128)(2,1)S(1)}, bf16[2,256,384]{2,1,0:T(8,128)(2,1)S(1)}, u32[]{:S(2)}, u32[]{:S(2)}) collective-permute-start(bf16[2,256,384]{2,1,0:T(8,128)(2,1)S(1)} %pad_maximum_fusion.refs_8_), channel_id=1, source_target_pairs={{0,128},{8,136},{16,144},{24,152},{32,160},{40,168},{48,176},{56,1... | collective-permute-start | bytes 1179656 | tf_op jit(solution)/shard_map/ppermute | solution.py:24
  92.0 0.0 collective-permute-done.4.refs_1_
  92.0 2.3 %collective-permute-start.10 = (bf16[528,256]{1,0:T(8,128)(2,1)S(1)}, bf16[528,256]{1,0:T(8,128)(2,1)S(1)}, u32[]{:S(2)}, u32[]{:S(2)}) collective-permute-start(bf16[528,256]{1,0:T(8,128)(2,1)S(1)} %constant_dynamic-update-slice_fusion.2.refs_4_), channel_id=1, source_target_pairs={{0,2},{1,3},{2,0},{3,1},{4,6},{5,7},{6,4},{7,5},{8,10},{9,11},{10,... | collective-permute-start | bytes 811016 | tf_op jit(solution)/shard_map/ppermute | solution.py:24
  94.3 0.0 collective-permute-done.11.refs_7_
  94.3 2.4 %collective-permute-start.9 = (bf16[528,256]{1,0:T(8,128)(2,1)S(1)}, bf16[528,256]{1,0:T(8,128)(2,1)}, u32[]{:S(2)}, u32[]{:S(2)}) collective-permute-start(bf16[528,256]{1,0:T(8,128)(2,1)S(1)} %constant_dynamic-update-slice_fusion.2.refs_4_), channel_id=1, source_target_pairs={{0,1},{1,0},{2,3},{3,2},{4,5},{5,4},{6,7},{7,6},{8,9},{9,8},{10,11... | collective-permute-start | bytes 811016 | tf_op jit(solution)/shard_map/ppermute | solution.py:24
  96.7 0.1 pad_add_fusion.match
  96.8 4.2 %collective-permute-done.10.refs_6_ = bf16[528,256]{1,0:T(8,128)(2,1)S(1)} collective-permute-done((bf16[528,256]{1,0:T(8,128)(2,1)S(1)}, bf16[528,256]{1,0:T(8,128)(2,1)S(1)}, u32[]{:S(2)}, u32[]{:S(2)}) %collective-permute-start.10) | collective-permute-done | bytes 270368 | tf_op jit(solution)/shard_map/ppermute | solution.py:24
  101.0 0.8 collective-permute-done.9.refs_5_
  101.8 0.0 collective-permute-done.15.refs_11_
  101.8 0.0 collective-permute-done.14.refs_10_
  101.8 2.4 %collective-permute-done.13.refs_9_ = bf16[2,256,384]{2,1,0:T(8,128)(2,1)S(1)} collective-permute-done((bf16[2,256,384]{2,1,0:T(8,128)(2,1)S(1)}, bf16[2,256,384]{2,1,0:T(8,128)(2,1)S(1)}, u32[]{:S(2)}, u32[]{:S(2)}) %collective-permute-start.13) | collective-permute-done | bytes 393248 | tf_op jit(solution)/shard_map/ppermute | solution.py:24
  104.3 2.3 %project.1 = (f32[816,128]{1,0:T(8,128)S(1)}, f32[816,128]{1,0:T(8,128)S(1)}) custom-call(s32[3]{0:T(128)S(1)} %pad_add_fusion.match, bf16[528,256]{1,0:T(8,128)(2,1)S(1)} %constant_dynamic-update-slice_fusion.refs_0_, bf16[528,256]{1,0:T(8,128)(2,1)S(1)} %collective-permute-done.4.refs_1_, bf16[528,256]{1,0:T(8,128)(2,1)S(1)} %collective-permute-done.5.refs_2_, ...), custom_call_target="tpu_custom_call" | custom-call | flops 830472192 | bytes 3735552 | tf_op jit(solution)/shard_map/project/pallas_call | solution.py:115
  106.6 7.0 %collective-permute-start.16 = (f32[816,128]{1,0:T(8,128)S(1)}, f32[816,128]{1,0:T(8,128)S(1)}, u32[]{:S(2)}, u32[]{:S(2)}) collective-permute-start(f32[816,128]{1,0:T(8,128)S(1)} %get-tuple-element.38), channel_id=1, source_target_pairs={{0,8},{8,0},{16,24},{24,16},{32,40},{40,32},{48,56},{56,48},{64,72... | collective-permute-start | bytes 1253384 | tf_op jit(solution)/shard_map/ppermute | solution.py:24
  113.6 1.4 collective-permute-done.16.theirs
  115.0 0.1 merge.1
  115.1 1.9 %collective-permute-start.17 = (f32[672,128]{1,0:T(8,128)S(1)}, f32[672,128]{1,0:T(8,128)S(1)}, u32[]{:S(2)}, u32[]{:S(2)}) collective-permute-start(f32[672,128]{1,0:T(8,128)S(1)} %get-tuple-element.40), channel_id=1, source_target_pairs={{0,16},{8,24},{16,0},{24,8},{32,48},{40,56},{48,32},{56,40},{64,80... | collective-permute-start | bytes 1032200 | tf_op jit(solution)/shard_map/ppermute | solution.py:24
  117.0 9.2 %collective-permute-done.17 = f32[672,128]{1,0:T(8,128)S(1)} collective-permute-done((f32[672,128]{1,0:T(8,128)S(1)}, f32[672,128]{1,0:T(8,128)S(1)}, u32[]{:S(2)}, u32[]{:S(2)}) %collective-permute-start.17) | collective-permute-done | bytes 344096 | tf_op jit(solution)/shard_map/ppermute | solution.py:24
  126.3 3.1 %collective-permute-start.18 = (bf16[528,128]{1,0:T(8,128)(2,1)S(1)}, bf16[528,128]{1,0:T(8,128)(2,1)S(1)}, u32[]{:S(2)}, u32[]{:S(2)}) collective-permute-start(bf16[528,128]{1,0:T(8,128)(2,1)S(1)} %fusion.mine), channel_id=1, source_target_pairs={{0,8},{8,0},{16,24},{24,16},{32,40},{40,32},{48,56},{56,48},{64,72... | collective-permute-start | bytes 405512 | tf_op jit(solution)/shard_map/ppermute | solution.py:24
  129.4 0.5 tables.1
  130.0 0.0 copy-start.3
  130.0 0.4 collective-permute-done.18.theirs
  130.4 0.3 copy-done.3
  130.7 0.7 drive.1
  131.4 2.3 %collective-permute-start.21 = (f32[16,128]{1,0:T(8,128)S(1)}, f32[16,128]{1,0:T(8,128)S(1)}, u32[]{:S(2)}, u32[]{:S(2)}) collective-permute-start(f32[16,128]{1,0:T(8,128)S(1)} %get-tuple-element.48.state), channel_id=1, source_target_pairs={{0,96},{8,104},{16,112},{24,120},{32,64},{40,72},{48,80},{56,88},{... | collective-permute-start | bytes 24584 | tf_op jit(solution)/shard_map/ppermute | solution.py:24
  133.7 2.1 %collective-permute-start.20 = (f32[16,128]{1,0:T(8,128)S(1)}, f32[16,128]{1,0:T(8,128)S(1)}, u32[]{:S(2)}, u32[]{:S(2)}) collective-permute-start(f32[16,128]{1,0:T(8,128)S(1)} %get-tuple-element.48.state), channel_id=1, source_target_pairs={{0,64},{8,72},{16,80},{24,88},{32,96},{40,104},{48,112},{56,120},{... | collective-permute-start | bytes 24584 | tf_op jit(solution)/shard_map/ppermute | solution.py:24
  135.8 8.8 %collective-permute-start.19 = (f32[16,128]{1,0:T(8,128)S(1)}, f32[16,128]{1,0:T(8,128)S(1)}, u32[]{:S(2)}, u32[]{:S(2)}) collective-permute-start(f32[16,128]{1,0:T(8,128)S(1)} %get-tuple-element.48.state), channel_id=1, source_target_pairs={{0,32},{8,40},{16,48},{24,56},{32,0},{40,8},{48,16},{56,24},{64,96... | collective-permute-start | bytes 24584 | tf_op jit(solution)/shard_map/ppermute | solution.py:24
  144.6 0.0 collective-permute-done.21.p3
  144.6 0.0 collective-permute-done.20.p2
  144.6 1.0 collective-permute-done.19.p1
  145.6 3.8 %collective-permute-start.24 = (f32[16,128]{1,0:T(8,128)S(1)}, f32[16,128]{1,0:T(8,128)S(1)}, u32[]{:S(2)}, u32[]{:S(2)}) collective-permute-start(f32[16,128]{1,0:T(8,128)S(1)} %get-tuple-element.53), channel_id=1, source_target_pairs={{0,384},{8,392},{16,400},{24,408},{32,416},{40,424},{48,432},{56,4... | collective-permute-start | bytes 24584 | tf_op jit(solution)/shard_map/ppermute | solution.py:24
  149.4 3.0 %collective-permute-start.23 = (f32[16,128]{1,0:T(8,128)S(1)}, f32[16,128]{1,0:T(8,128)S(1)}, u32[]{:S(2)}, u32[]{:S(2)}) collective-permute-start(f32[16,128]{1,0:T(8,128)S(1)} %get-tuple-element.53), channel_id=1, source_target_pairs={{0,256},{8,264},{16,272},{24,280},{32,288},{40,296},{48,304},{56,3... | collective-permute-start | bytes 24584 | tf_op jit(solution)/shard_map/ppermute | solution.py:24
  152.5 2.1 %collective-permute-start.22 = (f32[16,128]{1,0:T(8,128)S(1)}, f32[16,128]{1,0:T(8,128)S(1)}, u32[]{:S(2)}, u32[]{:S(2)}) collective-permute-start(f32[16,128]{1,0:T(8,128)S(1)} %get-tuple-element.53), channel_id=1, source_target_pairs={{0,128},{8,136},{16,144},{24,152},{32,160},{40,168},{48,176},{56,1... | collective-permute-start | bytes 24584 | tf_op jit(solution)/shard_map/ppermute | solution.py:24
  154.6 0.0 copy-start.4
  154.6 0.6 copy-done.4
  155.3 0.3 near.1.inner
  155.6 0.0 collective-permute-done.23.p2
  155.6 1.5 collective-permute-done.22.p1
  157.1 0.8 finish.1
  (23 shorter events, 0.3 us)
Async XLA Ops:
  0.0 0.9 copy-start
  1.0 9.8 %collective-permute-start = (bf16[2,128,256]{2,1,0:T(8,128)(2,1)S(1)}, bf16[2,128,256]{2,1,0:T(8,128)(2,1)S(1)}, u32[]{:S(2)}, u32[]{:S(2)}) collective-permute-start(bf16[2,128,256]{2,1,0:T(8,128)(2,1)S(1)} %get-tuple-element.30), channel_id=1, source_target_pairs={{0,8},{8,0},{16,24},{24,16},{32,40},{40,32},{48,56},{56,48},{64,72... | collective-permute-start | bytes 393224 | tf_op jit(solution)/shard_map/ppermute | solution.py:24
  10.8 2.0 %copy-start.5 = (bf16[3,128,128]{2,1,0:T(8,128)(2,1)S(1)}, bf16[3,128,128]{2,1,0:T(8,128)(2,1)}, u32[]{:S(2)}) copy-start(bf16[3,128,128]{2,1,0:T(8,128)(2,1)} %param.7) | copy-start | bytes 294916
  10.9 7.1 %collective-permute-start.1 = (bf16[256,256]{1,0:T(8,128)(2,1)S(1)}, bf16[256,256]{1,0:T(8,128)(2,1)S(1)}, u32[]{:S(2)}, u32[]{:S(2)}) collective-permute-start(bf16[256,256]{1,0:T(8,128)(2,1)S(1)} %get-tuple-element.32), channel_id=1, source_target_pairs={{0,16},{8,24},{16,0},{24,8},{32,48},{40,56},{48,32},{56,40},{64,80... | collective-permute-start | bytes 393224 | tf_op jit(solution)/shard_map/ppermute | solution.py:24
  12.9 16.4 %collective-permute-start.2 = (bf16[1,128,384]{2,1,0:T(8,128)(2,1)S(1)}, bf16[1,128,384]{2,1,0:T(8,128)(2,1)S(1)}, u32[]{:S(2)}, u32[]{:S(2)}) collective-permute-start(bf16[1,128,384]{2,1,0:T(8,128)(2,1)S(1)} %maximum_bitcast_fusion), channel_id=1, source_target_pairs={{0,64},{8,72},{16,80},{24,88},{32,96},{40,104},{48,112},{56,120},{... | collective-permute-start | bytes 294920 | tf_op jit(solution)/shard_map/ppermute | solution.py:24
  18.0 52.6 %collective-permute-start.8 = (bf16[512,256]{1,0:T(8,128)(2,1)S(1)}, bf16[512,256]{1,0:T(8,128)(2,1)S(1)}, u32[]{:S(2)}, u32[]{:S(2)}) collective-permute-start(bf16[512,256]{1,0:T(8,128)(2,1)S(1)} %pad_maximum_fusion.1), channel_id=1, source_target_pairs={{0,4},{1,5},{2,6},{3,7},{4,0},{5,1},{6,2},{7,3},{8,12},{9,13},{10,... | collective-permute-start | bytes 786440 | tf_op jit(solution)/shard_map/ppermute | solution.py:24
  29.2 12.1 %collective-permute-start.3 = (bf16[16,256]{1,0:T(8,128)(2,1)S(1)}, bf16[16,256]{1,0:T(8,128)(2,1)S(1)}, u32[]{:S(2)}, u32[]{:S(2)}) collective-permute-start(bf16[16,256]{1,0:T(8,128)(2,1)S(1)} %slice.31), channel_id=1, source_target_pairs={{0,32},{8,40},{16,48},{24,56},{32,64},{40,72},{48,80},{56,88},{64,... | collective-permute-start | bytes 24584 | tf_op jit(solution)/shard_map/ppermute | solution.py:29
  30.9 44.3 %collective-permute-start.12 = (bf16[2,128,384]{2,1,0:T(8,128)(2,1)S(1)}, bf16[2,128,384]{2,1,0:T(8,128)(2,1)S(1)}, u32[]{:S(2)}, u32[]{:S(2)}) collective-permute-start(bf16[2,128,384]{2,1,0:T(8,128)(2,1)S(1)} %pad_maximum_fusion.2), channel_id=1, source_target_pairs={{0,32},{8,40},{16,48},{24,56},{32,0},{40,8},{48,16},{56,24},{64,96... | collective-permute-start | bytes 589832 | tf_op jit(solution)/shard_map/ppermute | solution.py:24
  41.3 27.1 %collective-permute-start.7 = (bf16[16,256]{1,0:T(8,128)(2,1)S(1)}, bf16[16,256]{1,0:T(8,128)(2,1)S(1)}, u32[]{:S(2)}, u32[]{:S(2)}) collective-permute-start(bf16[16,256]{1,0:T(8,128)(2,1)S(1)} %collective-permute-done.3), channel_id=1, source_target_pairs={{0,4},{1,5},{2,6},{3,7},{4,0},{5,1},{6,2},{7,3},{8,12},{9,13},{10,... | collective-permute-start | bytes 24584 | tf_op jit(solution)/shard_map/ppermute | solution.py:24
  61.4 26.1 %collective-permute-start.6 = (bf16[528,256]{1,0:T(8,128)(2,1)S(1)}, bf16[528,256]{1,0:T(8,128)(2,1)S(1)}, u32[]{:S(2)}, u32[]{:S(2)}) collective-permute-start(bf16[528,256]{1,0:T(8,128)(2,1)S(1)} %constant_dynamic-update-slice_fusion.refs_0_), channel_id=1, source_target_pairs={{0,3},{1,2},{2,1},{3,0},{4,7},{5,6},{6,5},{7,4},{8,11},{9,10},{10,... | collective-permute-start | bytes 811016 | tf_op jit(solution)/shard_map/ppermute | solution.py:24
  66.2 23.9 %collective-permute-start.5 = (bf16[528,256]{1,0:T(8,128)(2,1)S(1)}, bf16[528,256]{1,0:T(8,128)(2,1)S(1)}, u32[]{:S(2)}, u32[]{:S(2)}) collective-permute-start(bf16[528,256]{1,0:T(8,128)(2,1)S(1)} %constant_dynamic-update-slice_fusion.refs_0_), channel_id=1, source_target_pairs={{0,2},{1,3},{2,0},{3,1},{4,6},{5,7},{6,4},{7,5},{8,10},{9,11},{10,... | collective-permute-start | bytes 811016 | tf_op jit(solution)/shard_map/ppermute | solution.py:24
  68.4 23.6 %collective-permute-start.4 = (bf16[528,256]{1,0:T(8,128)(2,1)S(1)}, bf16[528,256]{1,0:T(8,128)(2,1)S(1)}, u32[]{:S(2)}, u32[]{:S(2)}) collective-permute-start(bf16[528,256]{1,0:T(8,128)(2,1)S(1)} %constant_dynamic-update-slice_fusion.refs_0_), channel_id=1, source_target_pairs={{0,1},{1,0},{2,3},{3,2},{4,5},{5,4},{6,7},{7,6},{8,9},{9,8},{10,11... | collective-permute-start | bytes 811016 | tf_op jit(solution)/shard_map/ppermute | solution.py:24
  70.7 23.6 %collective-permute-start.11 = (bf16[528,256]{1,0:T(8,128)(2,1)S(1)}, bf16[528,256]{1,0:T(8,128)(2,1)S(1)}, u32[]{:S(2)}, u32[]{:S(2)}) collective-permute-start(bf16[528,256]{1,0:T(8,128)(2,1)S(1)} %constant_dynamic-update-slice_fusion.2.refs_4_), channel_id=1, source_target_pairs={{0,3},{1,2},{2,1},{3,0},{4,7},{5,6},{6,5},{7,4},{8,11},{9,10},{10,... | collective-permute-start | bytes 811016 | tf_op jit(solution)/shard_map/ppermute | solution.py:24
  75.4 26.5 %collective-permute-start.15 = (bf16[2,256,384]{2,1,0:T(8,128)(2,1)S(1)}, bf16[2,256,384]{2,1,0:T(8,128)(2,1)S(1)}, u32[]{:S(2)}, u32[]{:S(2)}) collective-permute-start(bf16[2,256,384]{2,1,0:T(8,128)(2,1)S(1)} %pad_maximum_fusion.refs_8_), channel_id=1, source_target_pairs={{0,384},{8,392},{16,400},{24,408},{32,416},{40,424},{48,432},{56,4... | collective-permute-start | bytes 1179656 | tf_op jit(solution)/shard_map/ppermute | solution.py:24
  87.6 14.3 %collective-permute-start.14 = (bf16[2,256,384]{2,1,0:T(8,128)(2,1)S(1)}, bf16[2,256,384]{2,1,0:T(8,128)(2,1)S(1)}, u32[]{:S(2)}, u32[]{:S(2)}) collective-permute-start(bf16[2,256,384]{2,1,0:T(8,128)(2,1)S(1)} %pad_maximum_fusion.refs_8_), channel_id=1, source_target_pairs={{0,256},{8,264},{16,272},{24,280},{32,288},{40,296},{48,304},{56,3... | collective-permute-start | bytes 1179656 | tf_op jit(solution)/shard_map/ppermute | solution.py:24
  90.1 14.2 %collective-permute-start.13 = (bf16[2,256,384]{2,1,0:T(8,128)(2,1)S(1)}, bf16[2,256,384]{2,1,0:T(8,128)(2,1)S(1)}, u32[]{:S(2)}, u32[]{:S(2)}) collective-permute-start(bf16[2,256,384]{2,1,0:T(8,128)(2,1)S(1)} %pad_maximum_fusion.refs_8_), channel_id=1, source_target_pairs={{0,128},{8,136},{16,144},{24,152},{32,160},{40,168},{48,176},{56,1... | collective-permute-start | bytes 1179656 | tf_op jit(solution)/shard_map/ppermute | solution.py:24
  92.0 9.0 %collective-permute-start.10 = (bf16[528,256]{1,0:T(8,128)(2,1)S(1)}, bf16[528,256]{1,0:T(8,128)(2,1)S(1)}, u32[]{:S(2)}, u32[]{:S(2)}) collective-permute-start(bf16[528,256]{1,0:T(8,128)(2,1)S(1)} %constant_dynamic-update-slice_fusion.2.refs_4_), channel_id=1, source_target_pairs={{0,2},{1,3},{2,0},{3,1},{4,6},{5,7},{6,4},{7,5},{8,10},{9,11},{10,... | collective-permute-start | bytes 811016 | tf_op jit(solution)/shard_map/ppermute | solution.py:24
  94.3 7.5 %collective-permute-start.9 = (bf16[528,256]{1,0:T(8,128)(2,1)S(1)}, bf16[528,256]{1,0:T(8,128)(2,1)}, u32[]{:S(2)}, u32[]{:S(2)}) collective-permute-start(bf16[528,256]{1,0:T(8,128)(2,1)S(1)} %constant_dynamic-update-slice_fusion.2.refs_4_), channel_id=1, source_target_pairs={{0,1},{1,0},{2,3},{3,2},{4,5},{5,4},{6,7},{7,6},{8,9},{9,8},{10,11... | collective-permute-start | bytes 811016 | tf_op jit(solution)/shard_map/ppermute | solution.py:24
  106.6 8.4 %collective-permute-start.16 = (f32[816,128]{1,0:T(8,128)S(1)}, f32[816,128]{1,0:T(8,128)S(1)}, u32[]{:S(2)}, u32[]{:S(2)}) collective-permute-start(f32[816,128]{1,0:T(8,128)S(1)} %get-tuple-element.38), channel_id=1, source_target_pairs={{0,8},{8,0},{16,24},{24,16},{32,40},{40,32},{48,56},{56,48},{64,72... | collective-permute-start | bytes 1253384 | tf_op jit(solution)/shard_map/ppermute | solution.py:24
  115.1 11.2 %collective-permute-start.17 = (f32[672,128]{1,0:T(8,128)S(1)}, f32[672,128]{1,0:T(8,128)S(1)}, u32[]{:S(2)}, u32[]{:S(2)}) collective-permute-start(f32[672,128]{1,0:T(8,128)S(1)} %get-tuple-element.40), channel_id=1, source_target_pairs={{0,16},{8,24},{16,0},{24,8},{32,48},{40,56},{48,32},{56,40},{64,80... | collective-permute-start | bytes 1032200 | tf_op jit(solution)/shard_map/ppermute | solution.py:24
  126.2 3.2 %copy-start.1 = (f32[128,16]{0,1:T(8,128)S(1)}, f32[128,16]{0,1:T(8,128)}, u32[]{:S(2)}) copy-start(f32[128,16]{0,1:T(8,128)} %param.9) | copy-start | bytes 24580
  126.2 3.2 %copy-start.2 = (f32[128,16]{0,1:T(8,128)S(1)}, f32[128,16]{0,1:T(8,128)}, u32[]{:S(2)}) copy-start(f32[128,16]{0,1:T(8,128)} %param.10) | copy-start | bytes 24580
  126.3 4.1 %collective-permute-start.18 = (bf16[528,128]{1,0:T(8,128)(2,1)S(1)}, bf16[528,128]{1,0:T(8,128)(2,1)S(1)}, u32[]{:S(2)}, u32[]{:S(2)}) collective-permute-start(bf16[528,128]{1,0:T(8,128)(2,1)S(1)} %fusion.mine), channel_id=1, source_target_pairs={{0,8},{8,0},{16,24},{24,16},{32,40},{40,32},{48,56},{56,48},{64,72... | collective-permute-start | bytes 405512 | tf_op jit(solution)/shard_map/ppermute | solution.py:24
  130.0 0.7 copy-start.3
  131.4 13.2 %collective-permute-start.21 = (f32[16,128]{1,0:T(8,128)S(1)}, f32[16,128]{1,0:T(8,128)S(1)}, u32[]{:S(2)}, u32[]{:S(2)}) collective-permute-start(f32[16,128]{1,0:T(8,128)S(1)} %get-tuple-element.48.state), channel_id=1, source_target_pairs={{0,96},{8,104},{16,112},{24,120},{32,64},{40,72},{48,80},{56,88},{... | collective-permute-start | bytes 24584 | tf_op jit(solution)/shard_map/ppermute | solution.py:24
  133.7 10.9 %collective-permute-start.20 = (f32[16,128]{1,0:T(8,128)S(1)}, f32[16,128]{1,0:T(8,128)S(1)}, u32[]{:S(2)}, u32[]{:S(2)}) collective-permute-start(f32[16,128]{1,0:T(8,128)S(1)} %get-tuple-element.48.state), channel_id=1, source_target_pairs={{0,64},{8,72},{16,80},{24,88},{32,96},{40,104},{48,112},{56,120},{... | collective-permute-start | bytes 24584 | tf_op jit(solution)/shard_map/ppermute | solution.py:24
  135.8 9.8 %collective-permute-start.19 = (f32[16,128]{1,0:T(8,128)S(1)}, f32[16,128]{1,0:T(8,128)S(1)}, u32[]{:S(2)}, u32[]{:S(2)}) collective-permute-start(f32[16,128]{1,0:T(8,128)S(1)} %get-tuple-element.48.state), channel_id=1, source_target_pairs={{0,32},{8,40},{16,48},{24,56},{32,0},{40,8},{48,16},{56,24},{64,96... | collective-permute-start | bytes 24584 | tf_op jit(solution)/shard_map/ppermute | solution.py:24
  145.6 10.0 %collective-permute-start.24 = (f32[16,128]{1,0:T(8,128)S(1)}, f32[16,128]{1,0:T(8,128)S(1)}, u32[]{:S(2)}, u32[]{:S(2)}) collective-permute-start(f32[16,128]{1,0:T(8,128)S(1)} %get-tuple-element.53), channel_id=1, source_target_pairs={{0,384},{8,392},{16,400},{24,408},{32,416},{40,424},{48,432},{56,4... | collective-permute-start | bytes 24584 | tf_op jit(solution)/shard_map/ppermute | solution.py:24
  149.4 6.2 %collective-permute-start.23 = (f32[16,128]{1,0:T(8,128)S(1)}, f32[16,128]{1,0:T(8,128)S(1)}, u32[]{:S(2)}, u32[]{:S(2)}) collective-permute-start(f32[16,128]{1,0:T(8,128)S(1)} %get-tuple-element.53), channel_id=1, source_target_pairs={{0,256},{8,264},{16,272},{24,280},{32,288},{40,296},{48,304},{56,3... | collective-permute-start | bytes 24584 | tf_op jit(solution)/shard_map/ppermute | solution.py:24
  152.5 4.7 %collective-permute-start.22 = (f32[16,128]{1,0:T(8,128)S(1)}, f32[16,128]{1,0:T(8,128)S(1)}, u32[]{:S(2)}, u32[]{:S(2)}) collective-permute-start(f32[16,128]{1,0:T(8,128)S(1)} %get-tuple-element.53), channel_id=1, source_target_pairs={{0,128},{8,136},{16,144},{24,152},{32,160},{40,168},{48,176},{56,1... | collective-permute-start | bytes 24584 | tf_op jit(solution)/shard_map/ppermute | solution.py:24
  154.6 0.7 copy-start.4

commit v4 on v3

--- a/solution.py
+++ b/solution.py
@@ -35,55 +35,74 @@
     return jnp.concatenate([first, second], axis=axis)
 
 
+def share(x, axis, groups):
+    size = len(groups[0])
+    return swap(jnp.broadcast_to(x[None], (size,) + x.shape), axis, groups)
+
+
+def swap(x, axis, groups):
+    return lax.all_to_all(x, axis, 0, 0, axis_index_groups=groups)
+
+
+NEIGHBOURS = [[4 * i + j for j in range(4)] for i in range(16)]
+LINE = [[16 * x + 4 * i + low for i in range(4)] for x in range(4) for low in range(4)]
+ACROSS = [[p + 16 * i for i in range(4)] for p in range(16)]
+ROUND = [[0, 1, 2, 3], [4, 5, 6, 7]]
+
+
 def flip_many(x, axis, masks):
     return [flip(x, axis, m) for m in masks]
 
 
-def split_kernel(place, tokens, kept, given):
+def split_kernel(place, tokens, halo, kept, given):
     core = place[0] & 1
     for out, side in ((kept, core), (given, 1 - core)):
         for bit8 in range(2):
             for bit9 in range(2):
                 start = pl.multiple_of(512 * bit9 + 256 * bit8 + side * 128, 128)
-                out[bit8, :, 128 * bit9 : 128 * bit9 + 128] = tokens[:, pl.ds(start, 128)]
-
-
-def split(place, tokens):
-    shape = jax.ShapeDtypeStruct((2, BLOCK, 256), BF16)
+                there = slice(128 * bit9, 128 * bit9 + 128)
+                out[bit8, :HALO, there] = halo[:, pl.ds(start, 128)]
+                out[bit8, HALO:, there] = tokens[:, pl.ds(start, 128)]
+
+
+def split(place, tokens, halo):
+    shape = jax.ShapeDtypeStruct((2, PIECE, 256), BF16)
     return pl.pallas_call(
         split_kernel,
         out_shape=(shape, shape),
-        in_specs=[SMEM, VMEM],
+        in_specs=[SMEM, VMEM, VMEM],
         out_specs=(VMEM, VMEM),
         compiler_params=PARAMS,
         name="split",
-    )(place, tokens)
+    )(place, tokens, halo)
+
+
+def joined(upper, own, other, axis):
+    first = jnp.where(upper, other, own)
+    second = jnp.where(upper, own, other)
+    rest = lax.slice_in_dim(second, HALO, second.shape[axis], axis=axis)
+    return jnp.concatenate([first, rest], axis=axis)
 
 
 def gather(tokens, in_weight, place):
-    kept, given = split(place[None], tokens)
-    both = ordered((place & 1) == 1, kept, flip(given, "ctx", 1), 1)
+    held = jnp.concatenate([in_weight[1], in_weight[2], in_weight[0]], axis=1)[None]
+    held = jnp.concatenate([held, flip(held, "ctx", 8)], axis=0)
+    held = ordered((place & 4) == 4, held, flip(held, "ctx", 4), 1)
+    weights = [held] + flip_many(held, "ctx", (16, 32, 48))
+    halo = ahead(tokens[BLOCK - HALO :], "ctx", 1)
+    kept, given = split(place[None], tokens, halo)
+    both = joined((place & 1) == 1, kept, flip(given, "ctx", 1), 1)
     upper = (place & 2) == 2
     keep = jnp.where(upper, both[1], both[0])
     give = jnp.where(upper, both[0], both[1])
-    keep, give, in_weight = lax.optimization_barrier((keep, give, in_weight))
-    held = jnp.concatenate([in_weight[1], in_weight[2], in_weight[0]], axis=1)[None]
-    near_h = ordered(upper, keep, flip(give, "ctx", 2), 0)
-    past = flip(held, "ctx", 8)
-    far_h = flip(near_h, "tp", 4)
-    near_h, past = lax.optimization_barrier((near_h, past))
-    halo = ahead(near_h[GROUP - HALO :], "ctx", 4)
-    held = jnp.concatenate([held, past], axis=0)
-    held = ordered((place & 4) == 4, held, flip(held, "ctx", 4), 1)
-    far_halo = flip(halo, "tp", 4)
-    found = []
-    for part in (jnp.concatenate([halo, near_h]), jnp.concatenate([far_halo, far_h])):
-        found += [part] + flip_many(part, "tp", (1, 2, 3))
-    return found, [held] + flip_many(held, "ctx", (16, 32, 48))
-
-
-def project_kernel(match, *refs):
-    tokens, weights, kept, given, total = refs[:8], refs[8:12], refs[12], refs[13], refs[14]
+    near_h = joined(upper, keep, flip(give, "ctx", 2), 0)
+    turns = [near_h] + flip_many(near_h, "tp", (1, 2, 3))
+    far_h, turns, weights[2] = lax.optimization_barrier((flip(near_h, "tp", 4), turns, weights[2]))
+    return turns, share(far_h, "tp", ROUND), weights
+
+
+def project_kernel(match, t0, t1, t2, t3, far_h, w0, w1, w2, w3, kept, given, total):
+    near_h, weights = (t0, t1, t2, t3), (w0, w1, w2, w3)
     for case in range(4):
 
         @pl.when(match[0] == case)
@@ -91,9 +110,10 @@
             added = jnp.zeros(total.shape, F32)
             for turn in range(8):
                 turn_h, turn_y = turn >> 2, turn & 3
+                part = far_h[match[3] ^ turn_y] if turn_h else near_h[turn_y][...]
                 turn_x = case ^ (turn_h << 1 | turn_y >> 1)
                 weight = weights[turn_x][match[1] ^ (turn_y & 1)]
-                added += jnp.dot(tokens[turn][...], weight, preferred_element_type=F32)
+                added += jnp.dot(part, weight, preferred_element_type=F32)
             total[...] = added
 
     for core in range(2):
@@ -109,13 +129,13 @@
                     ]
 
 
-def project(match, tokens, weights):
+def project(match, near_h, far_h, weights):
     columns = weights[0].shape[2]
     shape = jax.ShapeDtypeStruct((ROWS + OWN, BLOCK), F32)
     return pl.pallas_call(
         project_kernel,
         out_shape=(shape, shape),
-        in_specs=[SMEM] + [VMEM] * 12,
+        in_specs=[SMEM] + [VMEM] * 9,
         out_specs=(VMEM, VMEM),
         scratch_shapes=[pltpu.VMEM((ROWS, columns), F32)],
         compiler_params=PARAMS,
@@ -123,7 +143,7 @@
             flops=2 * ROWS * 2048 * columns, bytes_accessed=2048 * 2 * (ROWS + columns), transcendentals=0
         ),
         name="project",
-    )(match, *tokens, *weights)
+    )(match, *near_h, far_h, *weights)
 
 
 def merge_kernel(place, mine, theirs, pair, query, gift):
@@ -176,15 +196,17 @@
             held = jnp.where(spot == b, past, held)
             past = decay * past + jnp.sum(w * signal[BLOCK * b : BLOCK * b + BLOCK], axis=0, keepdims=True)
         before[r : r + 1] = held
-        state[r : r + 1] = past
+        for i in range(4):
+            state[i, r : r + 1] = past
 
 
 def drive(place, mine, theirs, own, other, taps, weigh, step):
     square = jax.ShapeDtypeStruct((BLOCK, BLOCK), F32)
     modes = jax.ShapeDtypeStruct((MODES, BLOCK), F32)
+    copies = jax.ShapeDtypeStruct((4, MODES, BLOCK), F32)
     return pl.pallas_call(
         drive_kernel,
-        out_shape=(square, square, modes, modes),
+        out_shape=(square, square, modes, copies),
         in_specs=[SMEM] + [VMEM] * 7,
         out_specs=(VMEM,) * 4,
         scratch_shapes=[pltpu.VMEM((GROUP, BLOCK), F32)],
@@ -207,13 +229,11 @@
     taps[...] = total
     rate = rates[...]
     step[...] = jnp.exp(-rate * float(BLOCK))
-    for turn in range(4):
-        group = (line >> 2) ^ turn
-        whole[turn] = jnp.exp(-rate * (GROUP * (3 - group)).astype(F32))
-        if turn:
-            for out, after in ((toward, line - 4 * (group + 1)), (last, at - 16 * (((at >> 4) ^ turn) + 1))):
-                decay = jnp.exp(-rate * (BLOCK * jnp.maximum(after, 0)).astype(F32))
-                out[turn - 1] = jnp.where(after >= 0, decay, 0.0)
+    for i in range(4):
+        whole[i] = jnp.exp(-rate * float(GROUP * (3 - i)))
+        for out, after in ((toward, line - 4 * (i + 1)), (last, at - 16 * (i + 1))):
+            decay = jnp.exp(-rate * (BLOCK * jnp.maximum(after, 0)).astype(F32))
+            out[i] = jnp.where(after >= 0, decay, 0.0)
 
 
 def tables(place, residues, rates):
@@ -227,9 +247,9 @@
             full(MODES, BLOCK, BLOCK),
             full(BLOCK, BLOCK),
             full(MODES, BLOCK),
-            full(3, MODES, BLOCK),
             full(4, MODES, BLOCK),
-            full(3, MODES, BLOCK),
+            full(4, MODES, BLOCK),
+            full(4, MODES, BLOCK),
         ),
         in_specs=[SMEM, VMEM, VMEM],
         out_specs=(VMEM,) * 7,
@@ -238,21 +258,27 @@
     )(place, residues, rates)
 
 
-def advance_kernel(state, p1, p2, p3, before, toward, whole, out_before, out_state):
-    out_before[...] = before[...] + toward[0] * p1[...] + toward[1] * p2[...] + toward[2] * p3[...]
-    out_state[...] = whole[0] * state[...] + whole[1] * p1[...] + whole[2] * p2[...] + whole[3] * p3[...]
-
-
-def advance(state, others, before, toward, whole):
+def advance_kernel(states, before, toward, whole, out_before, out_state):
+    held, total = before[...], jnp.zeros((MODES, BLOCK), F32)
+    for i in range(4):
+        held = held + toward[i] * states[i]
+        total = total + whole[i] * states[i]
+    out_before[...] = held
+    for i in range(4):
+        out_state[i] = total
+
+
+def advance(states, before, toward, whole):
     modes = jax.ShapeDtypeStruct((MODES, BLOCK), F32)
+    copies = jax.ShapeDtypeStruct((4, MODES, BLOCK), F32)
     return pl.pallas_call(
         advance_kernel,
-        out_shape=(modes, modes),
-        in_specs=[VMEM] * 7,
+        out_shape=(modes, copies),
+        in_specs=[VMEM] * 4,
         out_specs=(VMEM, VMEM),
         compiler_params=PARAMS,
         name="advance",
-    )(state, *others, before, toward, whole)
+    )(states, before, toward, whole)
 
 
 def near_kernel(driven, taps, gain, out, padded):
@@ -282,23 +308,25 @@
     )(driven, taps, gain)
 
 
-def finish_kernel(query, inner, reach, before, p1, p2, p3, last, out):
-    carry = before[...] + last[0] * p1[...] + last[1] * p2[...] + last[2] * p3[...]
+def finish_kernel(query, inner, reach, before, states, last, out):
+    carry = before[...]
+    for i in range(4):
+        carry = carry + last[i] * states[i]
     conv = inner[...]
     for r in range(MODES):
         conv = conv + reach[r] * carry[r : r + 1]
     out[...] = (query[...] * conv).T
 
 
-def finish(query, inner, reach, before, others, last):
+def finish(query, inner, reach, before, states, last):
     return pl.pallas_call(
         finish_kernel,
         out_shape=jax.ShapeDtypeStruct((BLOCK, BLOCK), F32),
-        in_specs=[VMEM] * 8,
+        in_specs=[VMEM] * 6,
         out_specs=VMEM,
         compiler_params=PARAMS,
         name="finish",
-    )(query, inner, reach, before, *others, last)
+    )(query, inner, reach, before, states, last)
 
 
 def body(tokens, in_weight, short_taps, residues, rates, skip_gain):
@@ -306,23 +334,21 @@
     tp = lax.axis_index("tp")
     spot = place[None]
     apart = tp ^ (place >> 3)
-    match = jnp.stack([apart >> 1, apart & 1, place & 1])
-
-    features, weights = gather(tokens, in_weight, place)
+    match = jnp.stack([apart >> 1, apart & 1, place & 1, tp & 3])
+
+    near_h, far_h, weights = gather(tokens, in_weight, place)
     weigh, reach, taps, step, toward, whole, last = tables(spot, residues.T, rates.T)
 
-    mine, gift = project(match, features, weights)
+    mine, gift = project(match, near_h, far_h, weights)
     pair, own, gift = merge(spot, mine, flip(gift, "ctx", 1))
     theirs = flip(gift, "ctx", 2)
     mine = (pair + theirs[:ROWS]).astype(BF16)
     query, driven, before, state = drive(
         spot, mine, flip(mine, "ctx", 1), own, theirs[ROWS:], short_taps.transpose(0, 2, 1), weigh, step
     )
-    others = flip_many(state, "ctx", (4, 8, 12))
     inner = near(driven, taps, skip_gain[None])
-    before, state = advance(state, others, before, toward, whole)
-    others = flip_many(state, "ctx", (16, 32, 48))
-    return finish(query, inner, reach, before, others, last)
+    before, state = advance(swap(state, "ctx", LINE), before, toward, whole)
+    return finish(query, inner, reach, before, swap(state, "ctx", ACROSS), last)
 
 
 def solution(mesh):

time: 160 us -> 146 us (0.912)
  starting transfers between devices: 121 us -> 76.4 us
  blocking collectives: 0 us -> 15 us
  waiting for transfers between devices: 29.6 us -> 41.9 us
  local copies, waits for them, and re-layouts: 1.99 us -> 4.58 us
    ppermute x24 -> x14, starting transfers between devices: 119 us -> 65.3 us  [flip(): return lax.ppermute(x, axis, [(i, i ^ mask) for i in range(length)])]
    all_to_all x0 -> x1, blocking collectives: none -> 15 us  [swap(): return lax.all_to_all(x, axis, 0, 0, axis_index_groups=groups)]
    ppermute x24 -> x14, waiting for transfers between devices: 23.4 us -> 36.9 us  [flip(): return lax.ppermute(x, axis, [(i, i ^ mask) for i in range(length)])]
    all_to_all x0 -> x2, starting transfers between devices: none -> 6.78 us  [swap(): return lax.all_to_all(x, axis, 0, 0, axis_index_groups=groups)]
    ppermute x1, waiting for transfers between devices: 6.15 us -> 1 us  [ahead(): return lax.ppermute(x, axis, [(i, i + by) for i in range(length - by)])]
    all_to_all x0 -> x2, waiting for transfers between devices: none -> 3.92 us  [swap(): return lax.all_to_all(x, axis, 0, 0, axis_index_groups=groups)]
    ppermute x1, starting transfers between devices: 1.64 us -> 4.37 us  [ahead(): return lax.ppermute(x, axis, [(i, i + by) for i in range(length - by)])]
  transfers between devices with their start and end apart: 25 -> 17, of which waited for: 11 -> 11; matrix products, arithmetic and copies ran while one was open for 0% -> 1% of each run, Pallas kernels for 1% -> 1%
where the time goes in v4:
time: 146 us; the launch traced here: 144 us
  starting transfers between devices  76.4 us (52%)
  waiting for transfers between devices  41.9 us (29%)
  blocking collectives  15 us (10%)
  Pallas kernels  5.05 us (3%)
  local copies, waits for them, and re-layouts  4.58 us (3%)
    ppermute x14, starting transfers between devices, flip(): return lax.ppermute(x, axis, [(i, i ^ mask) for i in range(length)])  65.3 us
    ppermute x14, waiting for transfers between devices, flip(): return lax.ppermute(x, axis, [(i, i ^ mask) for i in range(length)])  36.9 us
    all_to_all x1, blocking collectives, swap(): return lax.all_to_all(x, axis, 0, 0, axis_index_groups=groups)  15 us
    all_to_all x2, starting transfers between devices, swap(): return lax.all_to_all(x, axis, 0, 0, axis_index_groups=groups)  6.78 us
    ppermute x1, starting transfers between devices, ahead(): return lax.ppermute(x, axis, [(i, i + by) for i in range(length - by)])  4.37 us
    all_to_all x2, waiting for transfers between devices, swap(): return lax.all_to_all(x, axis, 0, 0, axis_index_groups=groups)  3.92 us
  transfers between devices with their start and end apart: 17, of which 11 were waited for; matrix products, arithmetic and copies ran while one was open for 1% of the time, Pallas kernels for 1%

profile of v4, /device:TPU:1, one launch (start us, length us, event | category | flops | bytes accessed | tf_op | source)
XLA Modules:
  0.0 143.7 jit_solution(2573828853705741317)
XLA Ops:
  0.0 0.8 slice_bitcast_fusion.2
  0.8 9.6 %collective-permute-start.7 = (bf16[1,128,384]{2,1,0:T(8,128)(2,1)S(1)}, bf16[1,128,384]{2,1,0:T(8,128)(2,1)S(1)}, u32[]{:S(2)}, u32[]{:S(2)}) collective-permute-start(bf16[1,128,384]{2,1,0:T(8,128)(2,1)S(1)} %maximum_bitcast_fusion), channel_id=1, source_target_pairs={{0,64},{8,72},{16,80},{24,88},{32,96},{40,104},{48,112},{56,120},{... | collective-permute-start | bytes 294920 | tf_op jit(solution)/shard_map/ppermute | solution.py:24
  10.5 0.8 slice.32
  11.2 4.4 %collective-permute-start = (bf16[16,1024]{1,0:T(8,128)(2,1)S(1)}, bf16[16,1024]{1,0:T(8,128)(2,1)S(1)}, u32[]{:S(2)}, u32[]{:S(2)}) collective-permute-start(bf16[16,1024]{1,0:T(8,128)(2,1)S(1)} %slice.32), channel_id=1, source_target_pairs={{0,8},{8,16},{16,24},{24,32},{32,40},{40,48},{48,56},{56,64},{64,7... | collective-permute-start | bytes 98312 | tf_op jit(solution)/shard_map/ppermute | solution.py:29
  15.6 1.0 collective-permute-done.halo
  16.6 0.0 copy-start
  16.6 0.9 copy-done
  17.6 0.1 split.1
  17.6 1.9 %collective-permute-start.1 = (bf16[2,144,256]{2,1,0:T(8,128)(2,1)S(1)}, bf16[2,144,256]{2,1,0:T(8,128)(2,1)S(1)}, u32[]{:S(2)}, u32[]{:S(2)}) collective-permute-start(bf16[2,144,256]{2,1,0:T(8,128)(2,1)S(1)} %get-tuple-element.31), channel_id=1, source_target_pairs={{0,8},{8,0},{16,24},{24,16},{32,40},{40,32},{48,56},{56,48},{64,72... | collective-permute-start | bytes 442376 | tf_op jit(solution)/shard_map/ppermute | solution.py:24
  19.6 0.0 collective-permute-done.7
  19.6 5.7 %collective-permute-start.8 = (bf16[2,128,384]{2,1,0:T(8,128)(2,1)S(1)}, bf16[2,128,384]{2,1,0:T(8,128)(2,1)S(1)}, u32[]{:S(2)}, u32[]{:S(2)}) collective-permute-start(bf16[2,128,384]{2,1,0:T(8,128)(2,1)S(1)} %pad_maximum_fusion.2), channel_id=1, source_target_pairs={{0,32},{8,40},{16,48},{24,56},{32,0},{40,8},{48,16},{56,24},{64,96... | collective-permute-start | bytes 589832 | tf_op jit(solution)/shard_map/ppermute | solution.py:24
  25.3 0.0 collective-permute-done.1
  25.4 4.5 %collective-permute-start.2 = (bf16[272,256]{1,0:T(8,128)(2,1)S(1)}, bf16[272,256]{1,0:T(8,128)(2,1)S(1)}, u32[]{:S(2)}, u32[]{:S(2)}) collective-permute-start(bf16[272,256]{1,0:T(8,128)(2,1)S(1)} %select_bitcast_fusion.1), channel_id=1, source_target_pairs={{0,16},{8,24},{16,0},{24,8},{32,48},{40,56},{48,32},{56,40},{64,80... | collective-permute-start | bytes 417800 | tf_op jit(solution)/shard_map/ppermute | solution.py:24
  30.0 4.8 %collective-permute-done.8 = bf16[2,128,384]{2,1,0:T(8,128)(2,1)S(1)} collective-permute-done((bf16[2,128,384]{2,1,0:T(8,128)(2,1)S(1)}, bf16[2,128,384]{2,1,0:T(8,128)(2,1)S(1)}, u32[]{:S(2)}, u32[]{:S(2)}) %collective-permute-start.8) | collective-permute-done | bytes 196640 | tf_op jit(solution)/shard_map/ppermute | solution.py:24
  34.7 0.1 broadcast_select_fusion.1
  34.8 7.2 %collective-permute-start.9 = (bf16[2,256,384]{2,1,0:T(8,128)(2,1)S(1)}, bf16[2,256,384]{2,1,0:T(8,128)(2,1)S(1)}, u32[]{:S(2)}, u32[]{:S(2)}) collective-permute-start(bf16[2,256,384]{2,1,0:T(8,128)(2,1)S(1)} %pad_maximum_fusion.w0), channel_id=1, source_target_pairs={{0,256},{8,264},{16,272},{24,280},{32,288},{40,296},{48,304},{56,3... | collective-permute-start | bytes 1179656 | tf_op jit(solution)/shard_map/ppermute | solution.py:24
  42.0 0.0 collective-permute-done.2
  42.0 0.1 broadcast_select_fusion.3
  42.2 10.6 %collective-permute-start.3 = (bf16[528,256]{1,0:T(8,128)(2,1)S(1)}, bf16[528,256]{1,0:T(8,128)(2,1)S(1)}, u32[]{:S(2)}, u32[]{:S(2)}) collective-permute-start(bf16[528,256]{1,0:T(8,128)(2,1)S(1)} %pad_maximum_fusion.1.t0), channel_id=1, source_target_pairs={{0,4},{1,5},{2,6},{3,7},{4,0},{5,1},{6,2},{7,3},{8,12},{9,13},{10,... | collective-permute-start | bytes 811016 | tf_op jit(solution)/shard_map/ppermute | solution.py:24
  52.8 3.2 %collective-permute-start.4 = (bf16[528,256]{1,0:T(8,128)(2,1)S(1)}, bf16[528,256]{1,0:T(8,128)(2,1)S(1)}, u32[]{:S(2)}, u32[]{:S(2)}) collective-permute-start(bf16[528,256]{1,0:T(8,128)(2,1)S(1)} %pad_maximum_fusion.1.t0), channel_id=1, source_target_pairs={{0,1},{1,0},{2,3},{3,2},{4,5},{5,4},{6,7},{7,6},{8,9},{9,8},{10,11... | collective-permute-start | bytes 811016 | tf_op jit(solution)/shard_map/ppermute | solution.py:24
  56.0 4.5 %collective-permute-start.5 = (bf16[528,256]{1,0:T(8,128)(2,1)S(1)}, bf16[528,256]{1,0:T(8,128)(2,1)S(1)}, u32[]{:S(2)}, u32[]{:S(2)}) collective-permute-start(bf16[528,256]{1,0:T(8,128)(2,1)S(1)} %pad_maximum_fusion.1.t0), channel_id=1, source_target_pairs={{0,2},{1,3},{2,0},{3,1},{4,6},{5,7},{6,4},{7,5},{8,10},{9,11},{10,... | collective-permute-start | bytes 811016 | tf_op jit(solution)/shard_map/ppermute | solution.py:24
  60.6 1.9 %collective-permute-start.6 = (bf16[528,256]{1,0:T(8,128)(2,1)S(1)}, bf16[528,256]{1,0:T(8,128)(2,1)S(1)}, u32[]{:S(2)}, u32[]{:S(2)}) collective-permute-start(bf16[528,256]{1,0:T(8,128)(2,1)S(1)} %pad_maximum_fusion.1.t0), channel_id=1, source_target_pairs={{0,3},{1,2},{2,1},{3,0},{4,7},{5,6},{6,5},{7,4},{8,11},{9,10},{10,... | collective-permute-start | bytes 811016 | tf_op jit(solution)/shard_map/ppermute | solution.py:24
  62.5 3.7 %collective-permute-done.3 = bf16[528,256]{1,0:T(8,128)(2,1)S(1)} collective-permute-done((bf16[528,256]{1,0:T(8,128)(2,1)S(1)}, bf16[528,256]{1,0:T(8,128)(2,1)S(1)}, u32[]{:S(2)}, u32[]{:S(2)}) %collective-permute-start.3) | collective-permute-done | bytes 270368 | tf_op jit(solution)/shard_map/ppermute | solution.py:24
  66.2 0.0 collective-permute-done.4.t1
  66.2 3.4 %collective-permute-done.5.t2 = bf16[528,256]{1,0:T(8,128)(2,1)S(1)} collective-permute-done((bf16[528,256]{1,0:T(8,128)(2,1)S(1)}, bf16[528,256]{1,0:T(8,128)(2,1)S(1)}, u32[]{:S(2)}, u32[]{:S(2)}) %collective-permute-start.5) | collective-permute-done | bytes 270368 | tf_op jit(solution)/shard_map/ppermute | solution.py:24
  69.5 6.3 %collective-permute-done.6.t3 = bf16[528,256]{1,0:T(8,128)(2,1)S(1)} collective-permute-done((bf16[528,256]{1,0:T(8,128)(2,1)S(1)}, bf16[528,256]{1,0:T(8,128)(2,1)S(1)}, u32[]{:S(2)}, u32[]{:S(2)}) %collective-permute-start.6) | collective-permute-done | bytes 270368 | tf_op jit(solution)/shard_map/ppermute | solution.py:24
  75.9 0.0 copy-start.1
  75.9 0.0 collective-permute-done.9.w2
  75.9 1.1 broadcast_in_dim.18
  76.9 0.0 copy-done.1
  76.9 3.5 %all-to-all-start = ((bf16[4,528,256]{2,1,0:T(8,128)(2,1)}), bf16[4,528,256]{2,1,0:T(8,128)(2,1)S(1)}, u32[]{:S(2)}, u32[]{:S(2)}) async-start(bf16[4,528,256]{2,1,0:T(8,128)(2,1)} %broadcast_in_dim.18), calls=%async_computation | async-start | bytes 2162688 | tf_op jit(solution)/shard_map/all_to_all | solution.py:44
  80.5 2.2 %collective-permute-start.10 = (bf16[2,256,384]{2,1,0:T(8,128)(2,1)S(1)}, bf16[2,256,384]{2,1,0:T(8,128)(2,1)S(1)}, u32[]{:S(2)}, u32[]{:S(2)}) collective-permute-start(bf16[2,256,384]{2,1,0:T(8,128)(2,1)S(1)} %pad_maximum_fusion.w0), channel_id=1, source_target_pairs={{0,128},{8,136},{16,144},{24,152},{32,160},{40,168},{48,176},{56,1... | collective-permute-start | bytes 1179656 | tf_op jit(solution)/shard_map/ppermute | solution.py:24
  82.7 4.0 %collective-permute-start.11 = (bf16[2,256,384]{2,1,0:T(8,128)(2,1)S(1)}, bf16[2,256,384]{2,1,0:T(8,128)(2,1)S(1)}, u32[]{:S(2)}, u32[]{:S(2)}) collective-permute-start(bf16[2,256,384]{2,1,0:T(8,128)(2,1)S(1)} %pad_maximum_fusion.w0), channel_id=1, source_target_pairs={{0,384},{8,392},{16,400},{24,408},{32,416},{40,424},{48,432},{56,4... | collective-permute-start | bytes 1179656 | tf_op jit(solution)/shard_map/ppermute | solution.py:24
  86.7 0.1 pad_add_fusion.match
  86.7 5.1 %collective-permute-done.10.w1 = bf16[2,256,384]{2,1,0:T(8,128)(2,1)S(1)} collective-permute-done((bf16[2,256,384]{2,1,0:T(8,128)(2,1)S(1)}, bf16[2,256,384]{2,1,0:T(8,128)(2,1)S(1)}, u32[]{:S(2)}, u32[]{:S(2)}) %collective-permute-start.10) | collective-permute-done | bytes 393248 | tf_op jit(solution)/shard_map/ppermute | solution.py:24
  91.8 3.2 %collective-permute-done.11.w3 = bf16[2,256,384]{2,1,0:T(8,128)(2,1)S(1)} collective-permute-done((bf16[2,256,384]{2,1,0:T(8,128)(2,1)S(1)}, bf16[2,256,384]{2,1,0:T(8,128)(2,1)S(1)}, u32[]{:S(2)}, u32[]{:S(2)}) %collective-permute-start.11) | collective-permute-done | bytes 393248 | tf_op jit(solution)/shard_map/ppermute | solution.py:24
  95.0 0.0 all-to-all-done.far_h
  95.0 0.0 copy-start.2
  95.0 1.0 copy-done.2
  95.9 1.9 %project.1 = (f32[816,128]{1,0:T(8,128)S(1)}, f32[816,128]{1,0:T(8,128)S(1)}) custom-call(s32[4]{0:T(128)S(1)} %pad_add_fusion.match, bf16[528,256]{1,0:T(8,128)(2,1)S(1)} %pad_maximum_fusion.1.t0, bf16[528,256]{1,0:T(8,128)(2,1)S(1)} %collective-permute-done.4.t1, bf16[528,256]{1,0:T(8,128)(2,1)S(1)} %collective-permute-done.5.t2, ...), custom_call_target="tpu_custom_call" | custom-call | flops 830472192 | bytes 3735552 | tf_op jit(solution)/shard_map/project/pallas_call | solution.py:135
  97.8 0.0 copy-start.3
  97.9 0.0 copy-start.4
  97.9 0.0 copy-start.5
  97.9 4.4 %collective-permute-start.12 = (f32[816,128]{1,0:T(8,128)S(1)}, f32[816,128]{1,0:T(8,128)S(1)}, u32[]{:S(2)}, u32[]{:S(2)}) collective-permute-start(f32[816,128]{1,0:T(8,128)S(1)} %get-tuple-element.40), channel_id=1, source_target_pairs={{0,8},{8,0},{16,24},{24,16},{32,40},{40,32},{48,56},{56,48},{64,72... | collective-permute-start | bytes 1253384 | tf_op jit(solution)/shard_map/ppermute | solution.py:24
  102.3 1.4 collective-permute-done.12.theirs
  103.7 0.1 merge.1
  103.7 2.3 %collective-permute-start.13 = (f32[672,128]{1,0:T(8,128)S(1)}, f32[672,128]{1,0:T(8,128)S(1)}, u32[]{:S(2)}, u32[]{:S(2)}) collective-permute-start(f32[672,128]{1,0:T(8,128)S(1)} %get-tuple-element.42), channel_id=1, source_target_pairs={{0,16},{8,24},{16,0},{24,8},{32,48},{40,56},{48,32},{56,40},{64,80... | collective-permute-start | bytes 1032200 | tf_op jit(solution)/shard_map/ppermute | solution.py:24
  106.0 8.9 %collective-permute-done.13 = f32[672,128]{1,0:T(8,128)S(1)} collective-permute-done((f32[672,128]{1,0:T(8,128)S(1)}, f32[672,128]{1,0:T(8,128)S(1)}, u32[]{:S(2)}, u32[]{:S(2)}) %collective-permute-start.13) | collective-permute-done | bytes 344096 | tf_op jit(solution)/shard_map/ppermute | solution.py:24
  114.9 0.0 copy-start.6
  114.9 3.1 %collective-permute-start.14 = (bf16[528,128]{1,0:T(8,128)(2,1)S(1)}, bf16[528,128]{1,0:T(8,128)(2,1)S(1)}, u32[]{:S(2)}, u32[]{:S(2)}) collective-permute-start(bf16[528,128]{1,0:T(8,128)(2,1)S(1)} %fusion.mine), channel_id=1, source_target_pairs={{0,8},{8,0},{16,24},{24,16},{32,40},{40,32},{48,56},{56,48},{64,72... | collective-permute-start | bytes 405512 | tf_op jit(solution)/shard_map/ppermute | solution.py:24
  118.1 0.0 copy-done.3
  118.1 0.0 copy-done.4
  118.1 0.5 tables.1
  118.6 0.4 collective-permute-done.14.theirs
  119.0 0.0 copy-done.5
  119.0 0.7 drive.1
  119.7 15.0 %all_to_all.15.states = f32[4,16,128]{2,1,0:T(8,128)S(1)} all-to-all(f32[4,16,128]{2,1,0:T(8,128)S(1)} %get-tuple-element.50), channel_id=1, replica_groups={{0,32,64,96},{8,40,72,104},{16,48,80,112},{24,56,88,120},{128,160,192,2..., dimensions={0} | all-to-all | bytes 65536 | tf_op jit(solution)/shard_map/all_to_all | solution.py:44
  134.7 0.6 advance.1
  135.3 3.3 %all-to-all-start.2 = ((f32[4,16,128]{2,1,0:T(8,128)}), f32[4,16,128]{2,1,0:T(8,128)S(1)}, u32[]{:S(2)}, u32[]{:S(2)}) async-start(f32[4,16,128]{2,1,0:T(8,128)} %get-tuple-element.55), calls=%async_computation.2 | async-start | bytes 65536 | tf_op jit(solution)/shard_map/all_to_all | solution.py:44
  138.6 0.0 copy-done.6
  138.6 0.3 near.1.inner
  139.0 3.9 %all-to-all-done.2.states = f32[4,16,128]{2,1,0:T(8,128)S(1)} async-done(((f32[4,16,128]{2,1,0:T(8,128)}), f32[4,16,128]{2,1,0:T(8,128)S(1)}, u32[]{:S(2)}, u32[]{:S(2)}) %all-to-all-start.2) | async-done | bytes 32800 | tf_op jit(solution)/shard_map/all_to_all | solution.py:44
  142.9 0.8 finish.1
  (10 shorter events, 0.2 us)
Async XLA Ops:
  0.8 18.8 %collective-permute-start.7 = (bf16[1,128,384]{2,1,0:T(8,128)(2,1)S(1)}, bf16[1,128,384]{2,1,0:T(8,128)(2,1)S(1)}, u32[]{:S(2)}, u32[]{:S(2)}) collective-permute-start(bf16[1,128,384]{2,1,0:T(8,128)(2,1)S(1)} %maximum_bitcast_fusion), channel_id=1, source_target_pairs={{0,64},{8,72},{16,80},{24,88},{32,96},{40,104},{48,112},{56,120},{... | collective-permute-start | bytes 294920 | tf_op jit(solution)/shard_map/ppermute | solution.py:24
  11.2 5.4 %collective-permute-start = (bf16[16,1024]{1,0:T(8,128)(2,1)S(1)}, bf16[16,1024]{1,0:T(8,128)(2,1)S(1)}, u32[]{:S(2)}, u32[]{:S(2)}) collective-permute-start(bf16[16,1024]{1,0:T(8,128)(2,1)S(1)} %slice.32), channel_id=1, source_target_pairs={{0,8},{8,16},{16,24},{24,32},{32,40},{40,48},{48,56},{56,64},{64,7... | collective-permute-start | bytes 98312 | tf_op jit(solution)/shard_map/ppermute | solution.py:29
  16.6 0.9 copy-start
  17.6 7.7 %collective-permute-start.1 = (bf16[2,144,256]{2,1,0:T(8,128)(2,1)S(1)}, bf16[2,144,256]{2,1,0:T(8,128)(2,1)S(1)}, u32[]{:S(2)}, u32[]{:S(2)}) collective-permute-start(bf16[2,144,256]{2,1,0:T(8,128)(2,1)S(1)} %get-tuple-element.31), channel_id=1, source_target_pairs={{0,8},{8,0},{16,24},{24,16},{32,40},{40,32},{48,56},{56,48},{64,72... | collective-permute-start | bytes 442376 | tf_op jit(solution)/shard_map/ppermute | solution.py:24
  19.6 15.1 %collective-permute-start.8 = (bf16[2,128,384]{2,1,0:T(8,128)(2,1)S(1)}, bf16[2,128,384]{2,1,0:T(8,128)(2,1)S(1)}, u32[]{:S(2)}, u32[]{:S(2)}) collective-permute-start(bf16[2,128,384]{2,1,0:T(8,128)(2,1)S(1)} %pad_maximum_fusion.2), channel_id=1, source_target_pairs={{0,32},{8,40},{16,48},{24,56},{32,0},{40,8},{48,16},{56,24},{64,96... | collective-permute-start | bytes 589832 | tf_op jit(solution)/shard_map/ppermute | solution.py:24
  25.4 16.6 %collective-permute-start.2 = (bf16[272,256]{1,0:T(8,128)(2,1)S(1)}, bf16[272,256]{1,0:T(8,128)(2,1)S(1)}, u32[]{:S(2)}, u32[]{:S(2)}) collective-permute-start(bf16[272,256]{1,0:T(8,128)(2,1)S(1)} %select_bitcast_fusion.1), channel_id=1, source_target_pairs={{0,16},{8,24},{16,0},{24,8},{32,48},{40,56},{48,32},{56,40},{64,80... | collective-permute-start | bytes 417800 | tf_op jit(solution)/shard_map/ppermute | solution.py:24
  34.8 41.0 %collective-permute-start.9 = (bf16[2,256,384]{2,1,0:T(8,128)(2,1)S(1)}, bf16[2,256,384]{2,1,0:T(8,128)(2,1)S(1)}, u32[]{:S(2)}, u32[]{:S(2)}) collective-permute-start(bf16[2,256,384]{2,1,0:T(8,128)(2,1)S(1)} %pad_maximum_fusion.w0), channel_id=1, source_target_pairs={{0,256},{8,264},{16,272},{24,280},{32,288},{40,296},{48,304},{56,3... | collective-permute-start | bytes 1179656 | tf_op jit(solution)/shard_map/ppermute | solution.py:24
  42.2 24.0 %collective-permute-start.3 = (bf16[528,256]{1,0:T(8,128)(2,1)S(1)}, bf16[528,256]{1,0:T(8,128)(2,1)S(1)}, u32[]{:S(2)}, u32[]{:S(2)}) collective-permute-start(bf16[528,256]{1,0:T(8,128)(2,1)S(1)} %pad_maximum_fusion.1.t0), channel_id=1, source_target_pairs={{0,4},{1,5},{2,6},{3,7},{4,0},{5,1},{6,2},{7,3},{8,12},{9,13},{10,... | collective-permute-start | bytes 811016 | tf_op jit(solution)/shard_map/ppermute | solution.py:24
  52.8 13.4 %collective-permute-start.4 = (bf16[528,256]{1,0:T(8,128)(2,1)S(1)}, bf16[528,256]{1,0:T(8,128)(2,1)S(1)}, u32[]{:S(2)}, u32[]{:S(2)}) collective-permute-start(bf16[528,256]{1,0:T(8,128)(2,1)S(1)} %pad_maximum_fusion.1.t0), channel_id=1, source_target_pairs={{0,1},{1,0},{2,3},{3,2},{4,5},{5,4},{6,7},{7,6},{8,9},{9,8},{10,11... | collective-permute-start | bytes 811016 | tf_op jit(solution)/shard_map/ppermute | solution.py:24
  56.0 13.5 %collective-permute-start.5 = (bf16[528,256]{1,0:T(8,128)(2,1)S(1)}, bf16[528,256]{1,0:T(8,128)(2,1)S(1)}, u32[]{:S(2)}, u32[]{:S(2)}) collective-permute-start(bf16[528,256]{1,0:T(8,128)(2,1)S(1)} %pad_maximum_fusion.1.t0), channel_id=1, source_target_pairs={{0,2},{1,3},{2,0},{3,1},{4,6},{5,7},{6,4},{7,5},{8,10},{9,11},{10,... | collective-permute-start | bytes 811016 | tf_op jit(solution)/shard_map/ppermute | solution.py:24
  60.6 15.3 %collective-permute-start.6 = (bf16[528,256]{1,0:T(8,128)(2,1)S(1)}, bf16[528,256]{1,0:T(8,128)(2,1)S(1)}, u32[]{:S(2)}, u32[]{:S(2)}) collective-permute-start(bf16[528,256]{1,0:T(8,128)(2,1)S(1)} %pad_maximum_fusion.1.t0), channel_id=1, source_target_pairs={{0,3},{1,2},{2,1},{3,0},{4,7},{5,6},{6,5},{7,4},{8,11},{9,10},{10,... | collective-permute-start | bytes 811016 | tf_op jit(solution)/shard_map/ppermute | solution.py:24
  75.9 1.1 copy-start.1
  76.9 18.0 %all-to-all-start = ((bf16[4,528,256]{2,1,0:T(8,128)(2,1)}), bf16[4,528,256]{2,1,0:T(8,128)(2,1)S(1)}, u32[]{:S(2)}, u32[]{:S(2)}) async-start(bf16[4,528,256]{2,1,0:T(8,128)(2,1)} %broadcast_in_dim.18), calls=%async_computation | async-start | bytes 2162688 | tf_op jit(solution)/shard_map/all_to_all | solution.py:44
  80.5 11.3 %collective-permute-start.10 = (bf16[2,256,384]{2,1,0:T(8,128)(2,1)S(1)}, bf16[2,256,384]{2,1,0:T(8,128)(2,1)S(1)}, u32[]{:S(2)}, u32[]{:S(2)}) collective-permute-start(bf16[2,256,384]{2,1,0:T(8,128)(2,1)S(1)} %pad_maximum_fusion.w0), channel_id=1, source_target_pairs={{0,128},{8,136},{16,144},{24,152},{32,160},{40,168},{48,176},{56,1... | collective-permute-start | bytes 1179656 | tf_op jit(solution)/shard_map/ppermute | solution.py:24
  82.7 12.3 %collective-permute-start.11 = (bf16[2,256,384]{2,1,0:T(8,128)(2,1)S(1)}, bf16[2,256,384]{2,1,0:T(8,128)(2,1)S(1)}, u32[]{:S(2)}, u32[]{:S(2)}) collective-permute-start(bf16[2,256,384]{2,1,0:T(8,128)(2,1)S(1)} %pad_maximum_fusion.w0), channel_id=1, source_target_pairs={{0,384},{8,392},{16,400},{24,408},{32,416},{40,424},{48,432},{56,4... | collective-permute-start | bytes 1179656 | tf_op jit(solution)/shard_map/ppermute | solution.py:24
  95.0 1.0 copy-start.2
  97.8 20.2 %copy-start.3 = (f32[128,16]{0,1:T(8,128)S(1)}, f32[128,16]{0,1:T(8,128)}, u32[]{:S(2)}) copy-start(f32[128,16]{0,1:T(8,128)} %param.9) | copy-start | bytes 24580
  97.9 20.2 %copy-start.4 = (f32[128,16]{0,1:T(8,128)S(1)}, f32[128,16]{0,1:T(8,128)}, u32[]{:S(2)}) copy-start(f32[128,16]{0,1:T(8,128)} %param.10) | copy-start | bytes 24580
  97.9 21.2 %copy-start.5 = (f32[3,128,3]{1,2,0:T(4,128)S(1)}, f32[3,128,3]{1,2,0:T(4,128)}, u32[]{:S(2)}) copy-start(f32[3,128,3]{1,2,0:T(4,128)} %param.8) | copy-start | bytes 13828
  97.9 5.8 %collective-permute-start.12 = (f32[816,128]{1,0:T(8,128)S(1)}, f32[816,128]{1,0:T(8,128)S(1)}, u32[]{:S(2)}, u32[]{:S(2)}) collective-permute-start(f32[816,128]{1,0:T(8,128)S(1)} %get-tuple-element.40), channel_id=1, source_target_pairs={{0,8},{8,0},{16,24},{24,16},{32,40},{40,32},{48,56},{56,48},{64,72... | collective-permute-start | bytes 1253384 | tf_op jit(solution)/shard_map/ppermute | solution.py:24
  103.7 11.2 %collective-permute-start.13 = (f32[672,128]{1,0:T(8,128)S(1)}, f32[672,128]{1,0:T(8,128)S(1)}, u32[]{:S(2)}, u32[]{:S(2)}) collective-permute-start(f32[672,128]{1,0:T(8,128)S(1)} %get-tuple-element.42), channel_id=1, source_target_pairs={{0,16},{8,24},{16,0},{24,8},{32,48},{40,56},{48,32},{56,40},{64,80... | collective-permute-start | bytes 1032200 | tf_op jit(solution)/shard_map/ppermute | solution.py:24
  114.9 23.7 %copy-start.6 = (f32[128]{0:T(128)S(1)}, f32[128]{0:T(128)}, u32[]{:S(2)}) copy-start(f32[128]{0:T(128)} %param.11) | copy-start | bytes 1540
  114.9 4.1 %collective-permute-start.14 = (bf16[528,128]{1,0:T(8,128)(2,1)S(1)}, bf16[528,128]{1,0:T(8,128)(2,1)S(1)}, u32[]{:S(2)}, u32[]{:S(2)}) collective-permute-start(bf16[528,128]{1,0:T(8,128)(2,1)S(1)} %fusion.mine), channel_id=1, source_target_pairs={{0,8},{8,0},{16,24},{24,16},{32,40},{40,32},{48,56},{56,48},{64,72... | collective-permute-start | bytes 405512 | tf_op jit(solution)/shard_map/ppermute | solution.py:24
  135.3 7.5 %all-to-all-start.2 = ((f32[4,16,128]{2,1,0:T(8,128)}), f32[4,16,128]{2,1,0:T(8,128)S(1)}, u32[]{:S(2)}, u32[]{:S(2)}) async-start(f32[4,16,128]{2,1,0:T(8,128)} %get-tuple-element.55), calls=%async_computation.2 | async-start | bytes 65536 | tf_op jit(solution)/shard_map/all_to_all | solution.py:44

commit v5 on v4

--- a/solution.py
+++ b/solution.py
@@ -45,8 +45,7 @@
 
 
 NEIGHBOURS = [[4 * i + j for j in range(4)] for i in range(16)]
-LINE = [[16 * x + 4 * i + low for i in range(4)] for x in range(4) for low in range(4)]
-ACROSS = [[p + 16 * i for i in range(4)] for p in range(16)]
+GROUPS = [[4 * i + low for i in range(16)] for low in range(4)]
 ROUND = [[0, 1, 2, 3], [4, 5, 6, 7]]
 
 
@@ -101,20 +100,32 @@
     return turns, share(far_h, "tp", ROUND), weights
 
 
-def project_kernel(match, t0, t1, t2, t3, far_h, w0, w1, w2, w3, kept, given, total):
+def project_kernel(match, t0, t1, t2, t3, far_ref, w0, w1, w2, w3, kept, given, total, far_h, landed):
+    bring = pltpu.make_async_copy(far_ref, far_h, landed)
+    bring.start()
     near_h, weights = (t0, t1, t2, t3), (w0, w1, w2, w3)
+
+    def half(case, turn_h):
+        added = jnp.zeros(total.shape, F32)
+        for turn_y in range(4):
+            part = far_h[match[3] ^ turn_y] if turn_h else near_h[turn_y][...]
+            turn_x = case ^ (turn_h << 1 | turn_y >> 1)
+            weight = weights[turn_x][match[1] ^ (turn_y & 1)]
+            added += jnp.dot(part, weight, preferred_element_type=F32)
+        return added
+
     for case in range(4):
 
         @pl.when(match[0] == case)
         def _():
-            added = jnp.zeros(total.shape, F32)
-            for turn in range(8):
-                turn_h, turn_y = turn >> 2, turn & 3
-                part = far_h[match[3] ^ turn_y] if turn_h else near_h[turn_y][...]
-                turn_x = case ^ (turn_h << 1 | turn_y >> 1)
-                weight = weights[turn_x][match[1] ^ (turn_y & 1)]
-                added += jnp.dot(part, weight, preferred_element_type=F32)
-            total[...] = added
+            total[...] = half(case, 0)
+
+    bring.wait()
+    for case in range(4):
+
+        @pl.when(match[0] == case)
+        def _():
+            total[...] += half(case, 1)
 
     for core in range(2):
 
@@ -135,9 +146,13 @@
     return pl.pallas_call(
         project_kernel,
         out_shape=(shape, shape),
-        in_specs=[SMEM] + [VMEM] * 9,
+        in_specs=[SMEM] + [VMEM] * 4 + [pl.BlockSpec(memory_space=pl.ANY)] + [VMEM] * 4,
         out_specs=(VMEM, VMEM),
-        scratch_shapes=[pltpu.VMEM((ROWS, columns), F32)],
+        scratch_shapes=[
+            pltpu.VMEM((ROWS, columns), F32),
+            pltpu.VMEM(far_h.shape, BF16),
+            pltpu.SemaphoreType.DMA(()),
+        ],
         compiler_params=PARAMS,
         cost_estimate=pl.CostEstimate(
             flops=2 * ROWS * 2048 * columns, bytes_accessed=2048 * 2 * (ROWS + columns), transcendentals=0
@@ -148,21 +163,17 @@
 
 def merge_kernel(place, mine, theirs, pair, query, gift):
     pair[...] = mine[:ROWS] + theirs[:ROWS]
-    gift[:ROWS] = pair[...]
     chip = (place[0] >> 1) & 1
-    for out, first, side in ((query, 0, chip), (gift, ROWS, 1 - chip)):
+    for out, side in ((query, chip), (gift, 1 - chip)):
         start = pl.multiple_of(ROWS + PIECE * side, 16)
-        out[first : first + PIECE] = mine[pl.ds(start, PIECE)] + theirs[pl.ds(start, PIECE)]
+        out[...] = mine[pl.ds(start, PIECE)] + theirs[pl.ds(start, PIECE)]
 
 
 def merge(place, mine, theirs):
+    piece = jax.ShapeDtypeStruct((PIECE, BLOCK), F32)
     return pl.pallas_call(
         merge_kernel,
-        out_shape=(
-            jax.ShapeDtypeStruct((ROWS, BLOCK), F32),
-            jax.ShapeDtypeStruct((PIECE, BLOCK), F32),
-            jax.ShapeDtypeStruct((ROWS + PIECE, BLOCK), F32),
-        ),
+        out_shape=(jax.ShapeDtypeStruct((ROWS, BLOCK), F32), piece, piece),
         in_specs=[SMEM, VMEM, VMEM],
         out_specs=(VMEM, VMEM, VMEM),
         compiler_params=PARAMS,
@@ -179,7 +190,7 @@
     )
 
 
-def drive_kernel(place, mine, theirs, own, other, taps, weigh, step, query, driven, before, state, signal):
+def drive_kernel(place, mine, theirs, taps, weigh, step, driven, before, state, signal, total):
     spot = place[0] & 3
     core = place[0] & 1
     first = jnp.where(core == 0, taps[1], taps[2])
@@ -187,7 +198,6 @@
     signal[...] = short(mine[...].astype(F32), first) * short(theirs[...].astype(F32), second)
     start = pl.multiple_of(spot * BLOCK, BLOCK)
     driven[...] = signal[pl.ds(start, BLOCK)]
-    query[...] = short((own[...] + other[...]).astype(BF16).astype(F32), taps[0])
     for r in range(MODES):
         w, decay = weigh[r], step[r : r + 1]
         past = jnp.zeros((1, BLOCK), F32)
@@ -196,29 +206,29 @@
             held = jnp.where(spot == b, past, held)
             past = decay * past + jnp.sum(w * signal[BLOCK * b : BLOCK * b + BLOCK], axis=0, keepdims=True)
         before[r : r + 1] = held
-        for i in range(4):
-            state[i, r : r + 1] = past
-
-
-def drive(place, mine, theirs, own, other, taps, weigh, step):
+        total[r : r + 1] = past
+    for i in range(16):
+        state[i] = total[...]
+
+
+def drive(place, mine, theirs, taps, weigh, step):
     square = jax.ShapeDtypeStruct((BLOCK, BLOCK), F32)
     modes = jax.ShapeDtypeStruct((MODES, BLOCK), F32)
-    copies = jax.ShapeDtypeStruct((4, MODES, BLOCK), F32)
+    copies = jax.ShapeDtypeStruct((16, MODES, BLOCK), F32)
     return pl.pallas_call(
         drive_kernel,
-        out_shape=(square, square, modes, copies),
-        in_specs=[SMEM] + [VMEM] * 7,
-        out_specs=(VMEM,) * 4,
-        scratch_shapes=[pltpu.VMEM((GROUP, BLOCK), F32)],
+        out_shape=(square, modes, copies),
+        in_specs=[SMEM] + [VMEM] * 5,
+        out_specs=(VMEM,) * 3,
+        scratch_shapes=[pltpu.VMEM((GROUP, BLOCK), F32), pltpu.VMEM((MODES, BLOCK), F32)],
         compiler_params=PARAMS,
         name="drive",
-    )(place, mine, theirs, own, other, taps, weigh, step)
-
-
-def tables_kernel(place, residues, rates, weigh, reach, taps, step, toward, whole, last):
+    )(place, mine, theirs, taps, weigh, step)
+
+
+def tables_kernel(place, residues, rates, weigh, reach, taps, step, last):
     at = place[0]
     index = lax.broadcasted_iota(jnp.int32, (BLOCK, BLOCK), 0).astype(F32)
-    line = at & 15
     total = jnp.zeros((BLOCK, BLOCK), F32)
     for r in range(MODES):
         rate = rates[r : r + 1]
@@ -229,11 +239,10 @@
     taps[...] = total
     rate = rates[...]
     step[...] = jnp.exp(-rate * float(BLOCK))
-    for i in range(4):
-        whole[i] = jnp.exp(-rate * float(GROUP * (3 - i)))
-        for out, after in ((toward, line - 4 * (i + 1)), (last, at - 16 * (i + 1))):
-            decay = jnp.exp(-rate * (BLOCK * jnp.maximum(after, 0)).astype(F32))
-            out[i] = jnp.where(after >= 0, decay, 0.0)
+    for i in range(16):
+        after = at - 4 * (i + 1)
+        decay = jnp.exp(-rate * (BLOCK * jnp.maximum(after, 0)).astype(F32))
+        last[i] = jnp.where(after >= 0, decay, 0.0)
 
 
 def tables(place, residues, rates):
@@ -247,38 +256,13 @@
             full(MODES, BLOCK, BLOCK),
             full(BLOCK, BLOCK),
             full(MODES, BLOCK),
-            full(4, MODES, BLOCK),
-            full(4, MODES, BLOCK),
-            full(4, MODES, BLOCK),
+            full(16, MODES, BLOCK),
         ),
         in_specs=[SMEM, VMEM, VMEM],
-        out_specs=(VMEM,) * 7,
+        out_specs=(VMEM,) * 5,
         compiler_params=PARAMS,
         name="tables",
     )(place, residues, rates)
-
-
-def advance_kernel(states, before, toward, whole, out_before, out_state):
-    held, total = before[...], jnp.zeros((MODES, BLOCK), F32)
-    for i in range(4):
-        held = held + toward[i] * states[i]
-        total = total + whole[i] * states[i]
-    out_before[...] = held
-    for i in range(4):
-        out_state[i] = total
-
-
-def advance(states, before, toward, whole):
-    modes = jax.ShapeDtypeStruct((MODES, BLOCK), F32)
-    copies = jax.ShapeDtypeStruct((4, MODES, BLOCK), F32)
-    return pl.pallas_call(
-        advance_kernel,
-        out_shape=(modes, copies),
-        in_specs=[VMEM] * 4,
-        out_specs=(VMEM, VMEM),
-        compiler_params=PARAMS,
-        name="advance",
-    )(states, before, toward, whole)
 
 
 def near_kernel(driven, taps, gain, out, padded):
@@ -308,25 +292,26 @@
     )(driven, taps, gain)
 
 
-def finish_kernel(query, inner, reach, before, states, last, out):
+def finish_kernel(own, other, taps, inner, reach, before, states, last, out):
+    query = short((own[...] + other[...]).astype(BF16).astype(F32), taps[0])
     carry = before[...]
-    for i in range(4):
+    for i in range(16):
         carry = carry + last[i] * states[i]
     conv = inner[...]
     for r in range(MODES):
         conv = conv + reach[r] * carry[r : r + 1]
-    out[...] = (query[...] * conv).T
-
-
-def finish(query, inner, reach, before, states, last):
+    out[...] = (query * conv).T
+
+
+def finish(own, other, taps, inner, reach, before, states, last):
     return pl.pallas_call(
         finish_kernel,
         out_shape=jax.ShapeDtypeStruct((BLOCK, BLOCK), F32),
-        in_specs=[VMEM] * 6,
+        in_specs=[VMEM] * 8,
         out_specs=VMEM,
         compiler_params=PARAMS,
         name="finish",
-    )(query, inner, reach, before, states, last)
+    )(own, other, taps, inner, reach, before, states, last)
 
 
 def body(tokens, in_weight, short_taps, residues, rates, skip_gain):
@@ -337,18 +322,16 @@
     match = jnp.stack([apart >> 1, apart & 1, place & 1, tp & 3])
 
     near_h, far_h, weights = gather(tokens, in_weight, place)
-    weigh, reach, taps, step, toward, whole, last = tables(spot, residues.T, rates.T)
+    weigh, reach, taps, step, last = tables(spot, residues.T, rates.T)
 
     mine, gift = project(match, near_h, far_h, weights)
     pair, own, gift = merge(spot, mine, flip(gift, "ctx", 1))
-    theirs = flip(gift, "ctx", 2)
-    mine = (pair + theirs[:ROWS]).astype(BF16)
-    query, driven, before, state = drive(
-        spot, mine, flip(mine, "ctx", 1), own, theirs[ROWS:], short_taps.transpose(0, 2, 1), weigh, step
-    )
+    mine = (pair + flip(pair, "ctx", 2)).astype(BF16)
+    other = flip(gift, "ctx", 2)
+    short_rows = short_taps.transpose(0, 2, 1)
+    driven, before, state = drive(spot, mine, flip(mine, "ctx", 1), short_rows, weigh, step)
     inner = near(driven, taps, skip_gain[None])
-    before, state = advance(swap(state, "ctx", LINE), before, toward, whole)
-    return finish(query, inner, reach, before, swap(state, "ctx", ACROSS), last)
+    return finish(own, other, short_rows, inner, reach, before, swap(state, "ctx", GROUPS), last)
 
 
 def solution(mesh):

time: 146 us -> 142 us (0.973); the launches traced: 144 us -> 141 us
  blocking collectives: 15 us -> 0 us
  starting transfers between devices: 76.4 us -> 82.8 us
  waiting for transfers between devices: 41.9 us -> 47.6 us
    all_to_all x1 -> x0, blocking collectives: 15 us -> none  [swap(): return lax.all_to_all(x, axis, 0, 0, axis_index_groups=groups)]
    all_to_all x2, starting transfers between devices: 6.78 us -> 11.2 us  [swap(): return lax.all_to_all(x, axis, 0, 0, axis_index_groups=groups)]
    all_to_all x2, waiting for transfers between devices: 3.92 us -> 7.76 us  [swap(): return lax.all_to_all(x, axis, 0, 0, axis_index_groups=groups)]
    ppermute x14 -> x15, waiting for transfers between devices: 36.9 us -> 38.9 us  [flip(): return lax.ppermute(x, axis, [(i, i ^ mask) for i in range(length)])]
    ppermute x14 -> x15, starting transfers between devices: 65.3 us -> 67.2 us  [flip(): return lax.ppermute(x, axis, [(i, i ^ mask) for i in range(length)])]
  transfers between devices with their start and end apart: 17 -> 18, of which waited for: 11 -> 12; matrix products, arithmetic and copies ran while one was open for 1% -> 1% of each run, Pallas kernels for 1% -> 1%
where the time goes in v5:
time: 142 us; the launch traced here: 141 us
  starting transfers between devices  82.8 us (58%)
  waiting for transfers between devices  47.6 us (34%)
  Pallas kernels  5.43 us (4%)
  local copies, waits for them, and re-layouts  4.58 us (3%)
    ppermute x15, starting transfers between devices, flip(): return lax.ppermute(x, axis, [(i, i ^ mask) for i in range(length)])  67.2 us
    ppermute x15, waiting for transfers between devices, flip(): return lax.ppermute(x, axis, [(i, i ^ mask) for i in range(length)])  38.9 us
    all_to_all x2, starting transfers between devices, swap(): return lax.all_to_all(x, axis, 0, 0, axis_index_groups=groups)  11.2 us
    all_to_all x2, waiting for transfers between devices, swap(): return lax.all_to_all(x, axis, 0, 0, axis_index_groups=groups)  7.76 us
    ppermute x1, starting transfers between devices, ahead(): return lax.ppermute(x, axis, [(i, i + by) for i in range(length - by)])  4.37 us
  transfers between devices with their start and end apart: 18, of which 12 were waited for; matrix products, arithmetic and copies ran while one was open for 1% of the time, Pallas kernels for 1%

profile of v5, /device:TPU:1, one launch (start us, length us, event | category | flops | bytes accessed | tf_op | source)
XLA Modules:
  0.0 141.2 jit_solution(8693249466749617)
XLA Ops:
  0.0 0.8 slice_bitcast_fusion.2
  0.8 9.6 %collective-permute-start.7 = (bf16[1,128,384]{2,1,0:T(8,128)(2,1)S(1)}, bf16[1,128,384]{2,1,0:T(8,128)(2,1)S(1)}, u32[]{:S(2)}, u32[]{:S(2)}) collective-permute-start(bf16[1,128,384]{2,1,0:T(8,128)(2,1)S(1)} %maximum_bitcast_fusion), channel_id=1, source_target_pairs={{0,64},{8,72},{16,80},{24,88},{32,96},{40,104},{48,112},{56,120},{... | collective-permute-start | bytes 294920 | tf_op jit(solution)/shard_map/ppermute | solution.py:24
  10.5 0.8 slice.26
  11.2 4.4 %collective-permute-start = (bf16[16,1024]{1,0:T(8,128)(2,1)S(1)}, bf16[16,1024]{1,0:T(8,128)(2,1)S(1)}, u32[]{:S(2)}, u32[]{:S(2)}) collective-permute-start(bf16[16,1024]{1,0:T(8,128)(2,1)S(1)} %slice.26), channel_id=1, source_target_pairs={{0,8},{8,16},{16,24},{24,32},{32,40},{40,48},{48,56},{56,64},{64,7... | collective-permute-start | bytes 98312 | tf_op jit(solution)/shard_map/ppermute | solution.py:29
  15.6 1.0 collective-permute-done.halo
  16.6 0.0 copy-start
  16.6 0.9 copy-done
  17.6 0.1 split.1
  17.6 1.9 %collective-permute-start.1 = (bf16[2,144,256]{2,1,0:T(8,128)(2,1)S(1)}, bf16[2,144,256]{2,1,0:T(8,128)(2,1)S(1)}, u32[]{:S(2)}, u32[]{:S(2)}) collective-permute-start(bf16[2,144,256]{2,1,0:T(8,128)(2,1)S(1)} %get-tuple-element.26), channel_id=1, source_target_pairs={{0,8},{8,0},{16,24},{24,16},{32,40},{40,32},{48,56},{56,48},{64,72... | collective-permute-start | bytes 442376 | tf_op jit(solution)/shard_map/ppermute | solution.py:24
  19.6 0.0 collective-permute-done.7
  19.6 5.7 %collective-permute-start.8 = (bf16[2,128,384]{2,1,0:T(8,128)(2,1)S(1)}, bf16[2,128,384]{2,1,0:T(8,128)(2,1)S(1)}, u32[]{:S(2)}, u32[]{:S(2)}) collective-permute-start(bf16[2,128,384]{2,1,0:T(8,128)(2,1)S(1)} %pad_maximum_fusion.2), channel_id=1, source_target_pairs={{0,32},{8,40},{16,48},{24,56},{32,0},{40,8},{48,16},{56,24},{64,96... | collective-permute-start | bytes 589832 | tf_op jit(solution)/shard_map/ppermute | solution.py:24
  25.3 0.0 collective-permute-done.1
  25.4 4.5 %collective-permute-start.2 = (bf16[272,256]{1,0:T(8,128)(2,1)S(1)}, bf16[272,256]{1,0:T(8,128)(2,1)S(1)}, u32[]{:S(2)}, u32[]{:S(2)}) collective-permute-start(bf16[272,256]{1,0:T(8,128)(2,1)S(1)} %select_bitcast_fusion.1), channel_id=1, source_target_pairs={{0,16},{8,24},{16,0},{24,8},{32,48},{40,56},{48,32},{56,40},{64,80... | collective-permute-start | bytes 417800 | tf_op jit(solution)/shard_map/ppermute | solution.py:24
  30.0 4.8 %collective-permute-done.8 = bf16[2,128,384]{2,1,0:T(8,128)(2,1)S(1)} collective-permute-done((bf16[2,128,384]{2,1,0:T(8,128)(2,1)S(1)}, bf16[2,128,384]{2,1,0:T(8,128)(2,1)S(1)}, u32[]{:S(2)}, u32[]{:S(2)}) %collective-permute-start.8) | collective-permute-done | bytes 196640 | tf_op jit(solution)/shard_map/ppermute | solution.py:24
  34.7 0.1 broadcast_select_fusion.1
  34.8 7.2 %collective-permute-start.9 = (bf16[2,256,384]{2,1,0:T(8,128)(2,1)S(1)}, bf16[2,256,384]{2,1,0:T(8,128)(2,1)S(1)}, u32[]{:S(2)}, u32[]{:S(2)}) collective-permute-start(bf16[2,256,384]{2,1,0:T(8,128)(2,1)S(1)} %pad_maximum_fusion.w0), channel_id=1, source_target_pairs={{0,256},{8,264},{16,272},{24,280},{32,288},{40,296},{48,304},{56,3... | collective-permute-start | bytes 1179656 | tf_op jit(solution)/shard_map/ppermute | solution.py:24
  42.0 0.0 collective-permute-done.2
  42.0 0.1 broadcast_select_fusion.3
  42.2 10.6 %collective-permute-start.3 = (bf16[528,256]{1,0:T(8,128)(2,1)S(1)}, bf16[528,256]{1,0:T(8,128)(2,1)S(1)}, u32[]{:S(2)}, u32[]{:S(2)}) collective-permute-start(bf16[528,256]{1,0:T(8,128)(2,1)S(1)} %pad_maximum_fusion.1.t0), channel_id=1, source_target_pairs={{0,4},{1,5},{2,6},{3,7},{4,0},{5,1},{6,2},{7,3},{8,12},{9,13},{10,... | collective-permute-start | bytes 811016 | tf_op jit(solution)/shard_map/ppermute | solution.py:24
  52.8 3.2 %collective-permute-start.4 = (bf16[528,256]{1,0:T(8,128)(2,1)S(1)}, bf16[528,256]{1,0:T(8,128)(2,1)S(1)}, u32[]{:S(2)}, u32[]{:S(2)}) collective-permute-start(bf16[528,256]{1,0:T(8,128)(2,1)S(1)} %pad_maximum_fusion.1.t0), channel_id=1, source_target_pairs={{0,1},{1,0},{2,3},{3,2},{4,5},{5,4},{6,7},{7,6},{8,9},{9,8},{10,11... | collective-permute-start | bytes 811016 | tf_op jit(solution)/shard_map/ppermute | solution.py:24
  56.0 4.5 %collective-permute-start.5 = (bf16[528,256]{1,0:T(8,128)(2,1)S(1)}, bf16[528,256]{1,0:T(8,128)(2,1)S(1)}, u32[]{:S(2)}, u32[]{:S(2)}) collective-permute-start(bf16[528,256]{1,0:T(8,128)(2,1)S(1)} %pad_maximum_fusion.1.t0), channel_id=1, source_target_pairs={{0,2},{1,3},{2,0},{3,1},{4,6},{5,7},{6,4},{7,5},{8,10},{9,11},{10,... | collective-permute-start | bytes 811016 | tf_op jit(solution)/shard_map/ppermute | solution.py:24
  60.6 1.9 %collective-permute-start.6 = (bf16[528,256]{1,0:T(8,128)(2,1)S(1)}, bf16[528,256]{1,0:T(8,128)(2,1)S(1)}, u32[]{:S(2)}, u32[]{:S(2)}) collective-permute-start(bf16[528,256]{1,0:T(8,128)(2,1)S(1)} %pad_maximum_fusion.1.t0), channel_id=1, source_target_pairs={{0,3},{1,2},{2,1},{3,0},{4,7},{5,6},{6,5},{7,4},{8,11},{9,10},{10,... | collective-permute-start | bytes 811016 | tf_op jit(solution)/shard_map/ppermute | solution.py:24
  62.5 3.7 %collective-permute-done.3 = bf16[528,256]{1,0:T(8,128)(2,1)S(1)} collective-permute-done((bf16[528,256]{1,0:T(8,128)(2,1)S(1)}, bf16[528,256]{1,0:T(8,128)(2,1)S(1)}, u32[]{:S(2)}, u32[]{:S(2)}) %collective-permute-start.3) | collective-permute-done | bytes 270368 | tf_op jit(solution)/shard_map/ppermute | solution.py:24
  66.2 0.0 collective-permute-done.4.t1
  66.2 3.4 %collective-permute-done.5.t2 = bf16[528,256]{1,0:T(8,128)(2,1)S(1)} collective-permute-done((bf16[528,256]{1,0:T(8,128)(2,1)S(1)}, bf16[528,256]{1,0:T(8,128)(2,1)S(1)}, u32[]{:S(2)}, u32[]{:S(2)}) %collective-permute-start.5) | collective-permute-done | bytes 270368 | tf_op jit(solution)/shard_map/ppermute | solution.py:24
  69.5 6.3 %collective-permute-done.6.t3 = bf16[528,256]{1,0:T(8,128)(2,1)S(1)} collective-permute-done((bf16[528,256]{1,0:T(8,128)(2,1)S(1)}, bf16[528,256]{1,0:T(8,128)(2,1)S(1)}, u32[]{:S(2)}, u32[]{:S(2)}) %collective-permute-start.6) | collective-permute-done | bytes 270368 | tf_op jit(solution)/shard_map/ppermute | solution.py:24
  75.9 0.0 copy-start.1
  75.9 0.0 collective-permute-done.9.w2
  75.9 1.1 broadcast_in_dim.18
  76.9 0.0 copy-done.1
  76.9 3.5 %all-to-all-start = ((bf16[4,528,256]{2,1,0:T(8,128)(2,1)}), bf16[4,528,256]{2,1,0:T(8,128)(2,1)S(1)}, u32[]{:S(2)}, u32[]{:S(2)}) async-start(bf16[4,528,256]{2,1,0:T(8,128)(2,1)} %broadcast_in_dim.18), calls=%async_computation | async-start | bytes 2162688 | tf_op jit(solution)/shard_map/all_to_all | solution.py:44
  80.5 2.2 %collective-permute-start.10 = (bf16[2,256,384]{2,1,0:T(8,128)(2,1)S(1)}, bf16[2,256,384]{2,1,0:T(8,128)(2,1)S(1)}, u32[]{:S(2)}, u32[]{:S(2)}) collective-permute-start(bf16[2,256,384]{2,1,0:T(8,128)(2,1)S(1)} %pad_maximum_fusion.w0), channel_id=1, source_target_pairs={{0,128},{8,136},{16,144},{24,152},{32,160},{40,168},{48,176},{56,1... | collective-permute-start | bytes 1179656 | tf_op jit(solution)/shard_map/ppermute | solution.py:24
  82.7 4.0 %collective-permute-start.11 = (bf16[2,256,384]{2,1,0:T(8,128)(2,1)S(1)}, bf16[2,256,384]{2,1,0:T(8,128)(2,1)S(1)}, u32[]{:S(2)}, u32[]{:S(2)}) collective-permute-start(bf16[2,256,384]{2,1,0:T(8,128)(2,1)S(1)} %pad_maximum_fusion.w0), channel_id=1, source_target_pairs={{0,384},{8,392},{16,400},{24,408},{32,416},{40,424},{48,432},{56,4... | collective-permute-start | bytes 1179656 | tf_op jit(solution)/shard_map/ppermute | solution.py:24
  86.7 0.1 pad_add_fusion.match
  86.7 5.1 %collective-permute-done.10.w1 = bf16[2,256,384]{2,1,0:T(8,128)(2,1)S(1)} collective-permute-done((bf16[2,256,384]{2,1,0:T(8,128)(2,1)S(1)}, bf16[2,256,384]{2,1,0:T(8,128)(2,1)S(1)}, u32[]{:S(2)}, u32[]{:S(2)}) %collective-permute-start.10) | collective-permute-done | bytes 393248 | tf_op jit(solution)/shard_map/ppermute | solution.py:24
  91.8 3.2 %collective-permute-done.11.w3 = bf16[2,256,384]{2,1,0:T(8,128)(2,1)S(1)} collective-permute-done((bf16[2,256,384]{2,1,0:T(8,128)(2,1)S(1)}, bf16[2,256,384]{2,1,0:T(8,128)(2,1)S(1)}, u32[]{:S(2)}, u32[]{:S(2)}) %collective-permute-start.11) | collective-permute-done | bytes 393248 | tf_op jit(solution)/shard_map/ppermute | solution.py:24
  95.0 0.0 all-to-all-done.far_ref
  95.0 0.0 copy-start.2
  95.0 1.0 copy-done.2
  95.9 2.2 %project.1 = (f32[816,128]{1,0:T(8,128)S(1)}, f32[816,128]{1,0:T(8,128)S(1)}) custom-call(s32[4]{0:T(128)S(1)} %pad_add_fusion.match, bf16[528,256]{1,0:T(8,128)(2,1)S(1)} %pad_maximum_fusion.1.t0, bf16[528,256]{1,0:T(8,128)(2,1)S(1)} %collective-permute-done.4.t1, bf16[528,256]{1,0:T(8,128)(2,1)S(1)} %collective-permute-done.5.t2, ...), custom_call_target="tpu_custom_call" | custom-call | flops 830472192 | bytes 3735552 | tf_op jit(solution)/shard_map/project/pallas_call | solution.py:146
  98.2 0.0 copy-start.4
  98.2 0.0 copy-start.5
  98.2 0.0 copy-start.3
  98.2 4.4 %collective-permute-start.12 = (f32[816,128]{1,0:T(8,128)S(1)}, f32[816,128]{1,0:T(8,128)S(1)}, u32[]{:S(2)}, u32[]{:S(2)}) collective-permute-start(f32[816,128]{1,0:T(8,128)S(1)} %get-tuple-element.35), channel_id=1, source_target_pairs={{0,8},{8,0},{16,24},{24,16},{32,40},{40,32},{48,56},{56,48},{64,72... | collective-permute-start | bytes 1253384 | tf_op jit(solution)/shard_map/ppermute | solution.py:24
  102.6 1.4 collective-permute-done.12.theirs
  104.0 0.1 merge.1
  104.1 0.0 copy-start.6
  104.1 2.3 %collective-permute-start.14 = (f32[528,128]{1,0:T(8,128)S(1)}, f32[528,128]{1,0:T(8,128)S(1)}, u32[]{:S(2)}, u32[]{:S(2)}) collective-permute-start(f32[528,128]{1,0:T(8,128)S(1)} %get-tuple-element.38), channel_id=1, source_target_pairs={{0,16},{8,24},{16,0},{24,8},{32,48},{40,56},{48,32},{56,40},{64,80... | collective-permute-start | bytes 811016 | tf_op jit(solution)/shard_map/ppermute | solution.py:24
  106.4 7.3 %collective-permute-done.14 = f32[528,128]{1,0:T(8,128)S(1)} collective-permute-done((f32[528,128]{1,0:T(8,128)S(1)}, f32[528,128]{1,0:T(8,128)S(1)}, u32[]{:S(2)}, u32[]{:S(2)}) %collective-permute-start.14) | collective-permute-done | bytes 270368 | tf_op jit(solution)/shard_map/ppermute | solution.py:24
  113.7 3.1 %collective-permute-start.15 = (bf16[528,128]{1,0:T(8,128)(2,1)S(1)}, bf16[528,128]{1,0:T(8,128)(2,1)S(1)}, u32[]{:S(2)}, u32[]{:S(2)}) collective-permute-start(bf16[528,128]{1,0:T(8,128)(2,1)S(1)} %add_convert_fusion.mine), channel_id=1, source_target_pairs={{0,8},{8,0},{16,24},{24,16},{32,40},{40,32},{48,56},{56,48},{64,72... | collective-permute-start | bytes 405512 | tf_op jit(solution)/shard_map/ppermute | solution.py:24
  116.8 0.0 copy-done.4
  116.8 0.0 copy-done.5
  116.8 0.6 tables.1
  117.4 0.4 collective-permute-done.15.theirs
  117.8 0.0 copy-done.3
  117.8 1.3 drive.1
  119.1 7.7 %all-to-all-start.1 = ((f32[16,16,128]{2,1,0:T(8,128)}), f32[16,16,128]{2,1,0:T(8,128)S(1)}, u32[]{:S(2)}, u32[]{:S(2)}) async-start(f32[16,16,128]{2,1,0:T(8,128)} %get-tuple-element.45), calls=%async_computation.1 | async-start | bytes 262144 | tf_op jit(solution)/shard_map/all_to_all | solution.py:44
  126.8 1.9 %collective-permute-start.13 = (f32[144,128]{1,0:T(8,128)S(1)}, f32[144,128]{1,0:T(8,128)S(1)}, u32[]{:S(2)}, u32[]{:S(2)}) collective-permute-start(f32[144,128]{1,0:T(8,128)S(1)} %get-tuple-element.37), channel_id=1, source_target_pairs={{0,16},{8,24},{16,0},{24,8},{32,48},{40,56},{48,32},{56,40},{64,80... | collective-permute-start | bytes 221192 | tf_op jit(solution)/shard_map/ppermute | solution.py:24
  128.7 0.0 copy-done.6
  128.7 0.3 near.1.inner
  129.1 3.5 %collective-permute-done.13.other = f32[144,128]{1,0:T(8,128)S(1)} collective-permute-done((f32[144,128]{1,0:T(8,128)S(1)}, f32[144,128]{1,0:T(8,128)S(1)}, u32[]{:S(2)}, u32[]{:S(2)}) %collective-permute-start.13) | collective-permute-done | bytes 73760 | tf_op jit(solution)/shard_map/ppermute | solution.py:24
  132.6 7.8 %all-to-all-done.1.states = f32[16,16,128]{2,1,0:T(8,128)S(1)} async-done(((f32[16,16,128]{2,1,0:T(8,128)}), f32[16,16,128]{2,1,0:T(8,128)S(1)}, u32[]{:S(2)}, u32[]{:S(2)}) %all-to-all-start.1) | async-done | bytes 131104 | tf_op jit(solution)/shard_map/all_to_all | solution.py:44
  140.3 0.8 finish.1
  (9 shorter events, 0.2 us)
Async XLA Ops:
  0.8 18.8 %collective-permute-start.7 = (bf16[1,128,384]{2,1,0:T(8,128)(2,1)S(1)}, bf16[1,128,384]{2,1,0:T(8,128)(2,1)S(1)}, u32[]{:S(2)}, u32[]{:S(2)}) collective-permute-start(bf16[1,128,384]{2,1,0:T(8,128)(2,1)S(1)} %maximum_bitcast_fusion), channel_id=1, source_target_pairs={{0,64},{8,72},{16,80},{24,88},{32,96},{40,104},{48,112},{56,120},{... | collective-permute-start | bytes 294920 | tf_op jit(solution)/shard_map/ppermute | solution.py:24
  11.2 5.4 %collective-permute-start = (bf16[16,1024]{1,0:T(8,128)(2,1)S(1)}, bf16[16,1024]{1,0:T(8,128)(2,1)S(1)}, u32[]{:S(2)}, u32[]{:S(2)}) collective-permute-start(bf16[16,1024]{1,0:T(8,128)(2,1)S(1)} %slice.26), channel_id=1, source_target_pairs={{0,8},{8,16},{16,24},{24,32},{32,40},{40,48},{48,56},{56,64},{64,7... | collective-permute-start | bytes 98312 | tf_op jit(solution)/shard_map/ppermute | solution.py:29
  16.6 0.9 copy-start
  17.6 7.7 %collective-permute-start.1 = (bf16[2,144,256]{2,1,0:T(8,128)(2,1)S(1)}, bf16[2,144,256]{2,1,0:T(8,128)(2,1)S(1)}, u32[]{:S(2)}, u32[]{:S(2)}) collective-permute-start(bf16[2,144,256]{2,1,0:T(8,128)(2,1)S(1)} %get-tuple-element.26), channel_id=1, source_target_pairs={{0,8},{8,0},{16,24},{24,16},{32,40},{40,32},{48,56},{56,48},{64,72... | collective-permute-start | bytes 442376 | tf_op jit(solution)/shard_map/ppermute | solution.py:24
  19.6 15.1 %collective-permute-start.8 = (bf16[2,128,384]{2,1,0:T(8,128)(2,1)S(1)}, bf16[2,128,384]{2,1,0:T(8,128)(2,1)S(1)}, u32[]{:S(2)}, u32[]{:S(2)}) collective-permute-start(bf16[2,128,384]{2,1,0:T(8,128)(2,1)S(1)} %pad_maximum_fusion.2), channel_id=1, source_target_pairs={{0,32},{8,40},{16,48},{24,56},{32,0},{40,8},{48,16},{56,24},{64,96... | collective-permute-start | bytes 589832 | tf_op jit(solution)/shard_map/ppermute | solution.py:24
  25.4 16.6 %collective-permute-start.2 = (bf16[272,256]{1,0:T(8,128)(2,1)S(1)}, bf16[272,256]{1,0:T(8,128)(2,1)S(1)}, u32[]{:S(2)}, u32[]{:S(2)}) collective-permute-start(bf16[272,256]{1,0:T(8,128)(2,1)S(1)} %select_bitcast_fusion.1), channel_id=1, source_target_pairs={{0,16},{8,24},{16,0},{24,8},{32,48},{40,56},{48,32},{56,40},{64,80... | collective-permute-start | bytes 417800 | tf_op jit(solution)/shard_map/ppermute | solution.py:24
  34.8 41.0 %collective-permute-start.9 = (bf16[2,256,384]{2,1,0:T(8,128)(2,1)S(1)}, bf16[2,256,384]{2,1,0:T(8,128)(2,1)S(1)}, u32[]{:S(2)}, u32[]{:S(2)}) collective-permute-start(bf16[2,256,384]{2,1,0:T(8,128)(2,1)S(1)} %pad_maximum_fusion.w0), channel_id=1, source_target_pairs={{0,256},{8,264},{16,272},{24,280},{32,288},{40,296},{48,304},{56,3... | collective-permute-start | bytes 1179656 | tf_op jit(solution)/shard_map/ppermute | solution.py:24
  42.2 24.0 %collective-permute-start.3 = (bf16[528,256]{1,0:T(8,128)(2,1)S(1)}, bf16[528,256]{1,0:T(8,128)(2,1)S(1)}, u32[]{:S(2)}, u32[]{:S(2)}) collective-permute-start(bf16[528,256]{1,0:T(8,128)(2,1)S(1)} %pad_maximum_fusion.1.t0), channel_id=1, source_target_pairs={{0,4},{1,5},{2,6},{3,7},{4,0},{5,1},{6,2},{7,3},{8,12},{9,13},{10,... | collective-permute-start | bytes 811016 | tf_op jit(solution)/shard_map/ppermute | solution.py:24
  52.8 13.4 %collective-permute-start.4 = (bf16[528,256]{1,0:T(8,128)(2,1)S(1)}, bf16[528,256]{1,0:T(8,128)(2,1)S(1)}, u32[]{:S(2)}, u32[]{:S(2)}) collective-permute-start(bf16[528,256]{1,0:T(8,128)(2,1)S(1)} %pad_maximum_fusion.1.t0), channel_id=1, source_target_pairs={{0,1},{1,0},{2,3},{3,2},{4,5},{5,4},{6,7},{7,6},{8,9},{9,8},{10,11... | collective-permute-start | bytes 811016 | tf_op jit(solution)/shard_map/ppermute | solution.py:24
  56.0 13.5 %collective-permute-start.5 = (bf16[528,256]{1,0:T(8,128)(2,1)S(1)}, bf16[528,256]{1,0:T(8,128)(2,1)S(1)}, u32[]{:S(2)}, u32[]{:S(2)}) collective-permute-start(bf16[528,256]{1,0:T(8,128)(2,1)S(1)} %pad_maximum_fusion.1.t0), channel_id=1, source_target_pairs={{0,2},{1,3},{2,0},{3,1},{4,6},{5,7},{6,4},{7,5},{8,10},{9,11},{10,... | collective-permute-start | bytes 811016 | tf_op jit(solution)/shard_map/ppermute | solution.py:24
  60.6 15.3 %collective-permute-start.6 = (bf16[528,256]{1,0:T(8,128)(2,1)S(1)}, bf16[528,256]{1,0:T(8,128)(2,1)S(1)}, u32[]{:S(2)}, u32[]{:S(2)}) collective-permute-start(bf16[528,256]{1,0:T(8,128)(2,1)S(1)} %pad_maximum_fusion.1.t0), channel_id=1, source_target_pairs={{0,3},{1,2},{2,1},{3,0},{4,7},{5,6},{6,5},{7,4},{8,11},{9,10},{10,... | collective-permute-start | bytes 811016 | tf_op jit(solution)/shard_map/ppermute | solution.py:24
  75.9 1.1 copy-start.1
  76.9 18.0 %all-to-all-start = ((bf16[4,528,256]{2,1,0:T(8,128)(2,1)}), bf16[4,528,256]{2,1,0:T(8,128)(2,1)S(1)}, u32[]{:S(2)}, u32[]{:S(2)}) async-start(bf16[4,528,256]{2,1,0:T(8,128)(2,1)} %broadcast_in_dim.18), calls=%async_computation | async-start | bytes 2162688 | tf_op jit(solution)/shard_map/all_to_all | solution.py:44
  80.5 11.3 %collective-permute-start.10 = (bf16[2,256,384]{2,1,0:T(8,128)(2,1)S(1)}, bf16[2,256,384]{2,1,0:T(8,128)(2,1)S(1)}, u32[]{:S(2)}, u32[]{:S(2)}) collective-permute-start(bf16[2,256,384]{2,1,0:T(8,128)(2,1)S(1)} %pad_maximum_fusion.w0), channel_id=1, source_target_pairs={{0,128},{8,136},{16,144},{24,152},{32,160},{40,168},{48,176},{56,1... | collective-permute-start | bytes 1179656 | tf_op jit(solution)/shard_map/ppermute | solution.py:24
  82.7 12.3 %collective-permute-start.11 = (bf16[2,256,384]{2,1,0:T(8,128)(2,1)S(1)}, bf16[2,256,384]{2,1,0:T(8,128)(2,1)S(1)}, u32[]{:S(2)}, u32[]{:S(2)}) collective-permute-start(bf16[2,256,384]{2,1,0:T(8,128)(2,1)S(1)} %pad_maximum_fusion.w0), channel_id=1, source_target_pairs={{0,384},{8,392},{16,400},{24,408},{32,416},{40,424},{48,432},{56,4... | collective-permute-start | bytes 1179656 | tf_op jit(solution)/shard_map/ppermute | solution.py:24
  95.0 1.0 copy-start.2
  98.2 18.6 %copy-start.4 = (f32[128,16]{0,1:T(8,128)S(1)}, f32[128,16]{0,1:T(8,128)}, u32[]{:S(2)}) copy-start(f32[128,16]{0,1:T(8,128)} %param.9) | copy-start | bytes 24580
  98.2 18.6 %copy-start.5 = (f32[128,16]{0,1:T(8,128)S(1)}, f32[128,16]{0,1:T(8,128)}, u32[]{:S(2)}) copy-start(f32[128,16]{0,1:T(8,128)} %param.10) | copy-start | bytes 24580
  98.2 19.6 %copy-start.3 = (f32[3,128,3]{1,2,0:T(4,128)S(1)}, f32[3,128,3]{1,2,0:T(4,128)}, u32[]{:S(2)}) copy-start(f32[3,128,3]{1,2,0:T(4,128)} %param.8) | copy-start | bytes 13828
  98.2 5.8 %collective-permute-start.12 = (f32[816,128]{1,0:T(8,128)S(1)}, f32[816,128]{1,0:T(8,128)S(1)}, u32[]{:S(2)}, u32[]{:S(2)}) collective-permute-start(f32[816,128]{1,0:T(8,128)S(1)} %get-tuple-element.35), channel_id=1, source_target_pairs={{0,8},{8,0},{16,24},{24,16},{32,40},{40,32},{48,56},{56,48},{64,72... | collective-permute-start | bytes 1253384 | tf_op jit(solution)/shard_map/ppermute | solution.py:24
  104.1 24.7 %copy-start.6 = (f32[128]{0:T(128)S(1)}, f32[128]{0:T(128)}, u32[]{:S(2)}) copy-start(f32[128]{0:T(128)} %param.11) | copy-start | bytes 1540
  104.1 9.6 %collective-permute-start.14 = (f32[528,128]{1,0:T(8,128)S(1)}, f32[528,128]{1,0:T(8,128)S(1)}, u32[]{:S(2)}, u32[]{:S(2)}) collective-permute-start(f32[528,128]{1,0:T(8,128)S(1)} %get-tuple-element.38), channel_id=1, source_target_pairs={{0,16},{8,24},{16,0},{24,8},{32,48},{40,56},{48,32},{56,40},{64,80... | collective-permute-start | bytes 811016 | tf_op jit(solution)/shard_map/ppermute | solution.py:24
  113.7 4.1 %collective-permute-start.15 = (bf16[528,128]{1,0:T(8,128)(2,1)S(1)}, bf16[528,128]{1,0:T(8,128)(2,1)S(1)}, u32[]{:S(2)}, u32[]{:S(2)}) collective-permute-start(bf16[528,128]{1,0:T(8,128)(2,1)S(1)} %add_convert_fusion.mine), channel_id=1, source_target_pairs={{0,8},{8,0},{16,24},{24,16},{32,40},{40,32},{48,56},{56,48},{64,72... | collective-permute-start | bytes 405512 | tf_op jit(solution)/shard_map/ppermute | solution.py:24
  119.1 21.2 %all-to-all-start.1 = ((f32[16,16,128]{2,1,0:T(8,128)}), f32[16,16,128]{2,1,0:T(8,128)S(1)}, u32[]{:S(2)}, u32[]{:S(2)}) async-start(f32[16,16,128]{2,1,0:T(8,128)} %get-tuple-element.45), calls=%async_computation.1 | async-start | bytes 262144 | tf_op jit(solution)/shard_map/all_to_all | solution.py:44
  126.8 5.8 %collective-permute-start.13 = (f32[144,128]{1,0:T(8,128)S(1)}, f32[144,128]{1,0:T(8,128)S(1)}, u32[]{:S(2)}, u32[]{:S(2)}) collective-permute-start(f32[144,128]{1,0:T(8,128)S(1)} %get-tuple-element.37), channel_id=1, source_target_pairs={{0,16},{8,24},{16,0},{24,8},{32,48},{40,56},{48,32},{56,40},{64,80... | collective-permute-start | bytes 221192 | tf_op jit(solution)/shard_map/ppermute | solution.py:24

commit v6 on v5

--- a/solution.py
+++ b/solution.py
@@ -96,18 +96,20 @@
     give = jnp.where(upper, both[0], both[1])
     near_h = joined(upper, keep, flip(give, "ctx", 2), 0)
     turns = [near_h] + flip_many(near_h, "tp", (1, 2, 3))
-    far_h, turns, weights[2] = lax.optimization_barrier((flip(near_h, "tp", 4), turns, weights[2]))
+    far_h, turns[:3] = lax.optimization_barrier((flip(near_h, "tp", 4), turns[:3]))
     return turns, share(far_h, "tp", ROUND), weights
 
 
-def project_kernel(match, t0, t1, t2, t3, far_ref, w0, w1, w2, w3, kept, given, total, far_h, landed):
-    bring = pltpu.make_async_copy(far_ref, far_h, landed)
+def project_kernel(match, t0, t1, t2, t3, far_ref, w0, w1, w2, w3, kept, given, total, far_h, t3_here, landed):
+    bring = pltpu.make_async_copy(far_ref, far_h, landed.at[0])
     bring.start()
-    near_h, weights = (t0, t1, t2, t3), (w0, w1, w2, w3)
-
-    def half(case, turn_h):
+    also = pltpu.make_async_copy(t3, t3_here, landed.at[1])
+    also.start()
+    near_h, weights = (t0, t1, t2, t3_here), (w0, w1, w2, w3)
+
+    def some(case, turn_h, turns):
         added = jnp.zeros(total.shape, F32)
-        for turn_y in range(4):
+        for turn_y in turns:
             part = far_h[match[3] ^ turn_y] if turn_h else near_h[turn_y][...]
             turn_x = case ^ (turn_h << 1 | turn_y >> 1)
             weight = weights[turn_x][match[1] ^ (turn_y & 1)]
@@ -118,14 +120,15 @@
 
         @pl.when(match[0] == case)
         def _():
-            total[...] = half(case, 0)
-
+            total[...] = some(case, 0, (0, 1, 2))
+
+    also.wait()
     bring.wait()
     for case in range(4):
 
         @pl.when(match[0] == case)
         def _():
-            total[...] += half(case, 1)
+            total[...] += some(case, 0, (3,)) + some(case, 1, (0, 1, 2, 3))
 
     for core in range(2):
 
@@ -146,12 +149,13 @@
     return pl.pallas_call(
         project_kernel,
         out_shape=(shape, shape),
-        in_specs=[SMEM] + [VMEM] * 4 + [pl.BlockSpec(memory_space=pl.ANY)] + [VMEM] * 4,
+        in_specs=[SMEM] + [VMEM] * 3 + [pl.BlockSpec(memory_space=pl.ANY)] * 2 + [VMEM] * 4,
         out_specs=(VMEM, VMEM),
         scratch_shapes=[
             pltpu.VMEM((ROWS, columns), F32),
             pltpu.VMEM(far_h.shape, BF16),
-            pltpu.SemaphoreType.DMA(()),
+            pltpu.VMEM(far_h.shape[1:], BF16),
+            pltpu.SemaphoreType.DMA((2,)),
         ],
         compiler_params=PARAMS,
         cost_estimate=pl.CostEstimate(

time: 142 us -> 138 us (0.972)
  the two profiles are of different devices: /device:TPU:1 before, /device:TPU:8 now
where the time goes in v6:
time: 138 us; the launch traced here: 137 us
  starting transfers between devices  79 us (57%)
  waiting for transfers between devices  48.8 us (35%)
  Pallas kernels  5.74 us (4%)
  local copies, waits for them, and re-layouts  2.81 us (2%)
    ppermute x15, starting transfers between devices, flip(): return lax.ppermute(x, axis, [(i, i ^ mask) for i in range(length)])  65 us
    ppermute x15, waiting for transfers between devices, flip(): return lax.ppermute(x, axis, [(i, i ^ mask) for i in range(length)])  39.8 us
    all_to_all x2, starting transfers between devices, swap(): return lax.all_to_all(x, axis, 0, 0, axis_index_groups=groups)  12.3 us
    all_to_all x2, waiting for transfers between devices, swap(): return lax.all_to_all(x, axis, 0, 0, axis_index_groups=groups)  8.13 us
  transfers between devices with their start and end apart: 18, of which 11 were waited for; matrix products, arithmetic and copies ran while one was open for 1% of the time, Pallas kernels for 1%

profile of v6, /device:TPU:8, one launch (start us, length us, event | category | flops | bytes accessed | tf_op | source)
XLA Modules:
  0.0 137.2 jit_solution(17082739313941099379)
XLA Ops:
  0.0 0.8 slice.26
  0.8 1.7 %collective-permute-start = (bf16[16,1024]{1,0:T(8,128)(2,1)S(1)}, bf16[16,1024]{1,0:T(8,128)(2,1)S(1)}, u32[]{:S(2)}, u32[]{:S(2)}) collective-permute-start(bf16[16,1024]{1,0:T(8,128)(2,1)S(1)} %slice.26), channel_id=1, source_target_pairs={{0,8},{8,16},{16,24},{24,32},{32,40},{40,48},{48,56},{56,64},{64,7... | collective-permute-start | bytes 98312 | tf_op jit(solution)/shard_map/ppermute | solution.py:29
  2.5 0.8 collective-permute-done.halo
  3.3 0.0 copy-start
  3.3 0.9 copy-done
  4.3 0.0 copy-start.5
  4.3 0.1 split.1
  4.4 4.3 %collective-permute-start.1 = (bf16[2,144,256]{2,1,0:T(8,128)(2,1)S(1)}, bf16[2,144,256]{2,1,0:T(8,128)(2,1)S(1)}, u32[]{:S(2)}, u32[]{:S(2)}) collective-permute-start(bf16[2,144,256]{2,1,0:T(8,128)(2,1)S(1)} %get-tuple-element.24), channel_id=1, source_target_pairs={{0,8},{8,0},{16,24},{24,16},{32,40},{40,32},{48,56},{56,48},{64,72... | collective-permute-start | bytes 442376 | tf_op jit(solution)/shard_map/ppermute | solution.py:24
  8.7 1.0 collective-permute-done.1
  9.7 4.5 %collective-permute-start.2 = (bf16[272,256]{1,0:T(8,128)(2,1)S(1)}, bf16[272,256]{1,0:T(8,128)(2,1)S(1)}, u32[]{:S(2)}, u32[]{:S(2)}) collective-permute-start(bf16[272,256]{1,0:T(8,128)(2,1)S(1)} %select_bitcast_fusion.1), channel_id=1, source_target_pairs={{0,16},{8,24},{16,0},{24,8},{32,48},{40,56},{48,32},{56,40},{64,80... | collective-permute-start | bytes 417800 | tf_op jit(solution)/shard_map/ppermute | solution.py:24
  14.2 0.0 copy-done.5
  14.3 9.1 %collective-permute-start.7 = (bf16[1,128,384]{2,1,0:T(8,128)(2,1)S(1)}, bf16[1,128,384]{2,1,0:T(8,128)(2,1)S(1)}, u32[]{:S(2)}, u32[]{:S(2)}) collective-permute-start(bf16[1,128,384]{2,1,0:T(8,128)(2,1)S(1)} %maximum_bitcast_fusion), channel_id=1, source_target_pairs={{0,64},{8,72},{16,80},{24,88},{32,96},{40,104},{48,112},{56,120},{... | collective-permute-start | bytes 294920 | tf_op jit(solution)/shard_map/ppermute | solution.py:24
  23.4 0.0 collective-permute-done.2
  23.4 0.1 broadcast_select_fusion.3
  23.5 10.2 %collective-permute-start.3 = (bf16[528,256]{1,0:T(8,128)(2,1)S(1)}, bf16[528,256]{1,0:T(8,128)(2,1)S(1)}, u32[]{:S(2)}, u32[]{:S(2)}) collective-permute-start(bf16[528,256]{1,0:T(8,128)(2,1)S(1)} %pad_maximum_fusion.1.t0), channel_id=1, source_target_pairs={{0,4},{1,5},{2,6},{3,7},{4,0},{5,1},{6,2},{7,3},{8,12},{9,13},{10,... | collective-permute-start | bytes 811016 | tf_op jit(solution)/shard_map/ppermute | solution.py:24
  33.7 2.4 %collective-permute-start.4 = (bf16[528,256]{1,0:T(8,128)(2,1)S(1)}, bf16[528,256]{1,0:T(8,128)(2,1)S(1)}, u32[]{:S(2)}, u32[]{:S(2)}) collective-permute-start(bf16[528,256]{1,0:T(8,128)(2,1)S(1)} %pad_maximum_fusion.1.t0), channel_id=1, source_target_pairs={{0,1},{1,0},{2,3},{3,2},{4,5},{5,4},{6,7},{7,6},{8,9},{9,8},{10,11... | collective-permute-start | bytes 811016 | tf_op jit(solution)/shard_map/ppermute | solution.py:24
  36.1 4.5 %collective-permute-start.5 = (bf16[528,256]{1,0:T(8,128)(2,1)S(1)}, bf16[528,256]{1,0:T(8,128)(2,1)S(1)}, u32[]{:S(2)}, u32[]{:S(2)}) collective-permute-start(bf16[528,256]{1,0:T(8,128)(2,1)S(1)} %pad_maximum_fusion.1.t0), channel_id=1, source_target_pairs={{0,2},{1,3},{2,0},{3,1},{4,6},{5,7},{6,4},{7,5},{8,10},{9,11},{10,... | collective-permute-start | bytes 811016 | tf_op jit(solution)/shard_map/ppermute | solution.py:24
  40.6 0.0 collective-permute-done.7
  40.6 6.4 %collective-permute-start.8 = (bf16[2,128,384]{2,1,0:T(8,128)(2,1)S(1)}, bf16[2,128,384]{2,1,0:T(8,128)(2,1)S(1)}, u32[]{:S(2)}, u32[]{:S(2)}) collective-permute-start(bf16[2,128,384]{2,1,0:T(8,128)(2,1)S(1)} %pad_maximum_fusion.2), channel_id=1, source_target_pairs={{0,32},{8,40},{16,48},{24,56},{32,0},{40,8},{48,16},{56,24},{64,96... | collective-permute-start | bytes 589832 | tf_op jit(solution)/shard_map/ppermute | solution.py:24
  47.1 0.0 collective-permute-done.3
  47.1 0.0 collective-permute-done.4.t1
  47.1 3.3 %collective-permute-done.5.t2 = bf16[528,256]{1,0:T(8,128)(2,1)S(1)} collective-permute-done((bf16[528,256]{1,0:T(8,128)(2,1)S(1)}, bf16[528,256]{1,0:T(8,128)(2,1)S(1)}, u32[]{:S(2)}, u32[]{:S(2)}) %collective-permute-start.5) | collective-permute-done | bytes 270368 | tf_op jit(solution)/shard_map/ppermute | solution.py:24
  50.4 1.1 broadcast_in_dim.17
  51.5 5.4 %all-to-all-start = ((bf16[4,528,256]{2,1,0:T(8,128)(2,1)}), bf16[4,528,256]{2,1,0:T(8,128)(2,1)S(1)}, u32[]{:S(2)}, u32[]{:S(2)}) async-start(bf16[4,528,256]{2,1,0:T(8,128)(2,1)} %broadcast_in_dim.17), calls=%async_computation | async-start | bytes 2162688 | tf_op jit(solution)/shard_map/all_to_all | solution.py:44
  56.8 11.8 %collective-permute-done.8 = bf16[2,128,384]{2,1,0:T(8,128)(2,1)S(1)} collective-permute-done((bf16[2,128,384]{2,1,0:T(8,128)(2,1)S(1)}, bf16[2,128,384]{2,1,0:T(8,128)(2,1)S(1)}, u32[]{:S(2)}, u32[]{:S(2)}) %collective-permute-start.8) | collective-permute-done | bytes 196640 | tf_op jit(solution)/shard_map/ppermute | solution.py:24
  68.6 0.1 broadcast_select_fusion.1
  68.7 7.0 %collective-permute-start.10 = (bf16[2,256,384]{2,1,0:T(8,128)(2,1)S(1)}, bf16[2,256,384]{2,1,0:T(8,128)(2,1)S(1)}, u32[]{:S(2)}, u32[]{:S(2)}) collective-permute-start(bf16[2,256,384]{2,1,0:T(8,128)(2,1)S(1)} %pad_maximum_fusion.w0), channel_id=1, source_target_pairs={{0,256},{8,264},{16,272},{24,280},{32,288},{40,296},{48,304},{56,3... | collective-permute-start | bytes 1179656 | tf_op jit(solution)/shard_map/ppermute | solution.py:24
  75.7 2.9 %collective-permute-start.11 = (bf16[2,256,384]{2,1,0:T(8,128)(2,1)S(1)}, bf16[2,256,384]{2,1,0:T(8,128)(2,1)S(1)}, u32[]{:S(2)}, u32[]{:S(2)}) collective-permute-start(bf16[2,256,384]{2,1,0:T(8,128)(2,1)S(1)} %pad_maximum_fusion.w0), channel_id=1, source_target_pairs={{0,384},{8,392},{16,400},{24,408},{32,416},{40,424},{48,432},{56,4... | collective-permute-start | bytes 1179656 | tf_op jit(solution)/shard_map/ppermute | solution.py:24
  78.6 1.9 %collective-permute-start.9 = (bf16[2,256,384]{2,1,0:T(8,128)(2,1)S(1)}, bf16[2,256,384]{2,1,0:T(8,128)(2,1)S(1)}, u32[]{:S(2)}, u32[]{:S(2)}) collective-permute-start(bf16[2,256,384]{2,1,0:T(8,128)(2,1)S(1)} %pad_maximum_fusion.w0), channel_id=1, source_target_pairs={{0,128},{8,136},{16,144},{24,152},{32,160},{40,168},{48,176},{56,1... | collective-permute-start | bytes 1179656 | tf_op jit(solution)/shard_map/ppermute | solution.py:24
  80.5 2.9 %collective-permute-start.6 = (bf16[528,256]{1,0:T(8,128)(2,1)S(1)}, bf16[528,256]{1,0:T(8,128)(2,1)}, u32[]{:S(2)}, u32[]{:S(2)}) collective-permute-start(bf16[528,256]{1,0:T(8,128)(2,1)S(1)} %pad_maximum_fusion.1.t0), channel_id=1, source_target_pairs={{0,3},{1,2},{2,1},{3,0},{4,7},{5,6},{6,5},{7,4},{8,11},{9,10},{10,... | collective-permute-start | bytes 811016 | tf_op jit(solution)/shard_map/ppermute | solution.py:24
  83.5 0.1 pad_add_fusion.match
  83.6 6.8 %collective-permute-done.6.t3 = bf16[528,256]{1,0:T(8,128)(2,1)} collective-permute-done((bf16[528,256]{1,0:T(8,128)(2,1)S(1)}, bf16[528,256]{1,0:T(8,128)(2,1)}, u32[]{:S(2)}, u32[]{:S(2)}) %collective-permute-start.6) | collective-permute-done | bytes 270368 | tf_op jit(solution)/shard_map/ppermute | solution.py:24
  90.4 0.0 collective-permute-done.10.w2
  90.4 3.1 %collective-permute-done.11.w3 = bf16[2,256,384]{2,1,0:T(8,128)(2,1)S(1)} collective-permute-done((bf16[2,256,384]{2,1,0:T(8,128)(2,1)S(1)}, bf16[2,256,384]{2,1,0:T(8,128)(2,1)S(1)}, u32[]{:S(2)}, u32[]{:S(2)}) %collective-permute-start.11) | collective-permute-done | bytes 393248 | tf_op jit(solution)/shard_map/ppermute | solution.py:24
  93.4 0.0 collective-permute-done.9.w1
  93.4 0.0 all-to-all-done.far_ref
  93.4 2.6 %project.1 = (f32[816,128]{1,0:T(8,128)S(1)}, f32[816,128]{1,0:T(8,128)S(1)}) custom-call(s32[4]{0:T(128)S(1)} %pad_add_fusion.match, bf16[528,256]{1,0:T(8,128)(2,1)S(1)} %pad_maximum_fusion.1.t0, bf16[528,256]{1,0:T(8,128)(2,1)S(1)} %collective-permute-done.4.t1, bf16[528,256]{1,0:T(8,128)(2,1)S(1)} %collective-permute-done.5.t2, ...), custom_call_target="tpu_custom_call" | custom-call | flops 830472192 | bytes 3735552 | tf_op jit(solution)/shard_map/project/pallas_call | solution.py:149
  96.0 0.0 copy-start.2
  96.1 0.0 copy-start.3
  96.1 0.0 copy-start.1
  96.1 2.1 %collective-permute-start.12 = (f32[816,128]{1,0:T(8,128)S(1)}, f32[816,128]{1,0:T(8,128)S(1)}, u32[]{:S(2)}, u32[]{:S(2)}) collective-permute-start(f32[816,128]{1,0:T(8,128)S(1)} %get-tuple-element.31), channel_id=1, source_target_pairs={{0,8},{8,0},{16,24},{24,16},{32,40},{40,32},{48,56},{56,48},{64,72... | collective-permute-start | bytes 1253384 | tf_op jit(solution)/shard_map/ppermute | solution.py:24
  98.1 1.7 %collective-permute-done.12.theirs = f32[816,128]{1,0:T(8,128)S(1)} collective-permute-done((f32[816,128]{1,0:T(8,128)S(1)}, f32[816,128]{1,0:T(8,128)S(1)}, u32[]{:S(2)}, u32[]{:S(2)}) %collective-permute-start.12) | collective-permute-done | bytes 417824 | tf_op jit(solution)/shard_map/ppermute | solution.py:24
  99.9 0.0 copy-start.4
  99.9 1.9 %collective-permute-start.14 = (f32[528,128]{1,0:T(8,128)S(1)}, f32[528,128]{1,0:T(8,128)S(1)}, u32[]{:S(2)}, u32[]{:S(2)}) collective-permute-start(f32[528,128]{1,0:T(8,128)S(1)} %get-tuple-element.34), channel_id=1, source_target_pairs={{0,16},{8,24},{16,0},{24,8},{32,48},{40,56},{48,32},{56,40},{64,80... | collective-permute-start | bytes 811016 | tf_op jit(solution)/shard_map/ppermute | solution.py:24
  101.9 8.5 %collective-permute-done.14 = f32[528,128]{1,0:T(8,128)S(1)} collective-permute-done((f32[528,128]{1,0:T(8,128)S(1)}, f32[528,128]{1,0:T(8,128)S(1)}, u32[]{:S(2)}, u32[]{:S(2)}) %collective-permute-start.14) | collective-permute-done | bytes 270368 | tf_op jit(solution)/shard_map/ppermute | solution.py:24
  110.4 1.9 %collective-permute-start.15 = (bf16[528,128]{1,0:T(8,128)(2,1)S(1)}, bf16[528,128]{1,0:T(8,128)(2,1)S(1)}, u32[]{:S(2)}, u32[]{:S(2)}) collective-permute-start(bf16[528,128]{1,0:T(8,128)(2,1)S(1)} %add_convert_fusion.mine), channel_id=1, source_target_pairs={{0,8},{8,0},{16,24},{24,16},{32,40},{40,32},{48,56},{56,48},{64,72... | collective-permute-start | bytes 405512 | tf_op jit(solution)/shard_map/ppermute | solution.py:24
  112.3 0.0 copy-done.2
  112.3 0.0 copy-done.3
  112.3 0.6 tables.1
  112.9 0.7 collective-permute-done.15.theirs
  113.6 0.0 copy-done.1
  113.6 1.3 drive.1
  115.0 7.0 %all-to-all-start.1 = ((f32[16,16,128]{2,1,0:T(8,128)}), f32[16,16,128]{2,1,0:T(8,128)S(1)}, u32[]{:S(2)}, u32[]{:S(2)}) async-start(f32[16,16,128]{2,1,0:T(8,128)} %get-tuple-element.41), calls=%async_computation.1 | async-start | bytes 262144 | tf_op jit(solution)/shard_map/all_to_all | solution.py:44
  121.9 3.0 %collective-permute-start.13 = (f32[144,128]{1,0:T(8,128)S(1)}, f32[144,128]{1,0:T(8,128)S(1)}, u32[]{:S(2)}, u32[]{:S(2)}) collective-permute-start(f32[144,128]{1,0:T(8,128)S(1)} %get-tuple-element.33), channel_id=1, source_target_pairs={{0,16},{8,24},{16,0},{24,8},{32,48},{40,56},{48,32},{56,40},{64,80... | collective-permute-start | bytes 221192 | tf_op jit(solution)/shard_map/ppermute | solution.py:24
  125.0 0.0 copy-done.4
  125.0 0.3 near.1.inner
  125.3 2.9 %collective-permute-done.13.other = f32[144,128]{1,0:T(8,128)S(1)} collective-permute-done((f32[144,128]{1,0:T(8,128)S(1)}, f32[144,128]{1,0:T(8,128)S(1)}, u32[]{:S(2)}, u32[]{:S(2)}) %collective-permute-start.13) | collective-permute-done | bytes 73760 | tf_op jit(solution)/shard_map/ppermute | solution.py:24
  128.2 8.1 %all-to-all-done.1.states = f32[16,16,128]{2,1,0:T(8,128)S(1)} async-done(((f32[16,16,128]{2,1,0:T(8,128)}), f32[16,16,128]{2,1,0:T(8,128)S(1)}, u32[]{:S(2)}, u32[]{:S(2)}) %all-to-all-start.1) | async-done | bytes 131104 | tf_op jit(solution)/shard_map/all_to_all | solution.py:44
  136.3 0.8 finish.1
  (11 shorter events, 0.3 us)
Async XLA Ops:
  0.8 2.6 %collective-permute-start = (bf16[16,1024]{1,0:T(8,128)(2,1)S(1)}, bf16[16,1024]{1,0:T(8,128)(2,1)S(1)}, u32[]{:S(2)}, u32[]{:S(2)}) collective-permute-start(bf16[16,1024]{1,0:T(8,128)(2,1)S(1)} %slice.26), channel_id=1, source_target_pairs={{0,8},{8,16},{16,24},{24,32},{32,40},{40,48},{48,56},{56,64},{64,7... | collective-permute-start | bytes 98312 | tf_op jit(solution)/shard_map/ppermute | solution.py:29
  3.3 0.9 copy-start
  4.3 9.9 %copy-start.5 = (bf16[3,128,128]{2,1,0:T(8,128)(2,1)S(1)}, bf16[3,128,128]{2,1,0:T(8,128)(2,1)}, u32[]{:S(2)}) copy-start(bf16[3,128,128]{2,1,0:T(8,128)(2,1)} %param.7) | copy-start | bytes 294916
  4.4 5.3 %collective-permute-start.1 = (bf16[2,144,256]{2,1,0:T(8,128)(2,1)S(1)}, bf16[2,144,256]{2,1,0:T(8,128)(2,1)S(1)}, u32[]{:S(2)}, u32[]{:S(2)}) collective-permute-start(bf16[2,144,256]{2,1,0:T(8,128)(2,1)S(1)} %get-tuple-element.24), channel_id=1, source_target_pairs={{0,8},{8,0},{16,24},{24,16},{32,40},{40,32},{48,56},{56,48},{64,72... | collective-permute-start | bytes 442376 | tf_op jit(solution)/shard_map/ppermute | solution.py:24
  9.7 13.6 %collective-permute-start.2 = (bf16[272,256]{1,0:T(8,128)(2,1)S(1)}, bf16[272,256]{1,0:T(8,128)(2,1)S(1)}, u32[]{:S(2)}, u32[]{:S(2)}) collective-permute-start(bf16[272,256]{1,0:T(8,128)(2,1)S(1)} %select_bitcast_fusion.1), channel_id=1, source_target_pairs={{0,16},{8,24},{16,0},{24,8},{32,48},{40,56},{48,32},{56,40},{64,80... | collective-permute-start | bytes 417800 | tf_op jit(solution)/shard_map/ppermute | solution.py:24
  14.3 26.3 %collective-permute-start.7 = (bf16[1,128,384]{2,1,0:T(8,128)(2,1)S(1)}, bf16[1,128,384]{2,1,0:T(8,128)(2,1)S(1)}, u32[]{:S(2)}, u32[]{:S(2)}) collective-permute-start(bf16[1,128,384]{2,1,0:T(8,128)(2,1)S(1)} %maximum_bitcast_fusion), channel_id=1, source_target_pairs={{0,64},{8,72},{16,80},{24,88},{32,96},{40,104},{48,112},{56,120},{... | collective-permute-start | bytes 294920 | tf_op jit(solution)/shard_map/ppermute | solution.py:24
  23.5 23.6 %collective-permute-start.3 = (bf16[528,256]{1,0:T(8,128)(2,1)S(1)}, bf16[528,256]{1,0:T(8,128)(2,1)S(1)}, u32[]{:S(2)}, u32[]{:S(2)}) collective-permute-start(bf16[528,256]{1,0:T(8,128)(2,1)S(1)} %pad_maximum_fusion.1.t0), channel_id=1, source_target_pairs={{0,4},{1,5},{2,6},{3,7},{4,0},{5,1},{6,2},{7,3},{8,12},{9,13},{10,... | collective-permute-start | bytes 811016 | tf_op jit(solution)/shard_map/ppermute | solution.py:24
  33.7 13.4 %collective-permute-start.4 = (bf16[528,256]{1,0:T(8,128)(2,1)S(1)}, bf16[528,256]{1,0:T(8,128)(2,1)S(1)}, u32[]{:S(2)}, u32[]{:S(2)}) collective-permute-start(bf16[528,256]{1,0:T(8,128)(2,1)S(1)} %pad_maximum_fusion.1.t0), channel_id=1, source_target_pairs={{0,1},{1,0},{2,3},{3,2},{4,5},{5,4},{6,7},{7,6},{8,9},{9,8},{10,11... | collective-permute-start | bytes 811016 | tf_op jit(solution)/shard_map/ppermute | solution.py:24
  36.1 14.3 %collective-permute-start.5 = (bf16[528,256]{1,0:T(8,128)(2,1)S(1)}, bf16[528,256]{1,0:T(8,128)(2,1)S(1)}, u32[]{:S(2)}, u32[]{:S(2)}) collective-permute-start(bf16[528,256]{1,0:T(8,128)(2,1)S(1)} %pad_maximum_fusion.1.t0), channel_id=1, source_target_pairs={{0,2},{1,3},{2,0},{3,1},{4,6},{5,7},{6,4},{7,5},{8,10},{9,11},{10,... | collective-permute-start | bytes 811016 | tf_op jit(solution)/shard_map/ppermute | solution.py:24
  40.6 28.0 %collective-permute-start.8 = (bf16[2,128,384]{2,1,0:T(8,128)(2,1)S(1)}, bf16[2,128,384]{2,1,0:T(8,128)(2,1)S(1)}, u32[]{:S(2)}, u32[]{:S(2)}) collective-permute-start(bf16[2,128,384]{2,1,0:T(8,128)(2,1)S(1)} %pad_maximum_fusion.2), channel_id=1, source_target_pairs={{0,32},{8,40},{16,48},{24,56},{32,0},{40,8},{48,16},{56,24},{64,96... | collective-permute-start | bytes 589832 | tf_op jit(solution)/shard_map/ppermute | solution.py:24
  51.5 42.0 %all-to-all-start = ((bf16[4,528,256]{2,1,0:T(8,128)(2,1)}), bf16[4,528,256]{2,1,0:T(8,128)(2,1)S(1)}, u32[]{:S(2)}, u32[]{:S(2)}) async-start(bf16[4,528,256]{2,1,0:T(8,128)(2,1)} %broadcast_in_dim.17), calls=%async_computation | async-start | bytes 2162688 | tf_op jit(solution)/shard_map/all_to_all | solution.py:44
  68.7 21.6 %collective-permute-start.10 = (bf16[2,256,384]{2,1,0:T(8,128)(2,1)S(1)}, bf16[2,256,384]{2,1,0:T(8,128)(2,1)S(1)}, u32[]{:S(2)}, u32[]{:S(2)}) collective-permute-start(bf16[2,256,384]{2,1,0:T(8,128)(2,1)S(1)} %pad_maximum_fusion.w0), channel_id=1, source_target_pairs={{0,256},{8,264},{16,272},{24,280},{32,288},{40,296},{48,304},{56,3... | collective-permute-start | bytes 1179656 | tf_op jit(solution)/shard_map/ppermute | solution.py:24
  75.7 17.7 %collective-permute-start.11 = (bf16[2,256,384]{2,1,0:T(8,128)(2,1)S(1)}, bf16[2,256,384]{2,1,0:T(8,128)(2,1)S(1)}, u32[]{:S(2)}, u32[]{:S(2)}) collective-permute-start(bf16[2,256,384]{2,1,0:T(8,128)(2,1)S(1)} %pad_maximum_fusion.w0), channel_id=1, source_target_pairs={{0,384},{8,392},{16,400},{24,408},{32,416},{40,424},{48,432},{56,4... | collective-permute-start | bytes 1179656 | tf_op jit(solution)/shard_map/ppermute | solution.py:24
  78.6 14.8 %collective-permute-start.9 = (bf16[2,256,384]{2,1,0:T(8,128)(2,1)S(1)}, bf16[2,256,384]{2,1,0:T(8,128)(2,1)S(1)}, u32[]{:S(2)}, u32[]{:S(2)}) collective-permute-start(bf16[2,256,384]{2,1,0:T(8,128)(2,1)S(1)} %pad_maximum_fusion.w0), channel_id=1, source_target_pairs={{0,128},{8,136},{16,144},{24,152},{32,160},{40,168},{48,176},{56,1... | collective-permute-start | bytes 1179656 | tf_op jit(solution)/shard_map/ppermute | solution.py:24
  80.5 9.8 %collective-permute-start.6 = (bf16[528,256]{1,0:T(8,128)(2,1)S(1)}, bf16[528,256]{1,0:T(8,128)(2,1)}, u32[]{:S(2)}, u32[]{:S(2)}) collective-permute-start(bf16[528,256]{1,0:T(8,128)(2,1)S(1)} %pad_maximum_fusion.1.t0), channel_id=1, source_target_pairs={{0,3},{1,2},{2,1},{3,0},{4,7},{5,6},{6,5},{7,4},{8,11},{9,10},{10,... | collective-permute-start | bytes 811016 | tf_op jit(solution)/shard_map/ppermute | solution.py:24
  96.0 16.3 %copy-start.2 = (f32[128,16]{0,1:T(8,128)S(1)}, f32[128,16]{0,1:T(8,128)}, u32[]{:S(2)}) copy-start(f32[128,16]{0,1:T(8,128)} %param.9) | copy-start | bytes 24580
  96.1 16.3 %copy-start.3 = (f32[128,16]{0,1:T(8,128)S(1)}, f32[128,16]{0,1:T(8,128)}, u32[]{:S(2)}) copy-start(f32[128,16]{0,1:T(8,128)} %param.10) | copy-start | bytes 24580
  96.1 17.6 %copy-start.1 = (f32[3,128,3]{1,2,0:T(4,128)S(1)}, f32[3,128,3]{1,2,0:T(4,128)}, u32[]{:S(2)}) copy-start(f32[3,128,3]{1,2,0:T(4,128)} %param.8) | copy-start | bytes 13828
  96.1 3.8 %collective-permute-start.12 = (f32[816,128]{1,0:T(8,128)S(1)}, f32[816,128]{1,0:T(8,128)S(1)}, u32[]{:S(2)}, u32[]{:S(2)}) collective-permute-start(f32[816,128]{1,0:T(8,128)S(1)} %get-tuple-element.31), channel_id=1, source_target_pairs={{0,8},{8,0},{16,24},{24,16},{32,40},{40,32},{48,56},{56,48},{64,72... | collective-permute-start | bytes 1253384 | tf_op jit(solution)/shard_map/ppermute | solution.py:24
  99.9 25.1 %copy-start.4 = (f32[128]{0:T(128)S(1)}, f32[128]{0:T(128)}, u32[]{:S(2)}) copy-start(f32[128]{0:T(128)} %param.11) | copy-start | bytes 1540
  99.9 10.4 %collective-permute-start.14 = (f32[528,128]{1,0:T(8,128)S(1)}, f32[528,128]{1,0:T(8,128)S(1)}, u32[]{:S(2)}, u32[]{:S(2)}) collective-permute-start(f32[528,128]{1,0:T(8,128)S(1)} %get-tuple-element.34), channel_id=1, source_target_pairs={{0,16},{8,24},{16,0},{24,8},{32,48},{40,56},{48,32},{56,40},{64,80... | collective-permute-start | bytes 811016 | tf_op jit(solution)/shard_map/ppermute | solution.py:24
  110.4 3.2 %collective-permute-start.15 = (bf16[528,128]{1,0:T(8,128)(2,1)S(1)}, bf16[528,128]{1,0:T(8,128)(2,1)S(1)}, u32[]{:S(2)}, u32[]{:S(2)}) collective-permute-start(bf16[528,128]{1,0:T(8,128)(2,1)S(1)} %add_convert_fusion.mine), channel_id=1, source_target_pairs={{0,8},{8,0},{16,24},{24,16},{32,40},{40,32},{48,56},{56,48},{64,72... | collective-permute-start | bytes 405512 | tf_op jit(solution)/shard_map/ppermute | solution.py:24
  115.0 21.4 %all-to-all-start.1 = ((f32[16,16,128]{2,1,0:T(8,128)}), f32[16,16,128]{2,1,0:T(8,128)S(1)}, u32[]{:S(2)}, u32[]{:S(2)}) async-start(f32[16,16,128]{2,1,0:T(8,128)} %get-tuple-element.41), calls=%async_computation.1 | async-start | bytes 262144 | tf_op jit(solution)/shard_map/all_to_all | solution.py:44
  121.9 6.3 %collective-permute-start.13 = (f32[144,128]{1,0:T(8,128)S(1)}, f32[144,128]{1,0:T(8,128)S(1)}, u32[]{:S(2)}, u32[]{:S(2)}) collective-permute-start(f32[144,128]{1,0:T(8,128)S(1)} %get-tuple-element.33), channel_id=1, source_target_pairs={{0,16},{8,24},{16,0},{24,8},{32,48},{40,56},{48,32},{56,40},{64,80... | collective-permute-start | bytes 221192 | tf_op jit(solution)/shard_map/ppermute | solution.py:24

commit v7 on v6

--- a/solution.py
+++ b/solution.py
@@ -53,27 +53,38 @@
     return [flip(x, axis, m) for m in masks]
 
 
-def split_kernel(place, tokens, halo, kept, given):
+def split_kernel(place, tokens, kept, given):
     core = place[0] & 1
     for out, side in ((kept, core), (given, 1 - core)):
         for bit8 in range(2):
             for bit9 in range(2):
                 start = pl.multiple_of(512 * bit9 + 256 * bit8 + side * 128, 128)
-                there = slice(128 * bit9, 128 * bit9 + 128)
-                out[bit8, :HALO, there] = halo[:, pl.ds(start, 128)]
-                out[bit8, HALO:, there] = tokens[:, pl.ds(start, 128)]
+                out[bit8, :, 128 * bit9 : 128 * bit9 + 128] = tokens[:, pl.ds(start, 128)]
+
+
+def insert_kernel(place, kept_rows, given_rows, halo, kept, given):
+    core = place[0] & 1
+    for out, rows, side in ((kept, kept_rows, core), (given, given_rows, 1 - core)):
+        out[:, HALO:] = rows[...]
+        for bit8 in range(2):
+            for bit9 in range(2):
+                start = pl.multiple_of(512 * bit9 + 256 * bit8 + side * 128, 128)
+                out[bit8, :HALO, 128 * bit9 : 128 * bit9 + 128] = halo[:, pl.ds(start, 128)]
 
 
 def split(place, tokens, halo):
-    shape = jax.ShapeDtypeStruct((2, PIECE, 256), BF16)
-    return pl.pallas_call(
-        split_kernel,
-        out_shape=(shape, shape),
-        in_specs=[SMEM, VMEM, VMEM],
-        out_specs=(VMEM, VMEM),
-        compiler_params=PARAMS,
-        name="split",
-    )(place, tokens, halo)
+    def call(kernel, rows, name, *args):
+        shape = jax.ShapeDtypeStruct((2, rows, 256), BF16)
+        return pl.pallas_call(
+            kernel,
+            out_shape=(shape, shape),
+            in_specs=[SMEM] + [VMEM] * len(args),
+            out_specs=(VMEM, VMEM),
+            compiler_params=PARAMS,
+            name=name,
+        )(place, *args)
+
+    return call(insert_kernel, PIECE, "insert", *call(split_kernel, BLOCK, "split", tokens), halo)
 
 
 def joined(upper, own, other, axis):

time: 138 us -> 137 us (level)
  transfers between devices with their start and end apart: 18 -> 18, of which waited for: 11 -> 10; matrix products, arithmetic and copies ran while one was open for 1% -> 1% of each run, Pallas kernels for 1% -> 1%
where the time goes in v7:
time: 137 us; the launch traced here: 136 us
  starting transfers between devices  79 us (58%)
  waiting for transfers between devices  47.8 us (35%)
  Pallas kernels  5.76 us (4%)
  local copies, waits for them, and re-layouts  2.8 us (2%)
    ppermute x15, starting transfers between devices, flip(): return lax.ppermute(x, axis, [(i, i ^ mask) for i in range(length)])  64.9 us
    ppermute x15, waiting for transfers between devices, flip(): return lax.ppermute(x, axis, [(i, i ^ mask) for i in range(length)])  39.7 us
    all_to_all x2, starting transfers between devices, swap(): return lax.all_to_all(x, axis, 0, 0, axis_index_groups=groups)  12.4 us
    all_to_all x2, waiting for transfers between devices, swap(): return lax.all_to_all(x, axis, 0, 0, axis_index_groups=groups)  8.13 us
  transfers between devices with their start and end apart: 18, of which 10 were waited for; matrix products, arithmetic and copies ran while one was open for 1% of the time, Pallas kernels for 1%

profile of v7, /device:TPU:8, one launch (start us, length us, event | category | flops | bytes accessed | tf_op | source)
XLA Modules:
  0.0 136.2 jit_solution(18054675701770288591)
XLA Ops:
  0.0 0.8 slice.26
  0.8 1.7 %collective-permute-start = (bf16[16,1024]{1,0:T(8,128)(2,1)S(1)}, bf16[16,1024]{1,0:T(8,128)(2,1)S(1)}, u32[]{:S(2)}, u32[]{:S(2)}) collective-permute-start(bf16[16,1024]{1,0:T(8,128)(2,1)S(1)} %slice.26), channel_id=1, source_target_pairs={{0,8},{8,16},{16,24},{24,32},{32,40},{40,48},{48,56},{56,64},{64,7... | collective-permute-start | bytes 98312 | tf_op jit(solution)/shard_map/ppermute | solution.py:29
  2.5 0.0 copy-start
  2.5 0.9 copy-done
  3.5 0.0 copy-start.5
  3.5 0.1 split.1
  3.5 0.0 collective-permute-done.halo
  3.6 4.1 %collective-permute-start.1 = (bf16[2,144,256]{2,1,0:T(8,128)(2,1)S(1)}, bf16[2,144,256]{2,1,0:T(8,128)(2,1)S(1)}, u32[]{:S(2)}, u32[]{:S(2)}) collective-permute-start(bf16[2,144,256]{2,1,0:T(8,128)(2,1)S(1)} %get-tuple-element.28), channel_id=1, source_target_pairs={{0,8},{8,0},{16,24},{24,16},{32,40},{40,32},{48,56},{56,48},{64,72... | collective-permute-start | bytes 442376 | tf_op jit(solution)/shard_map/ppermute | solution.py:24
  7.7 1.0 collective-permute-done.1
  8.8 4.4 %collective-permute-start.2 = (bf16[272,256]{1,0:T(8,128)(2,1)S(1)}, bf16[272,256]{1,0:T(8,128)(2,1)S(1)}, u32[]{:S(2)}, u32[]{:S(2)}) collective-permute-start(bf16[272,256]{1,0:T(8,128)(2,1)S(1)} %select_bitcast_fusion.1), channel_id=1, source_target_pairs={{0,16},{8,24},{16,0},{24,8},{32,48},{40,56},{48,32},{56,40},{64,80... | collective-permute-start | bytes 417800 | tf_op jit(solution)/shard_map/ppermute | solution.py:24
  13.2 0.0 copy-done.5
  13.3 9.1 %collective-permute-start.7 = (bf16[1,128,384]{2,1,0:T(8,128)(2,1)S(1)}, bf16[1,128,384]{2,1,0:T(8,128)(2,1)S(1)}, u32[]{:S(2)}, u32[]{:S(2)}) collective-permute-start(bf16[1,128,384]{2,1,0:T(8,128)(2,1)S(1)} %maximum_bitcast_fusion), channel_id=1, source_target_pairs={{0,64},{8,72},{16,80},{24,88},{32,96},{40,104},{48,112},{56,120},{... | collective-permute-start | bytes 294920 | tf_op jit(solution)/shard_map/ppermute | solution.py:24
  22.4 0.0 collective-permute-done.2
  22.4 0.1 broadcast_select_fusion.3
  22.5 10.2 %collective-permute-start.3 = (bf16[528,256]{1,0:T(8,128)(2,1)S(1)}, bf16[528,256]{1,0:T(8,128)(2,1)S(1)}, u32[]{:S(2)}, u32[]{:S(2)}) collective-permute-start(bf16[528,256]{1,0:T(8,128)(2,1)S(1)} %pad_maximum_fusion.1.t0), channel_id=1, source_target_pairs={{0,4},{1,5},{2,6},{3,7},{4,0},{5,1},{6,2},{7,3},{8,12},{9,13},{10,... | collective-permute-start | bytes 811016 | tf_op jit(solution)/shard_map/ppermute | solution.py:24
  32.7 2.4 %collective-permute-start.4 = (bf16[528,256]{1,0:T(8,128)(2,1)S(1)}, bf16[528,256]{1,0:T(8,128)(2,1)S(1)}, u32[]{:S(2)}, u32[]{:S(2)}) collective-permute-start(bf16[528,256]{1,0:T(8,128)(2,1)S(1)} %pad_maximum_fusion.1.t0), channel_id=1, source_target_pairs={{0,1},{1,0},{2,3},{3,2},{4,5},{5,4},{6,7},{7,6},{8,9},{9,8},{10,11... | collective-permute-start | bytes 811016 | tf_op jit(solution)/shard_map/ppermute | solution.py:24
  35.1 4.5 %collective-permute-start.5 = (bf16[528,256]{1,0:T(8,128)(2,1)S(1)}, bf16[528,256]{1,0:T(8,128)(2,1)S(1)}, u32[]{:S(2)}, u32[]{:S(2)}) collective-permute-start(bf16[528,256]{1,0:T(8,128)(2,1)S(1)} %pad_maximum_fusion.1.t0), channel_id=1, source_target_pairs={{0,2},{1,3},{2,0},{3,1},{4,6},{5,7},{6,4},{7,5},{8,10},{9,11},{10,... | collective-permute-start | bytes 811016 | tf_op jit(solution)/shard_map/ppermute | solution.py:24
  39.6 0.0 collective-permute-done.7
  39.6 6.5 %collective-permute-start.8 = (bf16[2,128,384]{2,1,0:T(8,128)(2,1)S(1)}, bf16[2,128,384]{2,1,0:T(8,128)(2,1)S(1)}, u32[]{:S(2)}, u32[]{:S(2)}) collective-permute-start(bf16[2,128,384]{2,1,0:T(8,128)(2,1)S(1)} %pad_maximum_fusion.2), channel_id=1, source_target_pairs={{0,32},{8,40},{16,48},{24,56},{32,0},{40,8},{48,16},{56,24},{64,96... | collective-permute-start | bytes 589832 | tf_op jit(solution)/shard_map/ppermute | solution.py:24
  46.1 0.0 collective-permute-done.3
  46.1 0.0 collective-permute-done.4.t1
  46.1 3.2 %collective-permute-done.5.t2 = bf16[528,256]{1,0:T(8,128)(2,1)S(1)} collective-permute-done((bf16[528,256]{1,0:T(8,128)(2,1)S(1)}, bf16[528,256]{1,0:T(8,128)(2,1)S(1)}, u32[]{:S(2)}, u32[]{:S(2)}) %collective-permute-start.5) | collective-permute-done | bytes 270368 | tf_op jit(solution)/shard_map/ppermute | solution.py:24
  49.4 1.1 broadcast_in_dim.17
  50.4 5.4 %all-to-all-start = ((bf16[4,528,256]{2,1,0:T(8,128)(2,1)}), bf16[4,528,256]{2,1,0:T(8,128)(2,1)S(1)}, u32[]{:S(2)}, u32[]{:S(2)}) async-start(bf16[4,528,256]{2,1,0:T(8,128)(2,1)} %broadcast_in_dim.17), calls=%async_computation | async-start | bytes 2162688 | tf_op jit(solution)/shard_map/all_to_all | solution.py:44
  55.8 11.8 %collective-permute-done.8 = bf16[2,128,384]{2,1,0:T(8,128)(2,1)S(1)} collective-permute-done((bf16[2,128,384]{2,1,0:T(8,128)(2,1)S(1)}, bf16[2,128,384]{2,1,0:T(8,128)(2,1)S(1)}, u32[]{:S(2)}, u32[]{:S(2)}) %collective-permute-start.8) | collective-permute-done | bytes 196640 | tf_op jit(solution)/shard_map/ppermute | solution.py:24
  67.6 0.1 broadcast_select_fusion.1
  67.7 6.9 %collective-permute-start.10 = (bf16[2,256,384]{2,1,0:T(8,128)(2,1)S(1)}, bf16[2,256,384]{2,1,0:T(8,128)(2,1)S(1)}, u32[]{:S(2)}, u32[]{:S(2)}) collective-permute-start(bf16[2,256,384]{2,1,0:T(8,128)(2,1)S(1)} %pad_maximum_fusion.w0), channel_id=1, source_target_pairs={{0,256},{8,264},{16,272},{24,280},{32,288},{40,296},{48,304},{56,3... | collective-permute-start | bytes 1179656 | tf_op jit(solution)/shard_map/ppermute | solution.py:24
  74.7 2.8 %collective-permute-start.11 = (bf16[2,256,384]{2,1,0:T(8,128)(2,1)S(1)}, bf16[2,256,384]{2,1,0:T(8,128)(2,1)S(1)}, u32[]{:S(2)}, u32[]{:S(2)}) collective-permute-start(bf16[2,256,384]{2,1,0:T(8,128)(2,1)S(1)} %pad_maximum_fusion.w0), channel_id=1, source_target_pairs={{0,384},{8,392},{16,400},{24,408},{32,416},{40,424},{48,432},{56,4... | collective-permute-start | bytes 1179656 | tf_op jit(solution)/shard_map/ppermute | solution.py:24
  77.5 1.9 %collective-permute-start.9 = (bf16[2,256,384]{2,1,0:T(8,128)(2,1)S(1)}, bf16[2,256,384]{2,1,0:T(8,128)(2,1)S(1)}, u32[]{:S(2)}, u32[]{:S(2)}) collective-permute-start(bf16[2,256,384]{2,1,0:T(8,128)(2,1)S(1)} %pad_maximum_fusion.w0), channel_id=1, source_target_pairs={{0,128},{8,136},{16,144},{24,152},{32,160},{40,168},{48,176},{56,1... | collective-permute-start | bytes 1179656 | tf_op jit(solution)/shard_map/ppermute | solution.py:24
  79.5 3.1 %collective-permute-start.6 = (bf16[528,256]{1,0:T(8,128)(2,1)S(1)}, bf16[528,256]{1,0:T(8,128)(2,1)}, u32[]{:S(2)}, u32[]{:S(2)}) collective-permute-start(bf16[528,256]{1,0:T(8,128)(2,1)S(1)} %pad_maximum_fusion.1.t0), channel_id=1, source_target_pairs={{0,3},{1,2},{2,1},{3,0},{4,7},{5,6},{6,5},{7,4},{8,11},{9,10},{10,... | collective-permute-start | bytes 811016 | tf_op jit(solution)/shard_map/ppermute | solution.py:24
  82.5 0.1 pad_add_fusion.match
  82.6 6.7 %collective-permute-done.6.t3 = bf16[528,256]{1,0:T(8,128)(2,1)} collective-permute-done((bf16[528,256]{1,0:T(8,128)(2,1)S(1)}, bf16[528,256]{1,0:T(8,128)(2,1)}, u32[]{:S(2)}, u32[]{:S(2)}) %collective-permute-start.6) | collective-permute-done | bytes 270368 | tf_op jit(solution)/shard_map/ppermute | solution.py:24
  89.3 0.0 collective-permute-done.10.w2
  89.3 3.1 %collective-permute-done.11.w3 = bf16[2,256,384]{2,1,0:T(8,128)(2,1)S(1)} collective-permute-done((bf16[2,256,384]{2,1,0:T(8,128)(2,1)S(1)}, bf16[2,256,384]{2,1,0:T(8,128)(2,1)S(1)}, u32[]{:S(2)}, u32[]{:S(2)}) %collective-permute-start.11) | collective-permute-done | bytes 393248 | tf_op jit(solution)/shard_map/ppermute | solution.py:24
  92.4 0.0 collective-permute-done.9.w1
  92.4 0.0 all-to-all-done.far_ref
  92.4 2.6 %project.1 = (f32[816,128]{1,0:T(8,128)S(1)}, f32[816,128]{1,0:T(8,128)S(1)}) custom-call(s32[4]{0:T(128)S(1)} %pad_add_fusion.match, bf16[528,256]{1,0:T(8,128)(2,1)S(1)} %pad_maximum_fusion.1.t0, bf16[528,256]{1,0:T(8,128)(2,1)S(1)} %collective-permute-done.4.t1, bf16[528,256]{1,0:T(8,128)(2,1)S(1)} %collective-permute-done.5.t2, ...), custom_call_target="tpu_custom_call" | custom-call | flops 830472192 | bytes 3735552 | tf_op jit(solution)/shard_map/project/pallas_call | solution.py:160
  95.0 0.0 copy-start.2
  95.0 0.0 copy-start.3
  95.0 0.0 copy-start.1
  95.0 2.1 %collective-permute-start.12 = (f32[816,128]{1,0:T(8,128)S(1)}, f32[816,128]{1,0:T(8,128)S(1)}, u32[]{:S(2)}, u32[]{:S(2)}) collective-permute-start(f32[816,128]{1,0:T(8,128)S(1)} %get-tuple-element.35), channel_id=1, source_target_pairs={{0,8},{8,0},{16,24},{24,16},{32,40},{40,32},{48,56},{56,48},{64,72... | collective-permute-start | bytes 1253384 | tf_op jit(solution)/shard_map/ppermute | solution.py:24
  97.1 1.7 %collective-permute-done.12.theirs = f32[816,128]{1,0:T(8,128)S(1)} collective-permute-done((f32[816,128]{1,0:T(8,128)S(1)}, f32[816,128]{1,0:T(8,128)S(1)}, u32[]{:S(2)}, u32[]{:S(2)}) %collective-permute-start.12) | collective-permute-done | bytes 417824 | tf_op jit(solution)/shard_map/ppermute | solution.py:24
  98.9 0.0 copy-start.4
  98.9 1.9 %collective-permute-start.14 = (f32[528,128]{1,0:T(8,128)S(1)}, f32[528,128]{1,0:T(8,128)S(1)}, u32[]{:S(2)}, u32[]{:S(2)}) collective-permute-start(f32[528,128]{1,0:T(8,128)S(1)} %get-tuple-element.38), channel_id=1, source_target_pairs={{0,16},{8,24},{16,0},{24,8},{32,48},{40,56},{48,32},{56,40},{64,80... | collective-permute-start | bytes 811016 | tf_op jit(solution)/shard_map/ppermute | solution.py:24
  100.8 8.5 %collective-permute-done.14 = f32[528,128]{1,0:T(8,128)S(1)} collective-permute-done((f32[528,128]{1,0:T(8,128)S(1)}, f32[528,128]{1,0:T(8,128)S(1)}, u32[]{:S(2)}, u32[]{:S(2)}) %collective-permute-start.14) | collective-permute-done | bytes 270368 | tf_op jit(solution)/shard_map/ppermute | solution.py:24
  109.3 1.9 %collective-permute-start.15 = (bf16[528,128]{1,0:T(8,128)(2,1)S(1)}, bf16[528,128]{1,0:T(8,128)(2,1)S(1)}, u32[]{:S(2)}, u32[]{:S(2)}) collective-permute-start(bf16[528,128]{1,0:T(8,128)(2,1)S(1)} %add_convert_fusion.mine), channel_id=1, source_target_pairs={{0,8},{8,0},{16,24},{24,16},{32,40},{40,32},{48,56},{56,48},{64,72... | collective-permute-start | bytes 405512 | tf_op jit(solution)/shard_map/ppermute | solution.py:24
  111.2 0.0 copy-done.2
  111.3 0.0 copy-done.3
  111.3 0.6 tables.1
  111.8 0.7 collective-permute-done.15.theirs
  112.6 0.0 copy-done.1
  112.6 1.3 drive.1
  113.9 7.1 %all-to-all-start.1 = ((f32[16,16,128]{2,1,0:T(8,128)}), f32[16,16,128]{2,1,0:T(8,128)S(1)}, u32[]{:S(2)}, u32[]{:S(2)}) async-start(f32[16,16,128]{2,1,0:T(8,128)} %get-tuple-element.45), calls=%async_computation.1 | async-start | bytes 262144 | tf_op jit(solution)/shard_map/all_to_all | solution.py:44
  121.0 3.0 %collective-permute-start.13 = (f32[144,128]{1,0:T(8,128)S(1)}, f32[144,128]{1,0:T(8,128)S(1)}, u32[]{:S(2)}, u32[]{:S(2)}) collective-permute-start(f32[144,128]{1,0:T(8,128)S(1)} %get-tuple-element.37), channel_id=1, source_target_pairs={{0,16},{8,24},{16,0},{24,8},{32,48},{40,56},{48,32},{56,40},{64,80... | collective-permute-start | bytes 221192 | tf_op jit(solution)/shard_map/ppermute | solution.py:24
  124.0 0.0 copy-done.4
  124.0 0.3 near.1.inner
  124.3 2.9 %collective-permute-done.13.other = f32[144,128]{1,0:T(8,128)S(1)} collective-permute-done((f32[144,128]{1,0:T(8,128)S(1)}, f32[144,128]{1,0:T(8,128)S(1)}, u32[]{:S(2)}, u32[]{:S(2)}) %collective-permute-start.13) | collective-permute-done | bytes 73760 | tf_op jit(solution)/shard_map/ppermute | solution.py:24
  127.3 8.1 %all-to-all-done.1.states = f32[16,16,128]{2,1,0:T(8,128)S(1)} async-done(((f32[16,16,128]{2,1,0:T(8,128)}), f32[16,16,128]{2,1,0:T(8,128)S(1)}, u32[]{:S(2)}, u32[]{:S(2)}) %all-to-all-start.1) | async-done | bytes 131104 | tf_op jit(solution)/shard_map/all_to_all | solution.py:44
  135.4 0.8 finish.1
  (12 shorter events, 0.3 us)
Async XLA Ops:
  0.8 2.8 %collective-permute-start = (bf16[16,1024]{1,0:T(8,128)(2,1)S(1)}, bf16[16,1024]{1,0:T(8,128)(2,1)S(1)}, u32[]{:S(2)}, u32[]{:S(2)}) collective-permute-start(bf16[16,1024]{1,0:T(8,128)(2,1)S(1)} %slice.26), channel_id=1, source_target_pairs={{0,8},{8,16},{16,24},{24,32},{32,40},{40,48},{48,56},{56,64},{64,7... | collective-permute-start | bytes 98312 | tf_op jit(solution)/shard_map/ppermute | solution.py:29
  2.5 1.0 copy-start
  3.5 9.7 %copy-start.5 = (bf16[3,128,128]{2,1,0:T(8,128)(2,1)S(1)}, bf16[3,128,128]{2,1,0:T(8,128)(2,1)}, u32[]{:S(2)}) copy-start(bf16[3,128,128]{2,1,0:T(8,128)(2,1)} %param.7) | copy-start | bytes 294916
  3.6 5.1 %collective-permute-start.1 = (bf16[2,144,256]{2,1,0:T(8,128)(2,1)S(1)}, bf16[2,144,256]{2,1,0:T(8,128)(2,1)S(1)}, u32[]{:S(2)}, u32[]{:S(2)}) collective-permute-start(bf16[2,144,256]{2,1,0:T(8,128)(2,1)S(1)} %get-tuple-element.28), channel_id=1, source_target_pairs={{0,8},{8,0},{16,24},{24,16},{32,40},{40,32},{48,56},{56,48},{64,72... | collective-permute-start | bytes 442376 | tf_op jit(solution)/shard_map/ppermute | solution.py:24
  8.8 13.6 %collective-permute-start.2 = (bf16[272,256]{1,0:T(8,128)(2,1)S(1)}, bf16[272,256]{1,0:T(8,128)(2,1)S(1)}, u32[]{:S(2)}, u32[]{:S(2)}) collective-permute-start(bf16[272,256]{1,0:T(8,128)(2,1)S(1)} %select_bitcast_fusion.1), channel_id=1, source_target_pairs={{0,16},{8,24},{16,0},{24,8},{32,48},{40,56},{48,32},{56,40},{64,80... | collective-permute-start | bytes 417800 | tf_op jit(solution)/shard_map/ppermute | solution.py:24
  13.3 26.3 %collective-permute-start.7 = (bf16[1,128,384]{2,1,0:T(8,128)(2,1)S(1)}, bf16[1,128,384]{2,1,0:T(8,128)(2,1)S(1)}, u32[]{:S(2)}, u32[]{:S(2)}) collective-permute-start(bf16[1,128,384]{2,1,0:T(8,128)(2,1)S(1)} %maximum_bitcast_fusion), channel_id=1, source_target_pairs={{0,64},{8,72},{16,80},{24,88},{32,96},{40,104},{48,112},{56,120},{... | collective-permute-start | bytes 294920 | tf_op jit(solution)/shard_map/ppermute | solution.py:24
  22.5 23.6 %collective-permute-start.3 = (bf16[528,256]{1,0:T(8,128)(2,1)S(1)}, bf16[528,256]{1,0:T(8,128)(2,1)S(1)}, u32[]{:S(2)}, u32[]{:S(2)}) collective-permute-start(bf16[528,256]{1,0:T(8,128)(2,1)S(1)} %pad_maximum_fusion.1.t0), channel_id=1, source_target_pairs={{0,4},{1,5},{2,6},{3,7},{4,0},{5,1},{6,2},{7,3},{8,12},{9,13},{10,... | collective-permute-start | bytes 811016 | tf_op jit(solution)/shard_map/ppermute | solution.py:24
  32.7 13.4 %collective-permute-start.4 = (bf16[528,256]{1,0:T(8,128)(2,1)S(1)}, bf16[528,256]{1,0:T(8,128)(2,1)S(1)}, u32[]{:S(2)}, u32[]{:S(2)}) collective-permute-start(bf16[528,256]{1,0:T(8,128)(2,1)S(1)} %pad_maximum_fusion.1.t0), channel_id=1, source_target_pairs={{0,1},{1,0},{2,3},{3,2},{4,5},{5,4},{6,7},{7,6},{8,9},{9,8},{10,11... | collective-permute-start | bytes 811016 | tf_op jit(solution)/shard_map/ppermute | solution.py:24
  35.1 14.3 %collective-permute-start.5 = (bf16[528,256]{1,0:T(8,128)(2,1)S(1)}, bf16[528,256]{1,0:T(8,128)(2,1)S(1)}, u32[]{:S(2)}, u32[]{:S(2)}) collective-permute-start(bf16[528,256]{1,0:T(8,128)(2,1)S(1)} %pad_maximum_fusion.1.t0), channel_id=1, source_target_pairs={{0,2},{1,3},{2,0},{3,1},{4,6},{5,7},{6,4},{7,5},{8,10},{9,11},{10,... | collective-permute-start | bytes 811016 | tf_op jit(solution)/shard_map/ppermute | solution.py:24
  39.6 28.0 %collective-permute-start.8 = (bf16[2,128,384]{2,1,0:T(8,128)(2,1)S(1)}, bf16[2,128,384]{2,1,0:T(8,128)(2,1)S(1)}, u32[]{:S(2)}, u32[]{:S(2)}) collective-permute-start(bf16[2,128,384]{2,1,0:T(8,128)(2,1)S(1)} %pad_maximum_fusion.2), channel_id=1, source_target_pairs={{0,32},{8,40},{16,48},{24,56},{32,0},{40,8},{48,16},{56,24},{64,96... | collective-permute-start | bytes 589832 | tf_op jit(solution)/shard_map/ppermute | solution.py:24
  50.4 41.9 %all-to-all-start = ((bf16[4,528,256]{2,1,0:T(8,128)(2,1)}), bf16[4,528,256]{2,1,0:T(8,128)(2,1)S(1)}, u32[]{:S(2)}, u32[]{:S(2)}) async-start(bf16[4,528,256]{2,1,0:T(8,128)(2,1)} %broadcast_in_dim.17), calls=%async_computation | async-start | bytes 2162688 | tf_op jit(solution)/shard_map/all_to_all | solution.py:44
  67.7 21.6 %collective-permute-start.10 = (bf16[2,256,384]{2,1,0:T(8,128)(2,1)S(1)}, bf16[2,256,384]{2,1,0:T(8,128)(2,1)S(1)}, u32[]{:S(2)}, u32[]{:S(2)}) collective-permute-start(bf16[2,256,384]{2,1,0:T(8,128)(2,1)S(1)} %pad_maximum_fusion.w0), channel_id=1, source_target_pairs={{0,256},{8,264},{16,272},{24,280},{32,288},{40,296},{48,304},{56,3... | collective-permute-start | bytes 1179656 | tf_op jit(solution)/shard_map/ppermute | solution.py:24
  74.7 17.7 %collective-permute-start.11 = (bf16[2,256,384]{2,1,0:T(8,128)(2,1)S(1)}, bf16[2,256,384]{2,1,0:T(8,128)(2,1)S(1)}, u32[]{:S(2)}, u32[]{:S(2)}) collective-permute-start(bf16[2,256,384]{2,1,0:T(8,128)(2,1)S(1)} %pad_maximum_fusion.w0), channel_id=1, source_target_pairs={{0,384},{8,392},{16,400},{24,408},{32,416},{40,424},{48,432},{56,4... | collective-permute-start | bytes 1179656 | tf_op jit(solution)/shard_map/ppermute | solution.py:24
  77.5 14.9 %collective-permute-start.9 = (bf16[2,256,384]{2,1,0:T(8,128)(2,1)S(1)}, bf16[2,256,384]{2,1,0:T(8,128)(2,1)S(1)}, u32[]{:S(2)}, u32[]{:S(2)}) collective-permute-start(bf16[2,256,384]{2,1,0:T(8,128)(2,1)S(1)} %pad_maximum_fusion.w0), channel_id=1, source_target_pairs={{0,128},{8,136},{16,144},{24,152},{32,160},{40,168},{48,176},{56,1... | collective-permute-start | bytes 1179656 | tf_op jit(solution)/shard_map/ppermute | solution.py:24
  79.5 9.8 %collective-permute-start.6 = (bf16[528,256]{1,0:T(8,128)(2,1)S(1)}, bf16[528,256]{1,0:T(8,128)(2,1)}, u32[]{:S(2)}, u32[]{:S(2)}) collective-permute-start(bf16[528,256]{1,0:T(8,128)(2,1)S(1)} %pad_maximum_fusion.1.t0), channel_id=1, source_target_pairs={{0,3},{1,2},{2,1},{3,0},{4,7},{5,6},{6,5},{7,4},{8,11},{9,10},{10,... | collective-permute-start | bytes 811016 | tf_op jit(solution)/shard_map/ppermute | solution.py:24
  95.0 16.3 %copy-start.2 = (f32[128,16]{0,1:T(8,128)S(1)}, f32[128,16]{0,1:T(8,128)}, u32[]{:S(2)}) copy-start(f32[128,16]{0,1:T(8,128)} %param.9) | copy-start | bytes 24580
  95.0 16.3 %copy-start.3 = (f32[128,16]{0,1:T(8,128)S(1)}, f32[128,16]{0,1:T(8,128)}, u32[]{:S(2)}) copy-start(f32[128,16]{0,1:T(8,128)} %param.10) | copy-start | bytes 24580
  95.0 17.6 %copy-start.1 = (f32[3,128,3]{1,2,0:T(4,128)S(1)}, f32[3,128,3]{1,2,0:T(4,128)}, u32[]{:S(2)}) copy-start(f32[3,128,3]{1,2,0:T(4,128)} %param.8) | copy-start | bytes 13828
  95.0 3.8 %collective-permute-start.12 = (f32[816,128]{1,0:T(8,128)S(1)}, f32[816,128]{1,0:T(8,128)S(1)}, u32[]{:S(2)}, u32[]{:S(2)}) collective-permute-start(f32[816,128]{1,0:T(8,128)S(1)} %get-tuple-element.35), channel_id=1, source_target_pairs={{0,8},{8,0},{16,24},{24,16},{32,40},{40,32},{48,56},{56,48},{64,72... | collective-permute-start | bytes 1253384 | tf_op jit(solution)/shard_map/ppermute | solution.py:24
  98.9 25.1 %copy-start.4 = (f32[128]{0:T(128)S(1)}, f32[128]{0:T(128)}, u32[]{:S(2)}) copy-start(f32[128]{0:T(128)} %param.11) | copy-start | bytes 1540
  98.9 10.4 %collective-permute-start.14 = (f32[528,128]{1,0:T(8,128)S(1)}, f32[528,128]{1,0:T(8,128)S(1)}, u32[]{:S(2)}, u32[]{:S(2)}) collective-permute-start(f32[528,128]{1,0:T(8,128)S(1)} %get-tuple-element.38), channel_id=1, source_target_pairs={{0,16},{8,24},{16,0},{24,8},{32,48},{40,56},{48,32},{56,40},{64,80... | collective-permute-start | bytes 811016 | tf_op jit(solution)/shard_map/ppermute | solution.py:24
  109.3 3.2 %collective-permute-start.15 = (bf16[528,128]{1,0:T(8,128)(2,1)S(1)}, bf16[528,128]{1,0:T(8,128)(2,1)S(1)}, u32[]{:S(2)}, u32[]{:S(2)}) collective-permute-start(bf16[528,128]{1,0:T(8,128)(2,1)S(1)} %add_convert_fusion.mine), channel_id=1, source_target_pairs={{0,8},{8,0},{16,24},{24,16},{32,40},{40,32},{48,56},{56,48},{64,72... | collective-permute-start | bytes 405512 | tf_op jit(solution)/shard_map/ppermute | solution.py:24
  113.9 21.5 %all-to-all-start.1 = ((f32[16,16,128]{2,1,0:T(8,128)}), f32[16,16,128]{2,1,0:T(8,128)S(1)}, u32[]{:S(2)}, u32[]{:S(2)}) async-start(f32[16,16,128]{2,1,0:T(8,128)} %get-tuple-element.45), calls=%async_computation.1 | async-start | bytes 262144 | tf_op jit(solution)/shard_map/all_to_all | solution.py:44
  121.0 6.3 %collective-permute-start.13 = (f32[144,128]{1,0:T(8,128)S(1)}, f32[144,128]{1,0:T(8,128)S(1)}, u32[]{:S(2)}, u32[]{:S(2)}) collective-permute-start(f32[144,128]{1,0:T(8,128)S(1)} %get-tuple-element.37), channel_id=1, source_target_pairs={{0,16},{8,24},{16,0},{24,8},{32,48},{40,56},{48,32},{56,40},{64,80... | collective-permute-start | bytes 221192 | tf_op jit(solution)/shard_map/ppermute | solution.py:24

commit v8 on v7

--- a/solution.py
+++ b/solution.py
@@ -112,16 +112,17 @@
 
 
 def project_kernel(match, t0, t1, t2, t3, far_ref, w0, w1, w2, w3, kept, given, total, far_h, t3_here, landed):
-    bring = pltpu.make_async_copy(far_ref, far_h, landed.at[0])
-    bring.start()
-    also = pltpu.make_async_copy(t3, t3_here, landed.at[1])
+    also = pltpu.make_async_copy(t3, t3_here, landed.at[4])
     also.start()
+    bring = [pltpu.make_async_copy(far_ref.at[match[3] ^ i], far_h.at[i], landed.at[i]) for i in range(4)]
+    for copy in bring:
+        copy.start()
     near_h, weights = (t0, t1, t2, t3_here), (w0, w1, w2, w3)
 
     def some(case, turn_h, turns):
         added = jnp.zeros(total.shape, F32)
         for turn_y in turns:
-            part = far_h[match[3] ^ turn_y] if turn_h else near_h[turn_y][...]
+            part = far_h[turn_y] if turn_h else near_h[turn_y][...]
             turn_x = case ^ (turn_h << 1 | turn_y >> 1)
             weight = weights[turn_x][match[1] ^ (turn_y & 1)]
             added += jnp.dot(part, weight, preferred_element_type=F32)
@@ -134,12 +135,15 @@
             total[...] = some(case, 0, (0, 1, 2))
 
     also.wait()
-    bring.wait()
-    for case in range(4):
-
-        @pl.when(match[0] == case)
-        def _():
-            total[...] += some(case, 0, (3,)) + some(case, 1, (0, 1, 2, 3))
+    for step in range(2):
+        for copy in bring[2 * step : 2 * step + 2]:
+            copy.wait()
+        for case in range(4):
+
+            @pl.when(match[0] == case)
+            def _():
+                added = some(case, 1, (2 * step, 2 * step + 1))
+                total[...] += added if step else added + some(case, 0, (3,))
 
     for core in range(2):
 
@@ -166,7 +170,7 @@
             pltpu.VMEM((ROWS, columns), F32),
             pltpu.VMEM(far_h.shape, BF16),
             pltpu.VMEM(far_h.shape[1:], BF16),
-            pltpu.SemaphoreType.DMA((2,)),
+            pltpu.SemaphoreType.DMA((5,)),
         ],
         compiler_params=PARAMS,
         cost_estimate=pl.CostEstimate(

time: 137 us -> 137 us (level)
  no operation moved by 1% of the time
where the time goes in v8:
time: 137 us; the launch traced here: 136 us
  starting transfers between devices  79 us (58%)
  waiting for transfers between devices  47.8 us (35%)
  Pallas kernels  5.88 us (4%)
  local copies, waits for them, and re-layouts  2.8 us (2%)
    ppermute x15, starting transfers between devices, flip(): return lax.ppermute(x, axis, [(i, i ^ mask) for i in range(length)])  64.9 us
    ppermute x15, waiting for transfers between devices, flip(): return lax.ppermute(x, axis, [(i, i ^ mask) for i in range(length)])  39.7 us
    all_to_all x2, starting transfers between devices, swap(): return lax.all_to_all(x, axis, 0, 0, axis_index_groups=groups)  12.4 us
    all_to_all x2, waiting for transfers between devices, swap(): return lax.all_to_all(x, axis, 0, 0, axis_index_groups=groups)  8.13 us
  transfers between devices with their start and end apart: 18, of which 10 were waited for; matrix products, arithmetic and copies ran while one was open for 1% of the time, Pallas kernels for 1%

profile of v8, /device:TPU:8, one launch (start us, length us, event | category | flops | bytes accessed | tf_op | source)
XLA Modules:
  0.0 136.3 jit_solution(910974400961676511)
XLA Ops:
  0.0 0.8 slice.26
  0.8 1.7 %collective-permute-start = (bf16[16,1024]{1,0:T(8,128)(2,1)S(1)}, bf16[16,1024]{1,0:T(8,128)(2,1)S(1)}, u32[]{:S(2)}, u32[]{:S(2)}) collective-permute-start(bf16[16,1024]{1,0:T(8,128)(2,1)S(1)} %slice.26), channel_id=1, source_target_pairs={{0,8},{8,16},{16,24},{24,32},{32,40},{40,48},{48,56},{56,64},{64,7... | collective-permute-start | bytes 98312 | tf_op jit(solution)/shard_map/ppermute | solution.py:29
  2.5 0.0 copy-start
  2.5 0.9 copy-done
  3.5 0.0 copy-start.5
  3.5 0.1 split.1
  3.5 0.0 collective-permute-done.halo
  3.6 4.1 %collective-permute-start.1 = (bf16[2,144,256]{2,1,0:T(8,128)(2,1)S(1)}, bf16[2,144,256]{2,1,0:T(8,128)(2,1)S(1)}, u32[]{:S(2)}, u32[]{:S(2)}) collective-permute-start(bf16[2,144,256]{2,1,0:T(8,128)(2,1)S(1)} %get-tuple-element.28), channel_id=1, source_target_pairs={{0,8},{8,0},{16,24},{24,16},{32,40},{40,32},{48,56},{56,48},{64,72... | collective-permute-start | bytes 442376 | tf_op jit(solution)/shard_map/ppermute | solution.py:24
  7.7 1.0 collective-permute-done.1
  8.8 4.4 %collective-permute-start.2 = (bf16[272,256]{1,0:T(8,128)(2,1)S(1)}, bf16[272,256]{1,0:T(8,128)(2,1)S(1)}, u32[]{:S(2)}, u32[]{:S(2)}) collective-permute-start(bf16[272,256]{1,0:T(8,128)(2,1)S(1)} %select_bitcast_fusion.1), channel_id=1, source_target_pairs={{0,16},{8,24},{16,0},{24,8},{32,48},{40,56},{48,32},{56,40},{64,80... | collective-permute-start | bytes 417800 | tf_op jit(solution)/shard_map/ppermute | solution.py:24
  13.2 0.0 copy-done.5
  13.3 9.1 %collective-permute-start.7 = (bf16[1,128,384]{2,1,0:T(8,128)(2,1)S(1)}, bf16[1,128,384]{2,1,0:T(8,128)(2,1)S(1)}, u32[]{:S(2)}, u32[]{:S(2)}) collective-permute-start(bf16[1,128,384]{2,1,0:T(8,128)(2,1)S(1)} %maximum_bitcast_fusion), channel_id=1, source_target_pairs={{0,64},{8,72},{16,80},{24,88},{32,96},{40,104},{48,112},{56,120},{... | collective-permute-start | bytes 294920 | tf_op jit(solution)/shard_map/ppermute | solution.py:24
  22.4 0.0 collective-permute-done.2
  22.4 0.1 broadcast_select_fusion.3
  22.5 10.2 %collective-permute-start.3 = (bf16[528,256]{1,0:T(8,128)(2,1)S(1)}, bf16[528,256]{1,0:T(8,128)(2,1)S(1)}, u32[]{:S(2)}, u32[]{:S(2)}) collective-permute-start(bf16[528,256]{1,0:T(8,128)(2,1)S(1)} %pad_maximum_fusion.1.t0), channel_id=1, source_target_pairs={{0,4},{1,5},{2,6},{3,7},{4,0},{5,1},{6,2},{7,3},{8,12},{9,13},{10,... | collective-permute-start | bytes 811016 | tf_op jit(solution)/shard_map/ppermute | solution.py:24
  32.7 2.4 %collective-permute-start.4 = (bf16[528,256]{1,0:T(8,128)(2,1)S(1)}, bf16[528,256]{1,0:T(8,128)(2,1)S(1)}, u32[]{:S(2)}, u32[]{:S(2)}) collective-permute-start(bf16[528,256]{1,0:T(8,128)(2,1)S(1)} %pad_maximum_fusion.1.t0), channel_id=1, source_target_pairs={{0,1},{1,0},{2,3},{3,2},{4,5},{5,4},{6,7},{7,6},{8,9},{9,8},{10,11... | collective-permute-start | bytes 811016 | tf_op jit(solution)/shard_map/ppermute | solution.py:24
  35.1 4.5 %collective-permute-start.5 = (bf16[528,256]{1,0:T(8,128)(2,1)S(1)}, bf16[528,256]{1,0:T(8,128)(2,1)S(1)}, u32[]{:S(2)}, u32[]{:S(2)}) collective-permute-start(bf16[528,256]{1,0:T(8,128)(2,1)S(1)} %pad_maximum_fusion.1.t0), channel_id=1, source_target_pairs={{0,2},{1,3},{2,0},{3,1},{4,6},{5,7},{6,4},{7,5},{8,10},{9,11},{10,... | collective-permute-start | bytes 811016 | tf_op jit(solution)/shard_map/ppermute | solution.py:24
  39.6 0.0 collective-permute-done.7
  39.6 6.5 %collective-permute-start.8 = (bf16[2,128,384]{2,1,0:T(8,128)(2,1)S(1)}, bf16[2,128,384]{2,1,0:T(8,128)(2,1)S(1)}, u32[]{:S(2)}, u32[]{:S(2)}) collective-permute-start(bf16[2,128,384]{2,1,0:T(8,128)(2,1)S(1)} %pad_maximum_fusion.2), channel_id=1, source_target_pairs={{0,32},{8,40},{16,48},{24,56},{32,0},{40,8},{48,16},{56,24},{64,96... | collective-permute-start | bytes 589832 | tf_op jit(solution)/shard_map/ppermute | solution.py:24
  46.1 0.0 collective-permute-done.3
  46.1 0.0 collective-permute-done.4.t1
  46.1 3.2 %collective-permute-done.5.t2 = bf16[528,256]{1,0:T(8,128)(2,1)S(1)} collective-permute-done((bf16[528,256]{1,0:T(8,128)(2,1)S(1)}, bf16[528,256]{1,0:T(8,128)(2,1)S(1)}, u32[]{:S(2)}, u32[]{:S(2)}) %collective-permute-start.5) | collective-permute-done | bytes 270368 | tf_op jit(solution)/shard_map/ppermute | solution.py:24
  49.4 1.1 broadcast_in_dim.17
  50.4 5.4 %all-to-all-start = ((bf16[4,528,256]{2,1,0:T(8,128)(2,1)}), bf16[4,528,256]{2,1,0:T(8,128)(2,1)S(1)}, u32[]{:S(2)}, u32[]{:S(2)}) async-start(bf16[4,528,256]{2,1,0:T(8,128)(2,1)} %broadcast_in_dim.17), calls=%async_computation | async-start | bytes 2162688 | tf_op jit(solution)/shard_map/all_to_all | solution.py:44
  55.8 11.8 %collective-permute-done.8 = bf16[2,128,384]{2,1,0:T(8,128)(2,1)S(1)} collective-permute-done((bf16[2,128,384]{2,1,0:T(8,128)(2,1)S(1)}, bf16[2,128,384]{2,1,0:T(8,128)(2,1)S(1)}, u32[]{:S(2)}, u32[]{:S(2)}) %collective-permute-start.8) | collective-permute-done | bytes 196640 | tf_op jit(solution)/shard_map/ppermute | solution.py:24
  67.6 0.1 broadcast_select_fusion.1
  67.7 6.9 %collective-permute-start.10 = (bf16[2,256,384]{2,1,0:T(8,128)(2,1)S(1)}, bf16[2,256,384]{2,1,0:T(8,128)(2,1)S(1)}, u32[]{:S(2)}, u32[]{:S(2)}) collective-permute-start(bf16[2,256,384]{2,1,0:T(8,128)(2,1)S(1)} %pad_maximum_fusion.w0), channel_id=1, source_target_pairs={{0,256},{8,264},{16,272},{24,280},{32,288},{40,296},{48,304},{56,3... | collective-permute-start | bytes 1179656 | tf_op jit(solution)/shard_map/ppermute | solution.py:24
  74.7 2.8 %collective-permute-start.11 = (bf16[2,256,384]{2,1,0:T(8,128)(2,1)S(1)}, bf16[2,256,384]{2,1,0:T(8,128)(2,1)S(1)}, u32[]{:S(2)}, u32[]{:S(2)}) collective-permute-start(bf16[2,256,384]{2,1,0:T(8,128)(2,1)S(1)} %pad_maximum_fusion.w0), channel_id=1, source_target_pairs={{0,384},{8,392},{16,400},{24,408},{32,416},{40,424},{48,432},{56,4... | collective-permute-start | bytes 1179656 | tf_op jit(solution)/shard_map/ppermute | solution.py:24
  77.5 1.9 %collective-permute-start.9 = (bf16[2,256,384]{2,1,0:T(8,128)(2,1)S(1)}, bf16[2,256,384]{2,1,0:T(8,128)(2,1)S(1)}, u32[]{:S(2)}, u32[]{:S(2)}) collective-permute-start(bf16[2,256,384]{2,1,0:T(8,128)(2,1)S(1)} %pad_maximum_fusion.w0), channel_id=1, source_target_pairs={{0,128},{8,136},{16,144},{24,152},{32,160},{40,168},{48,176},{56,1... | collective-permute-start | bytes 1179656 | tf_op jit(solution)/shard_map/ppermute | solution.py:24
  79.5 3.1 %collective-permute-start.6 = (bf16[528,256]{1,0:T(8,128)(2,1)S(1)}, bf16[528,256]{1,0:T(8,128)(2,1)}, u32[]{:S(2)}, u32[]{:S(2)}) collective-permute-start(bf16[528,256]{1,0:T(8,128)(2,1)S(1)} %pad_maximum_fusion.1.t0), channel_id=1, source_target_pairs={{0,3},{1,2},{2,1},{3,0},{4,7},{5,6},{6,5},{7,4},{8,11},{9,10},{10,... | collective-permute-start | bytes 811016 | tf_op jit(solution)/shard_map/ppermute | solution.py:24
  82.5 0.1 pad_add_fusion.match
  82.6 6.7 %collective-permute-done.6.t3 = bf16[528,256]{1,0:T(8,128)(2,1)} collective-permute-done((bf16[528,256]{1,0:T(8,128)(2,1)S(1)}, bf16[528,256]{1,0:T(8,128)(2,1)}, u32[]{:S(2)}, u32[]{:S(2)}) %collective-permute-start.6) | collective-permute-done | bytes 270368 | tf_op jit(solution)/shard_map/ppermute | solution.py:24
  89.3 0.0 collective-permute-done.10.w2
  89.3 3.1 %collective-permute-done.11.w3 = bf16[2,256,384]{2,1,0:T(8,128)(2,1)S(1)} collective-permute-done((bf16[2,256,384]{2,1,0:T(8,128)(2,1)S(1)}, bf16[2,256,384]{2,1,0:T(8,128)(2,1)S(1)}, u32[]{:S(2)}, u32[]{:S(2)}) %collective-permute-start.11) | collective-permute-done | bytes 393248 | tf_op jit(solution)/shard_map/ppermute | solution.py:24
  92.4 0.0 collective-permute-done.9.w1
  92.4 0.0 all-to-all-done.far_ref
  92.4 2.7 %project.1 = (f32[816,128]{1,0:T(8,128)S(1)}, f32[816,128]{1,0:T(8,128)S(1)}) custom-call(s32[4]{0:T(128)S(1)} %pad_add_fusion.match, bf16[528,256]{1,0:T(8,128)(2,1)S(1)} %pad_maximum_fusion.1.t0, bf16[528,256]{1,0:T(8,128)(2,1)S(1)} %collective-permute-done.4.t1, bf16[528,256]{1,0:T(8,128)(2,1)S(1)} %collective-permute-done.5.t2, ...), custom_call_target="tpu_custom_call" | custom-call | flops 830472192 | bytes 3735552 | tf_op jit(solution)/shard_map/project/pallas_call | solution.py:164
  95.1 0.0 copy-start.2
  95.1 0.0 copy-start.3
  95.1 0.0 copy-start.1
  95.1 2.1 %collective-permute-start.12 = (f32[816,128]{1,0:T(8,128)S(1)}, f32[816,128]{1,0:T(8,128)S(1)}, u32[]{:S(2)}, u32[]{:S(2)}) collective-permute-start(f32[816,128]{1,0:T(8,128)S(1)} %get-tuple-element.35), channel_id=1, source_target_pairs={{0,8},{8,0},{16,24},{24,16},{32,40},{40,32},{48,56},{56,48},{64,72... | collective-permute-start | bytes 1253384 | tf_op jit(solution)/shard_map/ppermute | solution.py:24
  97.2 1.7 %collective-permute-done.12.theirs = f32[816,128]{1,0:T(8,128)S(1)} collective-permute-done((f32[816,128]{1,0:T(8,128)S(1)}, f32[816,128]{1,0:T(8,128)S(1)}, u32[]{:S(2)}, u32[]{:S(2)}) %collective-permute-start.12) | collective-permute-done | bytes 417824 | tf_op jit(solution)/shard_map/ppermute | solution.py:24
  99.0 0.0 copy-start.4
  99.0 1.9 %collective-permute-start.14 = (f32[528,128]{1,0:T(8,128)S(1)}, f32[528,128]{1,0:T(8,128)S(1)}, u32[]{:S(2)}, u32[]{:S(2)}) collective-permute-start(f32[528,128]{1,0:T(8,128)S(1)} %get-tuple-element.38), channel_id=1, source_target_pairs={{0,16},{8,24},{16,0},{24,8},{32,48},{40,56},{48,32},{56,40},{64,80... | collective-permute-start | bytes 811016 | tf_op jit(solution)/shard_map/ppermute | solution.py:24
  100.9 8.5 %collective-permute-done.14 = f32[528,128]{1,0:T(8,128)S(1)} collective-permute-done((f32[528,128]{1,0:T(8,128)S(1)}, f32[528,128]{1,0:T(8,128)S(1)}, u32[]{:S(2)}, u32[]{:S(2)}) %collective-permute-start.14) | collective-permute-done | bytes 270368 | tf_op jit(solution)/shard_map/ppermute | solution.py:24
  109.4 1.9 %collective-permute-start.15 = (bf16[528,128]{1,0:T(8,128)(2,1)S(1)}, bf16[528,128]{1,0:T(8,128)(2,1)S(1)}, u32[]{:S(2)}, u32[]{:S(2)}) collective-permute-start(bf16[528,128]{1,0:T(8,128)(2,1)S(1)} %add_convert_fusion.mine), channel_id=1, source_target_pairs={{0,8},{8,0},{16,24},{24,16},{32,40},{40,32},{48,56},{56,48},{64,72... | collective-permute-start | bytes 405512 | tf_op jit(solution)/shard_map/ppermute | solution.py:24
  111.4 0.0 copy-done.2
  111.4 0.0 copy-done.3
  111.4 0.6 tables.1
  111.9 0.7 collective-permute-done.15.theirs
  112.7 0.0 copy-done.1
  112.7 1.3 drive.1
  114.0 7.1 %all-to-all-start.1 = ((f32[16,16,128]{2,1,0:T(8,128)}), f32[16,16,128]{2,1,0:T(8,128)S(1)}, u32[]{:S(2)}, u32[]{:S(2)}) async-start(f32[16,16,128]{2,1,0:T(8,128)} %get-tuple-element.45), calls=%async_computation.1 | async-start | bytes 262144 | tf_op jit(solution)/shard_map/all_to_all | solution.py:44
  121.1 3.0 %collective-permute-start.13 = (f32[144,128]{1,0:T(8,128)S(1)}, f32[144,128]{1,0:T(8,128)S(1)}, u32[]{:S(2)}, u32[]{:S(2)}) collective-permute-start(f32[144,128]{1,0:T(8,128)S(1)} %get-tuple-element.37), channel_id=1, source_target_pairs={{0,16},{8,24},{16,0},{24,8},{32,48},{40,56},{48,32},{56,40},{64,80... | collective-permute-start | bytes 221192 | tf_op jit(solution)/shard_map/ppermute | solution.py:24
  124.1 0.0 copy-done.4
  124.1 0.3 near.1.inner
  124.4 2.9 %collective-permute-done.13.other = f32[144,128]{1,0:T(8,128)S(1)} collective-permute-done((f32[144,128]{1,0:T(8,128)S(1)}, f32[144,128]{1,0:T(8,128)S(1)}, u32[]{:S(2)}, u32[]{:S(2)}) %collective-permute-start.13) | collective-permute-done | bytes 73760 | tf_op jit(solution)/shard_map/ppermute | solution.py:24
  127.4 8.1 %all-to-all-done.1.states = f32[16,16,128]{2,1,0:T(8,128)S(1)} async-done(((f32[16,16,128]{2,1,0:T(8,128)}), f32[16,16,128]{2,1,0:T(8,128)S(1)}, u32[]{:S(2)}, u32[]{:S(2)}) %all-to-all-start.1) | async-done | bytes 131104 | tf_op jit(solution)/shard_map/all_to_all | solution.py:44
  135.5 0.8 finish.1
  (12 shorter events, 0.3 us)
Async XLA Ops:
  0.8 2.8 %collective-permute-start = (bf16[16,1024]{1,0:T(8,128)(2,1)S(1)}, bf16[16,1024]{1,0:T(8,128)(2,1)S(1)}, u32[]{:S(2)}, u32[]{:S(2)}) collective-permute-start(bf16[16,1024]{1,0:T(8,128)(2,1)S(1)} %slice.26), channel_id=1, source_target_pairs={{0,8},{8,16},{16,24},{24,32},{32,40},{40,48},{48,56},{56,64},{64,7... | collective-permute-start | bytes 98312 | tf_op jit(solution)/shard_map/ppermute | solution.py:29
  2.5 1.0 copy-start
  3.5 9.7 %copy-start.5 = (bf16[3,128,128]{2,1,0:T(8,128)(2,1)S(1)}, bf16[3,128,128]{2,1,0:T(8,128)(2,1)}, u32[]{:S(2)}) copy-start(bf16[3,128,128]{2,1,0:T(8,128)(2,1)} %param.7) | copy-start | bytes 294916
  3.6 5.1 %collective-permute-start.1 = (bf16[2,144,256]{2,1,0:T(8,128)(2,1)S(1)}, bf16[2,144,256]{2,1,0:T(8,128)(2,1)S(1)}, u32[]{:S(2)}, u32[]{:S(2)}) collective-permute-start(bf16[2,144,256]{2,1,0:T(8,128)(2,1)S(1)} %get-tuple-element.28), channel_id=1, source_target_pairs={{0,8},{8,0},{16,24},{24,16},{32,40},{40,32},{48,56},{56,48},{64,72... | collective-permute-start | bytes 442376 | tf_op jit(solution)/shard_map/ppermute | solution.py:24
  8.8 13.6 %collective-permute-start.2 = (bf16[272,256]{1,0:T(8,128)(2,1)S(1)}, bf16[272,256]{1,0:T(8,128)(2,1)S(1)}, u32[]{:S(2)}, u32[]{:S(2)}) collective-permute-start(bf16[272,256]{1,0:T(8,128)(2,1)S(1)} %select_bitcast_fusion.1), channel_id=1, source_target_pairs={{0,16},{8,24},{16,0},{24,8},{32,48},{40,56},{48,32},{56,40},{64,80... | collective-permute-start | bytes 417800 | tf_op jit(solution)/shard_map/ppermute | solution.py:24
  13.3 26.3 %collective-permute-start.7 = (bf16[1,128,384]{2,1,0:T(8,128)(2,1)S(1)}, bf16[1,128,384]{2,1,0:T(8,128)(2,1)S(1)}, u32[]{:S(2)}, u32[]{:S(2)}) collective-permute-start(bf16[1,128,384]{2,1,0:T(8,128)(2,1)S(1)} %maximum_bitcast_fusion), channel_id=1, source_target_pairs={{0,64},{8,72},{16,80},{24,88},{32,96},{40,104},{48,112},{56,120},{... | collective-permute-start | bytes 294920 | tf_op jit(solution)/shard_map/ppermute | solution.py:24
  22.5 23.6 %collective-permute-start.3 = (bf16[528,256]{1,0:T(8,128)(2,1)S(1)}, bf16[528,256]{1,0:T(8,128)(2,1)S(1)}, u32[]{:S(2)}, u32[]{:S(2)}) collective-permute-start(bf16[528,256]{1,0:T(8,128)(2,1)S(1)} %pad_maximum_fusion.1.t0), channel_id=1, source_target_pairs={{0,4},{1,5},{2,6},{3,7},{4,0},{5,1},{6,2},{7,3},{8,12},{9,13},{10,... | collective-permute-start | bytes 811016 | tf_op jit(solution)/shard_map/ppermute | solution.py:24
  32.7 13.4 %collective-permute-start.4 = (bf16[528,256]{1,0:T(8,128)(2,1)S(1)}, bf16[528,256]{1,0:T(8,128)(2,1)S(1)}, u32[]{:S(2)}, u32[]{:S(2)}) collective-permute-start(bf16[528,256]{1,0:T(8,128)(2,1)S(1)} %pad_maximum_fusion.1.t0), channel_id=1, source_target_pairs={{0,1},{1,0},{2,3},{3,2},{4,5},{5,4},{6,7},{7,6},{8,9},{9,8},{10,11... | collective-permute-start | bytes 811016 | tf_op jit(solution)/shard_map/ppermute | solution.py:24
  35.1 14.3 %collective-permute-start.5 = (bf16[528,256]{1,0:T(8,128)(2,1)S(1)}, bf16[528,256]{1,0:T(8,128)(2,1)S(1)}, u32[]{:S(2)}, u32[]{:S(2)}) collective-permute-start(bf16[528,256]{1,0:T(8,128)(2,1)S(1)} %pad_maximum_fusion.1.t0), channel_id=1, source_target_pairs={{0,2},{1,3},{2,0},{3,1},{4,6},{5,7},{6,4},{7,5},{8,10},{9,11},{10,... | collective-permute-start | bytes 811016 | tf_op jit(solution)/shard_map/ppermute | solution.py:24
  39.6 28.0 %collective-permute-start.8 = (bf16[2,128,384]{2,1,0:T(8,128)(2,1)S(1)}, bf16[2,128,384]{2,1,0:T(8,128)(2,1)S(1)}, u32[]{:S(2)}, u32[]{:S(2)}) collective-permute-start(bf16[2,128,384]{2,1,0:T(8,128)(2,1)S(1)} %pad_maximum_fusion.2), channel_id=1, source_target_pairs={{0,32},{8,40},{16,48},{24,56},{32,0},{40,8},{48,16},{56,24},{64,96... | collective-permute-start | bytes 589832 | tf_op jit(solution)/shard_map/ppermute | solution.py:24
  50.4 41.9 %all-to-all-start = ((bf16[4,528,256]{2,1,0:T(8,128)(2,1)}), bf16[4,528,256]{2,1,0:T(8,128)(2,1)S(1)}, u32[]{:S(2)}, u32[]{:S(2)}) async-start(bf16[4,528,256]{2,1,0:T(8,128)(2,1)} %broadcast_in_dim.17), calls=%async_computation | async-start | bytes 2162688 | tf_op jit(solution)/shard_map/all_to_all | solution.py:44
  67.7 21.6 %collective-permute-start.10 = (bf16[2,256,384]{2,1,0:T(8,128)(2,1)S(1)}, bf16[2,256,384]{2,1,0:T(8,128)(2,1)S(1)}, u32[]{:S(2)}, u32[]{:S(2)}) collective-permute-start(bf16[2,256,384]{2,1,0:T(8,128)(2,1)S(1)} %pad_maximum_fusion.w0), channel_id=1, source_target_pairs={{0,256},{8,264},{16,272},{24,280},{32,288},{40,296},{48,304},{56,3... | collective-permute-start | bytes 1179656 | tf_op jit(solution)/shard_map/ppermute | solution.py:24
  74.7 17.7 %collective-permute-start.11 = (bf16[2,256,384]{2,1,0:T(8,128)(2,1)S(1)}, bf16[2,256,384]{2,1,0:T(8,128)(2,1)S(1)}, u32[]{:S(2)}, u32[]{:S(2)}) collective-permute-start(bf16[2,256,384]{2,1,0:T(8,128)(2,1)S(1)} %pad_maximum_fusion.w0), channel_id=1, source_target_pairs={{0,384},{8,392},{16,400},{24,408},{32,416},{40,424},{48,432},{56,4... | collective-permute-start | bytes 1179656 | tf_op jit(solution)/shard_map/ppermute | solution.py:24
  77.5 14.9 %collective-permute-start.9 = (bf16[2,256,384]{2,1,0:T(8,128)(2,1)S(1)}, bf16[2,256,384]{2,1,0:T(8,128)(2,1)S(1)}, u32[]{:S(2)}, u32[]{:S(2)}) collective-permute-start(bf16[2,256,384]{2,1,0:T(8,128)(2,1)S(1)} %pad_maximum_fusion.w0), channel_id=1, source_target_pairs={{0,128},{8,136},{16,144},{24,152},{32,160},{40,168},{48,176},{56,1... | collective-permute-start | bytes 1179656 | tf_op jit(solution)/shard_map/ppermute | solution.py:24
  79.5 9.8 %collective-permute-start.6 = (bf16[528,256]{1,0:T(8,128)(2,1)S(1)}, bf16[528,256]{1,0:T(8,128)(2,1)}, u32[]{:S(2)}, u32[]{:S(2)}) collective-permute-start(bf16[528,256]{1,0:T(8,128)(2,1)S(1)} %pad_maximum_fusion.1.t0), channel_id=1, source_target_pairs={{0,3},{1,2},{2,1},{3,0},{4,7},{5,6},{6,5},{7,4},{8,11},{9,10},{10,... | collective-permute-start | bytes 811016 | tf_op jit(solution)/shard_map/ppermute | solution.py:24
  95.1 16.3 %copy-start.2 = (f32[128,16]{0,1:T(8,128)S(1)}, f32[128,16]{0,1:T(8,128)}, u32[]{:S(2)}) copy-start(f32[128,16]{0,1:T(8,128)} %param.9) | copy-start | bytes 24580
  95.1 16.3 %copy-start.3 = (f32[128,16]{0,1:T(8,128)S(1)}, f32[128,16]{0,1:T(8,128)}, u32[]{:S(2)}) copy-start(f32[128,16]{0,1:T(8,128)} %param.10) | copy-start | bytes 24580
  95.1 17.6 %copy-start.1 = (f32[3,128,3]{1,2,0:T(4,128)S(1)}, f32[3,128,3]{1,2,0:T(4,128)}, u32[]{:S(2)}) copy-start(f32[3,128,3]{1,2,0:T(4,128)} %param.8) | copy-start | bytes 13828
  95.1 3.8 %collective-permute-start.12 = (f32[816,128]{1,0:T(8,128)S(1)}, f32[816,128]{1,0:T(8,128)S(1)}, u32[]{:S(2)}, u32[]{:S(2)}) collective-permute-start(f32[816,128]{1,0:T(8,128)S(1)} %get-tuple-element.35), channel_id=1, source_target_pairs={{0,8},{8,0},{16,24},{24,16},{32,40},{40,32},{48,56},{56,48},{64,72... | collective-permute-start | bytes 1253384 | tf_op jit(solution)/shard_map/ppermute | solution.py:24
  99.0 25.1 %copy-start.4 = (f32[128]{0:T(128)S(1)}, f32[128]{0:T(128)}, u32[]{:S(2)}) copy-start(f32[128]{0:T(128)} %param.11) | copy-start | bytes 1540
  99.0 10.4 %collective-permute-start.14 = (f32[528,128]{1,0:T(8,128)S(1)}, f32[528,128]{1,0:T(8,128)S(1)}, u32[]{:S(2)}, u32[]{:S(2)}) collective-permute-start(f32[528,128]{1,0:T(8,128)S(1)} %get-tuple-element.38), channel_id=1, source_target_pairs={{0,16},{8,24},{16,0},{24,8},{32,48},{40,56},{48,32},{56,40},{64,80... | collective-permute-start | bytes 811016 | tf_op jit(solution)/shard_map/ppermute | solution.py:24
  109.4 3.2 %collective-permute-start.15 = (bf16[528,128]{1,0:T(8,128)(2,1)S(1)}, bf16[528,128]{1,0:T(8,128)(2,1)S(1)}, u32[]{:S(2)}, u32[]{:S(2)}) collective-permute-start(bf16[528,128]{1,0:T(8,128)(2,1)S(1)} %add_convert_fusion.mine), channel_id=1, source_target_pairs={{0,8},{8,0},{16,24},{24,16},{32,40},{40,32},{48,56},{56,48},{64,72... | collective-permute-start | bytes 405512 | tf_op jit(solution)/shard_map/ppermute | solution.py:24
  114.0 21.5 %all-to-all-start.1 = ((f32[16,16,128]{2,1,0:T(8,128)}), f32[16,16,128]{2,1,0:T(8,128)S(1)}, u32[]{:S(2)}, u32[]{:S(2)}) async-start(f32[16,16,128]{2,1,0:T(8,128)} %get-tuple-element.45), calls=%async_computation.1 | async-start | bytes 262144 | tf_op jit(solution)/shard_map/all_to_all | solution.py:44
  121.1 6.3 %collective-permute-start.13 = (f32[144,128]{1,0:T(8,128)S(1)}, f32[144,128]{1,0:T(8,128)S(1)}, u32[]{:S(2)}, u32[]{:S(2)}) collective-permute-start(f32[144,128]{1,0:T(8,128)S(1)} %get-tuple-element.37), channel_id=1, source_target_pairs={{0,16},{8,24},{16,0},{24,8},{32,48},{40,56},{48,32},{56,40},{64,80... | collective-permute-start | bytes 221192 | tf_op jit(solution)/shard_map/ppermute | solution.py:24
